TPU v7x, 512 devices: a whole 4x8x8 slice. The times are simulated.
512 devices in a mesh: dp: 128 (over y, x, z_lo, core), mp: 4 (over z_hi).
Axes of the slice: x: 4, y: 8, z: 8 (z_hi: 4, z_lo: 2; z = z_hi * 2 + z_lo), core: 2. Of those that a mesh axis runs over, the one named last changes fastest.
Arguments:
- inputs: bfloat16 [32768, 2560], P('dp', 'mp'), may hold values from -6 to 6
- out_grads: bfloat16 [32768, 2560], P('dp', 'mp'), may hold values from -6 to 6
- doc_lengths: int32 [128, 16], P('dp'), may hold values from 1 to 128, 256 in all within a row
- owners: int32 [4, 4], P('mp'), may hold values from 0 to 127, as said below
- basis_in: bfloat16 [81920, 2560], P('dp', 'mp'), may hold values from -0.25 to 0.25
- basis_out: bfloat16 [81920, 2560], P('dp', 'mp'), may hold values from -0.25 to 0.25
- eig_in: float32 [128, 2560], P('dp', 'mp'), may hold values from 0.25 to 2
- eig_out: float32 [128, 2560], P('dp', 'mp'), may hold values from 0.25 to 2
Outputs:
- update: bfloat16 [2560, 2560], P('mp', 'dp')
Inputs may be any that keep to these rules, and one draw needn't show every extreme that they name: In each row the 4 owners are different dp indices.
All inputs are finite; a program needn't handle non-finite values.
Results may differ from a plain program's by a relative error of at most 0.013.
Values may be sent and summed in bfloat16 or wider, within the bound.
No kernel may reach another device: no remote copies, remote signals or barrier semaphores. Data moves between devices by JAX's collectives and lax.ppermute only.
A program may use at most 64 MiB of HBM per device.

v0:
```python
import jax
import jax.numpy as jnp
from jax import lax
from jax.sharding import PartitionSpec as P

DAMPING = 0.1


def broadcast(x, axis, root):
    mine = lax.axis_index(axis) == root
    return lax.psum(jnp.where(mine, x, jnp.zeros_like(x)), axis)


def token_weights(lengths, row_count, replicas):
    ends = jnp.cumsum(lengths)
    starts = ends - lengths
    positions = jnp.arange(row_count, dtype=jnp.int32)
    inside = (positions[:, None] >= starts[None, :]) & (positions[:, None] < ends[None, :])
    per_row = jnp.sum(jnp.where(inside, lengths[None, :], 0), axis=1)
    return 1.0 / (replicas * per_row.astype(jnp.float32))


def precondition(gradient_tile, in_basis, out_basis, in_value, out_value):
    rotated = lax.dot_general(
        in_basis, gradient_tile, (((0,), (0,)), ((), ())), preferred_element_type=jnp.float32
    ).astype(jnp.bfloat16)
    twice = jnp.dot(rotated, out_basis, preferred_element_type=jnp.float32)
    scaled = (twice / (in_value[:, None] * out_value[None, :] + DAMPING)).astype(jnp.bfloat16)
    returned = jnp.dot(in_basis, scaled, preferred_element_type=jnp.float32).astype(jnp.bfloat16)
    return lax.dot_general(
        returned, out_basis, (((1,), (1,)), ((), ())), preferred_element_type=jnp.float32
    ).astype(jnp.bfloat16)


def take_window(piece, target, block_size):
    width = piece.shape[1]
    margin = jnp.zeros((piece.shape[0], block_size), piece.dtype)
    padded = jnp.concatenate([margin, piece, margin], axis=1)
    begin = jnp.clip(target + block_size, 0, width + block_size)
    return lax.dynamic_slice_in_dim(padded, begin, block_size, 1)


def shards(inputs, out_grads, doc_lengths, owners, basis_in, basis_out, eig_in, eig_out):
    replicas = lax.axis_size("dp")
    position = lax.axis_index("dp")
    block_size = basis_in.shape[0]
    block_count = owners.shape[1]
    full_width = block_size * block_count
    own_columns = full_width // replicas
    weights = token_weights(doc_lengths[0], inputs.shape[0], replicas)
    weighted = (inputs.astype(jnp.float32) * weights[:, None]).astype(jnp.bfloat16)
    partial_term = lax.dot_general(
        weighted,
        lax.all_gather(out_grads, "mp", axis=1, tiled=True),
        (((0,), (0,)), ((), ())),
        preferred_element_type=jnp.float32,
    )
    rounded_term = partial_term.astype(jnp.bfloat16)
    matches = owners[0] == position
    owned_block = jnp.sum(jnp.where(matches, jnp.arange(block_count, dtype=jnp.int32), 0))
    target = owned_block * block_size
    start_pair = (
        jnp.zeros((block_size, block_size), jnp.bfloat16),
        jnp.zeros((1, block_size), jnp.float32),
    )
    start = jnp.int32(0)
    basis_piece = lax.all_gather(basis_out, "mp", axis=1, tiled=True)
    value_piece = lax.all_gather(eig_out.astype(jnp.bfloat16), "mp", axis=1, tiled=True).astype(
        jnp.float32
    )
    width = basis_piece.shape[1]
    columns = target + jnp.arange(block_size, dtype=jnp.int32)
    inside = (columns >= start) & (columns < start + width)
    basis_window = take_window(basis_piece, target, block_size)
    value_window = take_window(value_piece, target, block_size)
    out_basis = jnp.where(inside[None, :], basis_window, start_pair[0])
    out_value = jnp.where(inside[None, :], value_window, start_pair[1])

    def owned(gradient_tile):
        return precondition(gradient_tile, basis_in, out_basis, eig_in[0], out_value[0])

    def absent(gradient_tile):
        return jnp.zeros_like(gradient_tile)

    received = lax.all_to_all(rounded_term[None], "dp", split_axis=2, concat_axis=0, tiled=True)
    column_sum = jnp.sum(received.astype(jnp.float32), axis=0).astype(jnp.bfloat16)
    summed = lax.all_gather(column_sum, "dp", axis=1, tiled=True)
    first_column = position * own_columns
    results = []
    for column_block in range(block_count):
        gradient_tile = summed[:, column_block * block_size : (column_block + 1) * block_size]
        owner_index = owners[0, column_block]
        tile_result = lax.cond(position == owner_index, owned, absent, gradient_tile)
        results.append(broadcast(tile_result, "dp", owner_index))
    stacked = jnp.stack(results)
    chosen = lax.dynamic_index_in_dim(stacked, first_column // block_size, 0, keepdims=False)
    return lax.dynamic_slice_in_dim(chosen, first_column % block_size, own_columns, 1)


def solution(mesh):
    placed = (
        P("dp", "mp"),
        P("dp", "mp"),
        P("dp", None),
        P("mp", None),
        P("dp", "mp"),
        P("dp", "mp"),
        P("dp", "mp"),
        P("dp", "mp"),
    )
    return jax.shard_map(
        shards, mesh=mesh, in_specs=placed, out_specs=P("mp", "dp"), check_vma=False
    )
```

profile of v0, /device:TPU:1, one launch (start us, length us, event | category | flops | bytes accessed | tf_op | source)
XLA Modules:
  0.0 1521.2 jit_solution(14665076324240936189)
XLA Ops:
  9.6 47.4 %all-gather.5.cloned.1.call-done = bf16[256,2560]{1,0:T(8,128)(2,1)} async-done(((bf16[256,640]{1,0:T(8,128)(2,1)}), bf16[256,2560]{1,0:T(8,128)(2,1)}) %all-gather.5.cloned.1.call-update) | async-done | bytes 1310736 | tf_op jit(solution)/shard_map/all_gather | solution.py:54
  57.0 2.6 fusion.8
  59.5 9.8 copy.26
  69.8 19.3 %reduce.16 = bf16[2560,640]{1,0:T(8,128)(2,1)S(1)} reduce(bf16[2560,1,640]{2,1,0:T(2,128)(2,1)} %bitcast.61, bf16[]{:T(256)} %broadcast.85), dimensions={1}, to_apply=%bitcast.33.reduce_sub_computation | reduce | bytes 6553602
  89.1 2.6 reshape.55
  91.8 11.7 all-to-all-start
  104.3 73.9 %all-to-all-done = bf16[128,2,6400]{2,1,0:T(2,128)(2,1)S(1)} async-done(((bf16[128,2,6400]{2,1,0:T(2,128)(2,1)}), bf16[128,2,6400]{2,1,0:T(2,128)(2,1)S(1)}, u32[]{:S(2)}, u32[]{:S(2)}) %all-to-all-start) | async-done | bytes 3276832 | tf_op jit(solution)/shard_map/all_to_all | solution.py:85
  178.2 7.5 reshape.56
  185.7 18.6 %bitcast_reduce_fusion = bf16[640,2560]{0,1:T(8,128)(2,1)S(1)} fusion(bf16[2560,1,640]{2,1,0:T(2,128)(2,1)} %reshape.56), kind=kLoop, calls=%fused_computation.61 | loop fusion | bytes 6553600 | tf_op jit(solution)/shard_map/all_to_all | solution.py:85
  204.2 2.6 all_to_all.10
  206.8 3.4 reduce_sum.31
  211.6 10.7 all_gather.15
  225.7 3.3 fusion.11
  229.0 194.3 %all-gather.9.cloned.1.call-done = bf16[128,20,640]{2,1,0:T(8,128)(2,1)} async-done(((bf16[1,20,640]{2,1,0:T(8,128)(2,1)}), bf16[128,20,640]{2,1,0:T(8,128)(2,1)}) %all-gather.9.cloned.1.call-update) | async-done | bytes 3276816 | tf_op jit(solution)/shard_map/all_gather | solution.py:87
  423.3 4.6 reshape.43
  428.0 1.0 conditional.4
  428.0 1.0 broadcast.54
  428.9 1.0 conditional.5
  429.9 1.3 select_bitcast_fusion.2
  431.2 1.0 conditional.6
  431.2 1.0 broadcast.58
  432.5 1.3 select_bitcast_fusion
  433.9 1078.7 %all-reduce.3.cloned.1.call-done = (bf16[1,640,640]{2,1,0:T(8,128)(2,1)}, bf16[1,640,640]{2,1,0:T(8,128)(2,1)}, bf16[1,640,640]{2,1,0:T(8,128)(2,1)}, bf16[1,640,640]{2,1,0:T(8,128)(2,1)}) async-done(((bf16[1,640,640]{2,1,0:T(8,128)(2,1)}, bf16[1,640,640]{2,1,0:T(8,128)(2,1)}, bf16[1,640,640]{2,1,0:T(8,128)(2,1)}, bf16[1,640,640]{2,1,0:T(8,128)(2,1)}), (bf16[1,640,640]{2,1,0:T(8,128)(2,1)}, ...) | async-done | bytes 3276816 | tf_op jit(solution)/shard_map/psum | solution.py:11
  1512.6 1.3 fusion.15
  (34 shorter events, 8.0 us)
Async XLA Ops:
  6.5 50.4 %all-gather.5.cloned.1.call-start = ((), (), s32[]{:S(2)}) async-start(), calls=%async_computation.1 | async-start | bytes 1638400 | tf_op jit(solution)/shard_map/all_gather | solution.py:54
  91.8 86.4 %all-to-all-start = ((bf16[128,2,6400]{2,1,0:T(2,128)(2,1)}), bf16[128,2,6400]{2,1,0:T(2,128)(2,1)S(1)}, u32[]{:S(2)}, u32[]{:S(2)}) async-start(bf16[128,2,6400]{2,1,0:T(2,128)(2,1)} %reshape.55), calls=%async_computation | async-start | bytes 6553600 | tf_op jit(solution)/shard_map/all_to_all | solution.py:85
  103.5 122.1 %all-gather.7.cloned.1.call-start = ((), (), s32[]{:S(2)}) async-start(), calls=%async_computation.2 | async-start | bytes 4096000 | tf_op jit(solution)/shard_map/all_gather | solution.py:67
  104.3 319.0 %all-gather.9.cloned.1.call-start = ((), (), s32[]{:S(2)}) async-start(), calls=%async_computation.3 | async-start | bytes 3962880 | tf_op jit(solution)/shard_map/all_gather | solution.py:87
  206.8 3.5 copy-start.2
  206.8 4.8 copy-start.3
  210.3 1302.4 %all-reduce.3.cloned.1.call-start = ((), (), s32[]{:S(2)}) async-start(), calls=%async_computation.4 | async-start | bytes 6553600 | tf_op jit(solution)/shard_map/psum | solution.py:11
  229.0 198.9 %copy-start.1 = (f32[1,640]{1,0:T(1,128)S(1)}, f32[1,640]{1,0:T(1,128)}, u32[]{:S(2)}) copy-start(f32[1,640]{1,0:T(1,128)} %param.22) | copy-start | bytes 7684
Sparse Core Ops, SparseCore 0:
  9.5 47.4 all-gather.4
  106.5 99.7 all-gather.6
  210.4 212.8 all-gather.8
  434.0 1078.6 all-reduce.2
where the time goes:
time: 1520 us
  waiting for transfers between devices  1400 us (92%)
  local copies, waits for them, and re-layouts  51.3 us (3%)
  other arithmetic  32.4 us (2%)
  between operations  16.5 us (1%)
    psum x1, waiting for transfers between devices, broadcast(): return lax.psum(jnp.where(mine, x, jnp.zeros_like(x)), axis)  1080 us
    all_gather x1, waiting for transfers between devices, shards(): summed = lax.all_gather(column_sum, 'dp', axis=1, tiled=True)  194 us
    all_to_all x1, waiting for transfers between devices, shards(): lax.all_to_all(rounded_term[None], 'dp', split_axis=2, concat_axis=0, til...  73.9 us
    all_gather x1, waiting for transfers between devices, shards(): lax.all_gather(out_grads, 'mp', axis=1, tiled=True)  47.4 us
  transfers between devices with their start and end apart: 5, of which 4 were waited for; matrix products, arithmetic and copies ran while one was open for 2% of the time, Pallas kernels for 0%

commit v1 on v0

v1 whole, which is shorter than its diff:
```python
import jax
import jax.numpy as jnp
from jax import lax
from jax.sharding import Mesh
from jax.sharding import PartitionSpec as P

DAMPING = 0.1
SPLIT = (4, 2, 4, 2, 2, 4)
AXES = ("yj", "yh", "x", "zl", "c", "mp")
DP = AXES[:5]
ROW = ("x", "zl", "c")
NEXT_TO = [(0, 1), (1, 0), (2, 3), (3, 2)]
ACROSS = [(0, 3), (3, 0), (1, 2), (2, 1)]
PLACE = ((0, 2, 3, 1), (2, 0, 1, 3), (3, 1, 0, 2), (1, 3, 2, 0))
F32 = jnp.float32
BF16 = jnp.bfloat16


def token_weights(lengths, row_count, replicas):
    ends = jnp.cumsum(lengths)
    starts = ends - lengths
    positions = jnp.arange(row_count, dtype=jnp.int32)
    inside = (positions[:, None] >= starts[None, :]) & (positions[:, None] < ends[None, :])
    per_row = jnp.sum(jnp.where(inside, lengths[None, :], 0), axis=1)
    return 1.0 / (replicas * per_row.astype(F32))


def exchange(x, axes):
    return lax.all_to_all(x, axes, split_axis=0, concat_axis=0, tiled=True)


def pick(x, i):
    return lax.dynamic_index_in_dim(x, i, 0, keepdims=False)


def two_terms(v):
    high = lax.reduce_precision(v, 8, 7)
    return [high.astype(BF16), (v - high).astype(BF16)]


def partial_products(w, g):
    g2 = g.reshape(256, 2, 320).transpose(1, 0, 2)
    xp = lax.ppermute(w, "mp", NEXT_TO)
    gq = lax.ppermute(g2, "mp", ACROSS)
    xs = [lax.all_gather(v, "c", axis=0, tiled=True) for v in (w, xp)]
    gs = [exchange(v, "c").reshape(512, 320) for v in (g2, gq)]
    blocks = []
    for xm in xs:
        for gj in gs:
            d = lax.dot_general(gj, xm, (((0,), (0,)), ((), ())), preferred_element_type=F32)
            blocks.append(d.astype(BF16).reshape(4, 80, 640))
    return jnp.stack(blocks, axis=1)


def tile_of_gradient(parts):
    z = lax.axis_index("mp")
    summed = lax.psum_scatter(parts, "x", scatter_dimension=0, tiled=True)[0]
    other = lax.ppermute(summed[2:], "mp", NEXT_TO)
    four = jnp.concatenate([summed[:2], other], axis=0)
    places = jnp.asarray(PLACE, jnp.int32)[z]
    ordered = jnp.stack([pick(four, places[j]) for j in range(4)])
    received = exchange(ordered.reshape(16, 20, 640), ("yj", "yh", "zl"))
    piece = jnp.sum(received.astype(F32), axis=0).astype(BF16)
    spread = exchange(jnp.broadcast_to(piece[None], (16, 20, 640)), ("x", "yh", "zl"))
    return lax.all_gather(spread.reshape(320, 640), "c", axis=0, tiled=True)


def bases_of_tile(owners, u, v, ei, eo):
    z = lax.axis_index("mp")
    every = lax.all_gather(owners, "mp", axis=0, tiled=True)
    mine = owners[0]
    theirs = lax.dynamic_index_in_dim(every, z, 1, keepdims=False)
    small = jnp.stack(two_terms(ei[0]) + two_terms(eo[0]))
    sent = jnp.concatenate(
        [
            u.reshape(16, 40, 640),
            v.reshape(16, 40, 640),
            jnp.broadcast_to(small[None], (16, 4, 640)),
            jnp.zeros((16, 4, 640), BF16),
        ],
        axis=1,
    )
    row = exchange(sent, ROW)
    u_part = jnp.stack([pick(row, mine[j] % 16) for j in range(4)])
    v_part = exchange(jnp.stack([pick(row, theirs[m] % 16)[40:] for m in range(4)]), "mp")
    both = jnp.concatenate([u_part[:, :40], v_part[:, :40], u_part[:, 80:82], v_part[:, 42:44], u_part[:, 84:88]], axis=1)
    both = jnp.broadcast_to(both[:, None], (4, 2, 88, 640)).reshape(8, 88, 640)
    column = exchange(both, ("yj", "yh"))
    owner = pick(mine, lax.axis_index("yj"))
    whole = lax.all_gather(pick(column, owner // 16)[None], ROW, axis=0, tiled=True)
    u_tile = whole[:, :40].reshape(640, 640)
    v_tile = whole[:, 40:80].reshape(640, 640)
    small = whole[0, 80:84].astype(F32)
    return u_tile, v_tile, small[0] + small[1], small[2] + small[3]


def shards(inputs, out_grads, doc_lengths, owners, basis_in, basis_out, eig_in, eig_out):
    weights = token_weights(doc_lengths[0], inputs.shape[0], lax.axis_size(DP))
    weighted = (inputs.astype(F32) * weights[:, None]).astype(BF16)
    parts = partial_products(weighted, out_grads)
    u, v, ei, eo = bases_of_tile(owners, basis_in, basis_out, eig_in, eig_out)
    gt = tile_of_gradient(parts)
    first = (lax.axis_index(DP) % 32) * 20
    v_own = lax.dynamic_slice_in_dim(v, first, 20, 0)
    rotated = jnp.dot(gt, u, preferred_element_type=F32).astype(BF16)
    twice = lax.dot_general(v, rotated, (((0,), (0,)), ((), ())), preferred_element_type=F32)
    scaled = (twice / (eo[:, None] * ei[None, :] + DAMPING)).astype(BF16)
    back = jnp.dot(v_own, scaled, preferred_element_type=F32).astype(BF16)
    out = lax.dot_general(back, u, (((1,), (1,)), ((), ())), preferred_element_type=F32)
    return out.astype(BF16).T


def solution(mesh):
    fine = Mesh(mesh.devices.reshape(SPLIT), AXES)
    split = P(DP, "mp")
    placed = (split, split, P(DP, None), P("mp", None), split, split, split, split)
    return jax.shard_map(
        shards, mesh=fine, in_specs=placed, out_specs=P("mp", DP), check_vma=False
    )
```

time: 1520 us -> 218 us (0.14)
  waiting for transfers between devices: 1400 us -> 68.9 us
  local copies, waits for them, and re-layouts: 51.3 us -> 10.5 us
  blocking collectives: 10.7 us -> 43.8 us
  starting transfers between devices: 11.9 us -> 41.4 us
  other arithmetic: 32.4 us -> 7.34 us
  between operations: 16.5 us -> 40.2 us
    psum x1 -> x0, waiting for transfers between devices: 1080 us -> none  [broadcast(): return lax.psum(jnp.where(mine, x, jnp.zeros_like(x)), axis)]
    all_gather x3 -> x1, waiting for transfers between devices: 242 us -> 0.01 us  [bases_of_tile(): lax.all_gather(pick(column, owner // 16)[None], ROW, axis=0, tiled=True)]
    all_to_all x1 -> x5, waiting for transfers between devices: 73.9 us -> 35.1 us  [exchange(): return lax.all_to_all(x, axes, split_axis=0, concat_axis=0, tiled=True)]
    ppermute x0 -> x3, waiting for transfers between devices: none -> 33.7 us  [the longest x1 23 us: partial_products(): xp = lax.ppermute(w, 'mp', NEXT_TO)]
    all_to_all x2 -> x0, local copies, waits for them, and re-layouts: 21.1 us -> none  [shards(): lax.all_to_all(rounded_term[None], 'dp', split_axis=2, concat_axis=0, til...]
    all_to_all x0 -> x2, blocking collectives: none -> 19.9 us  [exchange(): return lax.all_to_all(x, axes, split_axis=0, concat_axis=0, tiled=True)]
    all_to_all x1 -> x5, starting transfers between devices: 11.7 us -> 31.5 us  [exchange(): return lax.all_to_all(x, axes, split_axis=0, concat_axis=0, tiled=True)]
    unnamed x1 -> x0, other arithmetic: 19.3 us -> none
  transfers between devices with their start and end apart: 5 -> 10, of which waited for: 4 -> 5; matrix products, arithmetic and copies ran while one was open for 2% -> 7% of each run, Pallas kernels for 0% -> 0%
where the time goes in v1:
time: 218 us; the launch traced here: 217 us
  waiting for transfers between devices  68.9 us (32%)
  blocking collectives  43.8 us (20%)
  starting transfers between devices  41.4 us (19%)
  between operations  40.2 us (18%)
  local copies, waits for them, and re-layouts  10.5 us (5%)
  other arithmetic  7.34 us (3%)
  matrix products  4.83 us (2%)
    all_to_all x5, waiting for transfers between devices, exchange(): return lax.all_to_all(x, axes, split_axis=0, concat_axis=0, tiled=True)  35.1 us
    all_to_all x5, starting transfers between devices, exchange(): return lax.all_to_all(x, axes, split_axis=0, concat_axis=0, tiled=True)  31.5 us
    ppermute x1, waiting for transfers between devices, partial_products(): xp = lax.ppermute(w, 'mp', NEXT_TO)  23 us
    all_to_all x2, blocking collectives, exchange(): return lax.all_to_all(x, axes, split_axis=0, concat_axis=0, tiled=True)  19.9 us
    ppermute x1, waiting for transfers between devices, partial_products(): gq = lax.ppermute(g2, 'mp', ACROSS)  10.7 us
    all_gather x1, blocking collectives, bases_of_tile(): every = lax.all_gather(owners, 'mp', axis=0, tiled=True)  10.6 us
    all_gather x1, blocking collectives, tile_of_gradient(): return lax.all_gather(spread.reshape(320, 640), 'c', axis=0, tiled=True)  8.52 us
    ppermute x1, starting transfers between devices, partial_products(): gq = lax.ppermute(g2, 'mp', ACROSS)  5.27 us
  transfers between devices with their start and end apart: 10, of which 5 were waited for; matrix products, arithmetic and copies ran while one was open for 7% of the time, Pallas kernels for 0%

profile of v1, /device:TPU:1, one launch (start us, length us, event | category | flops | bytes accessed | tf_op | source)
XLA Modules:
  0.0 217.0 jit_solution(18325663767071448485)
XLA Ops:
  7.4 2.0 copy.29
  9.3 10.3 %all-to-all-start.3 = ((bf16[2,256,320]{1,2,0:T(8,128)(2,1)}), bf16[2,256,320]{1,2,0:T(8,128)(2,1)S(1)}, u32[]{:S(2)}, u32[]{:S(2)}) async-start(bf16[2,256,320]{1,2,0:T(8,128)(2,1)} %bitcast.19), calls=%async_computation.3 | async-start | bytes 655360 | tf_op jit(solution)/shard_map/all_to_all | solution.py:29
  19.7 5.3 %collective-permute-start = (bf16[2,256,320]{1,2,0:T(8,128)(2,1)}, bf16[2,256,320]{1,2,0:T(8,128)(2,1)S(1)}, u32[]{:S(2)}, u32[]{:S(2)}) collective-permute-start(bf16[2,256,320]{1,2,0:T(8,128)(2,1)} %bitcast.19), channel_id=1, source_target_pairs={{0,3},{3,0},{1,2},{2,1},{4,7},{7,4},{5,6},{6,5},{8,11},{11,8},{9,1... | collective-permute-start | bytes 983048 | tf_op jit(solution)/shard_map/ppermute | solution.py:44
  25.8 2.9 %maximum_maximum_fusion = bf16[16,88,640]{2,1,0:T(8,128)(2,1)} fusion(bf16[16,4,640]{2,1,0:T(4,128)(2,1)S(1)} %broadcast_in_dim.22, bf16[16,40,640]{2,1,0:T(8,128)(2,1)S(1)} %bitcast.85, bf16[16,40,640]{2,1,0:T(8,128)(2,1)} %bitcast.86, bf16[88]{0:T(256)(128)(2,1)S(1)} %pad.21.clone), kind=kLoop, calls=%fused_computation | loop fusion | flops 7208960 | bytes 3522736 | tf_op jit(solution)/shard_map/concatenate | solution.py:74
  28.7 10.7 %collective-permute-done = bf16[2,256,320]{1,2,0:T(8,128)(2,1)S(1)} collective-permute-done((bf16[2,256,320]{1,2,0:T(8,128)(2,1)}, bf16[2,256,320]{1,2,0:T(8,128)(2,1)S(1)}, u32[]{:S(2)}, u32[]{:S(2)}) %collective-permute-start) | collective-permute-done | bytes 327712 | tf_op jit(solution)/shard_map/ppermute | solution.py:44
  39.4 4.4 %all_to_all.35 = bf16[2,256,320]{1,2,0:T(8,128)(2,1)S(1)} all-to-all(bf16[2,256,320]{1,2,0:T(8,128)(2,1)S(1)} %collective-permute-done), channel_id=1, replica_groups=mesh['yj'=4,'yh'=2,'x'=4,'zl'=2,'c'=2,'mp'=4] {'c'}, dimensions={0} | all-to-all | bytes 655360 | tf_op jit(solution)/shard_map/all_to_all | solution.py:29
  43.8 6.4 %all-to-all-start = ((bf16[16,88,640]{2,1,0:T(8,128)(2,1)}), bf16[16,88,640]{2,1,0:T(8,128)(2,1)S(1)}, u32[]{:S(2)}, u32[]{:S(2)}) async-start(bf16[16,88,640]{2,1,0:T(8,128)(2,1)} %maximum_maximum_fusion), calls=%async_computation | async-start | bytes 3604480 | tf_op jit(solution)/shard_map/all_to_all | solution.py:29
  50.7 1.9 collective-permute-start.1
  52.6 2.3 %all_gather.17 = bf16[512,640]{1,0:T(8,128)(2,1)S(1)} all-gather(bf16[256,640]{1,0:T(8,128)(2,1)S(1)} %multiply_convert_fusion), channel_id=1, replica_groups=mesh['yj'=4,'yh'=2,'x'=4,'zl'=2,'c'=2,'mp'=4] {'c'}, dimensions={0}, use_global_device_ids=true | all-gather | bytes 983040 | tf_op jit(solution)/shard_map/all_gather | solution.py:45
  55.4 23.0 %collective-permute-done.1 = bf16[256,640]{1,0:T(8,128)(2,1)S(1)} collective-permute-done((bf16[256,640]{1,0:T(8,128)(2,1)S(1)}, bf16[256,640]{1,0:T(8,128)(2,1)S(1)}, u32[]{:S(2)}, u32[]{:S(2)}) %collective-permute-start.1) | collective-permute-done | bytes 327712 | tf_op jit(solution)/shard_map/ppermute | solution.py:43
  78.4 2.5 %all_gather.18 = bf16[512,640]{1,0:T(8,128)(2,1)S(1)} all-gather(bf16[256,640]{1,0:T(8,128)(2,1)S(1)} %collective-permute-done.1), channel_id=1, replica_groups=mesh['yj'=4,'yh'=2,'x'=4,'zl'=2,'c'=2,'mp'=4] {'c'}, dimensions={0}, use_global_device_ids=true | all-gather | bytes 983040 | tf_op jit(solution)/shard_map/all_gather | solution.py:45
  82.2 1.4 pad_maximum_fusion
  83.6 10.6 %all-gather = s32[4,1,4]{2,1,0:T(1,128)S(1)} all-gather(s32[1,1,4]{2,1,0:T(1,128)S(1)} %bitcast.87), channel_id=1, replica_groups=mesh['yj'=4,'yh'=2,'x'=4,'zl'=2,'c'=2,'mp'=4] {'mp'}, dimensions={0}, use_global_device_ids=true | all-gather | bytes 80 | tf_op jit(solution)/shard_map/all_gather | solution.py:70
  111.3 3.4 %all-to-all-start.1 = ((bf16[4,48,640]{2,1,0:T(8,128)(2,1)}), bf16[4,48,640]{2,1,0:T(8,128)(2,1)S(1)}, u32[]{:S(2)}, u32[]{:S(2)}) async-start(bf16[4,48,640]{2,1,0:T(8,128)(2,1)} %pad_maximum_fusion.3), calls=%async_computation.1 | async-start | bytes 491520 | tf_op jit(solution)/shard_map/all_to_all | solution.py:29
  115.0 7.7 %all-to-all-done.1 = bf16[4,48,640]{2,1,0:T(8,128)(2,1)S(1)} async-done(((bf16[4,48,640]{2,1,0:T(8,128)(2,1)}), bf16[4,48,640]{2,1,0:T(8,128)(2,1)S(1)}, u32[]{:S(2)}, u32[]{:S(2)}) %all-to-all-start.1) | async-done | bytes 245792 | tf_op jit(solution)/shard_map/all_to_all | solution.py:29
  124.0 6.8 %all-to-all-start.2 = ((bf16[8,88,640]{2,1,0:T(8,128)(2,1)}), bf16[8,88,640]{2,1,0:T(8,128)(2,1)S(1)}, u32[]{:S(2)}, u32[]{:S(2)}) async-start(bf16[8,88,640]{2,1,0:T(8,128)(2,1)} %bitcast.11), calls=%async_computation.2 | async-start | bytes 1802240 | tf_op jit(solution)/shard_map/all_to_all | solution.py:29
  133.4 19.7 %all-to-all-done.2 = bf16[8,88,640]{2,1,0:T(8,128)(2,1)S(1)} async-done(((bf16[8,88,640]{2,1,0:T(8,128)(2,1)}), bf16[8,88,640]{2,1,0:T(8,128)(2,1)S(1)}, u32[]{:S(2)}, u32[]{:S(2)}) %all-to-all-start.2) | async-done | bytes 901152 | tf_op jit(solution)/shard_map/all_to_all | solution.py:29
  155.0 2.6 %collective-permute-start.2 = (bf16[2,80,640]{2,1,0:T(8,128)(2,1)S(1)}, bf16[2,80,640]{2,1,0:T(8,128)(2,1)S(1)}, u32[]{:S(2)}, u32[]{:S(2)}) collective-permute-start(bf16[2,80,640]{2,1,0:T(8,128)(2,1)S(1)} %get-tuple-element.21), channel_id=1, source_target_pairs={{0,1},{1,0},{2,3},{3,2},{4,5},{5,4},{6,7},{7,6},{8,9},{9,8},{10,11... | collective-permute-start | bytes 614408 | tf_op jit(solution)/shard_map/ppermute | solution.py:58
  166.8 15.5 %all_to_all.36 = bf16[16,20,640]{2,1,0:T(8,128)(2,1)S(1)} all-to-all(bf16[16,20,640]{2,1,0:T(8,128)(2,1)S(1)} %reshape.113), channel_id=1, replica_groups=mesh['yj'=4,'yh'=2,'x'=4,'zl'=2,'c'=2,'mp'=4] {'yj','yh','zl'}, dimensions={0} | all-to-all | bytes 819200 | tf_op jit(solution)/shard_map/all_to_all | solution.py:29
  183.2 4.6 %all-to-all-start.6 = ((bf16[16,20,640]{2,1,0:T(8,128)(2,1)}), bf16[16,20,640]{2,1,0:T(8,128)(2,1)S(1)}, u32[]{:S(2)}, u32[]{:S(2)}) async-start(bf16[16,20,640]{2,1,0:T(8,128)(2,1)} %broadcast_in_dim.28), calls=%async_computation.7 | async-start | bytes 983040 | tf_op jit(solution)/shard_map/all_to_all | solution.py:29
  187.8 7.7 %all-to-all-done.6 = bf16[16,20,640]{2,1,0:T(8,128)(2,1)S(1)} async-done(((bf16[16,20,640]{2,1,0:T(8,128)(2,1)}), bf16[16,20,640]{2,1,0:T(8,128)(2,1)S(1)}, u32[]{:S(2)}, u32[]{:S(2)}) %all-to-all-start.6) | async-done | bytes 409632 | tf_op jit(solution)/shard_map/all_to_all | solution.py:29
  195.6 8.5 %all_gather.19 = bf16[640,640]{1,0:T(8,128)(2,1)S(1)} all-gather(bf16[320,640]{1,0:T(8,128)(2,1)S(1)} %reshape.114), channel_id=1, replica_groups=mesh['yj'=4,'yh'=2,'x'=4,'zl'=2,'c'=2,'mp'=4] {'c'}, dimensions={0}, use_global_device_ids=true | all-gather | bytes 1228800 | tf_op jit(solution)/shard_map/all_gather | solution.py:65
  204.8 1.5 fusion.18
  207.3 1.3 fusion.1
  (62 shorter events, 13.8 us)
Async XLA Ops:
  7.4 18.4 %copy-start = (bf16[640,640]{1,0:T(8,128)(2,1)S(1)}, bf16[640,640]{1,0:T(8,128)(2,1)}, u32[]{:S(2)}) copy-start(bf16[640,640]{1,0:T(8,128)(2,1)} %param.14) | copy-start | bytes 2457604
  9.3 19.4 %all-to-all-start.3 = ((bf16[2,256,320]{1,2,0:T(8,128)(2,1)}), bf16[2,256,320]{1,2,0:T(8,128)(2,1)S(1)}, u32[]{:S(2)}, u32[]{:S(2)}) async-start(bf16[2,256,320]{1,2,0:T(8,128)(2,1)} %bitcast.19), calls=%async_computation.3 | async-start | bytes 655360 | tf_op jit(solution)/shard_map/all_to_all | solution.py:29
  19.7 19.7 %collective-permute-start = (bf16[2,256,320]{1,2,0:T(8,128)(2,1)}, bf16[2,256,320]{1,2,0:T(8,128)(2,1)S(1)}, u32[]{:S(2)}, u32[]{:S(2)}) collective-permute-start(bf16[2,256,320]{1,2,0:T(8,128)(2,1)} %bitcast.19), channel_id=1, source_target_pairs={{0,3},{3,0},{1,2},{2,1},{4,7},{7,4},{5,6},{6,5},{8,11},{11,8},{9,1... | collective-permute-start | bytes 983048 | tf_op jit(solution)/shard_map/ppermute | solution.py:44
  43.8 6.4 %copy-start.3 = (s32[1,16]{1,0:T(1,128)S(1)}, s32[1,16]{1,0:T(1,128)}, u32[]{:S(2)}) copy-start(s32[1,16]{1,0:T(1,128)} %param.11) | copy-start | bytes 196
  43.8 6.8 %copy-start.1 = (bf16[256,640]{1,0:T(8,128)(2,1)S(1)}, bf16[256,640]{1,0:T(8,128)(2,1)}, u32[]{:S(2)}) copy-start(bf16[256,640]{1,0:T(8,128)(2,1)} %param.9) | copy-start | bytes 983044
  43.8 66.7 %all-to-all-start = ((bf16[16,88,640]{2,1,0:T(8,128)(2,1)}), bf16[16,88,640]{2,1,0:T(8,128)(2,1)S(1)}, u32[]{:S(2)}, u32[]{:S(2)}) async-start(bf16[16,88,640]{2,1,0:T(8,128)(2,1)} %maximum_maximum_fusion), calls=%async_computation | async-start | bytes 3604480 | tf_op jit(solution)/shard_map/all_to_all | solution.py:29
  50.1 103.7 %reduce-scatter.2.cloned.1.call-start = ((), (), s32[]{:S(2)}) async-start(), calls=%async_computation.9 | async-start | bytes 2048000 | tf_op jit(solution)/shard_map/reduce_scatter | solution.py:57
  50.7 27.7 %collective-permute-start.1 = (bf16[256,640]{1,0:T(8,128)(2,1)S(1)}, bf16[256,640]{1,0:T(8,128)(2,1)S(1)}, u32[]{:S(2)}, u32[]{:S(2)}) collective-permute-start(bf16[256,640]{1,0:T(8,128)(2,1)S(1)} %multiply_convert_fusion), channel_id=1, source_target_pairs={{0,1},{1,0},{2,3},{3,2},{4,5},{5,4},{6,7},{7,6},{8,9},{9,8},{10,11... | collective-permute-start | bytes 983048 | tf_op jit(solution)/shard_map/ppermute | solution.py:43
  82.2 1.4 copy-start.2
  111.3 11.3 %all-to-all-start.1 = ((bf16[4,48,640]{2,1,0:T(8,128)(2,1)}), bf16[4,48,640]{2,1,0:T(8,128)(2,1)S(1)}, u32[]{:S(2)}, u32[]{:S(2)}) async-start(bf16[4,48,640]{2,1,0:T(8,128)(2,1)} %pad_maximum_fusion.3), calls=%async_computation.1 | async-start | bytes 491520 | tf_op jit(solution)/shard_map/all_to_all | solution.py:29
  124.0 29.2 %all-to-all-start.2 = ((bf16[8,88,640]{2,1,0:T(8,128)(2,1)}), bf16[8,88,640]{2,1,0:T(8,128)(2,1)S(1)}, u32[]{:S(2)}, u32[]{:S(2)}) async-start(bf16[8,88,640]{2,1,0:T(8,128)(2,1)} %bitcast.11), calls=%async_computation.2 | async-start | bytes 1802240 | tf_op jit(solution)/shard_map/all_to_all | solution.py:29
  130.8 73.3 %all-gather.3.cloned.1.call-start = ((), (), s32[]{:S(2)}) async-start(), calls=%async_computation.8 | async-start | bytes 1914880 | tf_op jit(solution)/shard_map/all_gather | solution.py:90
  155.0 11.5 %collective-permute-start.2 = (bf16[2,80,640]{2,1,0:T(8,128)(2,1)S(1)}, bf16[2,80,640]{2,1,0:T(8,128)(2,1)S(1)}, u32[]{:S(2)}, u32[]{:S(2)}) collective-permute-start(bf16[2,80,640]{2,1,0:T(8,128)(2,1)S(1)} %get-tuple-element.21), channel_id=1, source_target_pairs={{0,1},{1,0},{2,3},{3,2},{4,5},{5,4},{6,7},{7,6},{8,9},{9,8},{10,11... | collective-permute-start | bytes 614408 | tf_op jit(solution)/shard_map/ppermute | solution.py:58
  183.2 12.3 %all-to-all-start.6 = ((bf16[16,20,640]{2,1,0:T(8,128)(2,1)}), bf16[16,20,640]{2,1,0:T(8,128)(2,1)S(1)}, u32[]{:S(2)}, u32[]{:S(2)}) async-start(bf16[16,20,640]{2,1,0:T(8,128)(2,1)} %broadcast_in_dim.28), calls=%async_computation.7 | async-start | bytes 983040 | tf_op jit(solution)/shard_map/all_to_all | solution.py:29
Sparse Core Ops, SparseCore 0:
  83.7 31.6 reduce-scatter.1
Sparse Core Ops, SparseCore 1:
  153.9 36.2 all-gather.2

commit v2 on v1

v2 whole, which is shorter than its diff:
```python
import jax
import jax.numpy as jnp
from jax import lax
from jax.experimental import pallas as pl
from jax.experimental.pallas import tpu as pltpu
from jax.sharding import Mesh
from jax.sharding import PartitionSpec as P

DAMPING = 0.1
SPLIT = (4, 2, 4, 2, 2, 4)
AXES = ("yj", "yh", "x", "zl", "c", "mp")
DP = AXES[:5]
ROW = ("yh", "x", "c")
COLUMN = ("yj", "zl")
F32 = jnp.float32
BF16 = jnp.bfloat16


def token_weights(lengths, row_count, replicas):
    ends = jnp.cumsum(lengths)
    starts = ends - lengths
    positions = jnp.arange(row_count, dtype=jnp.int32)
    inside = (positions[:, None] >= starts[None, :]) & (positions[:, None] < ends[None, :])
    per_row = jnp.sum(jnp.where(inside, lengths[None, :], 0), axis=1)
    return 1.0 / (replicas * per_row.astype(F32))


def exchange(x, axes):
    return lax.all_to_all(x, axes, split_axis=0, concat_axis=0, tiled=True)


def pool(x):
    return lax.all_gather(x, "c", axis=0, tiled=True)


def by_block(entries):
    z = lax.axis_index("mp")
    a, b, c, d = entries
    low, high = z % 2 == 1, z // 2 == 1
    a, b = jnp.where(low, b, a), jnp.where(low, a, b)
    c, d = jnp.where(low, d, c), jnp.where(low, c, d)
    a, c = jnp.where(high, c, a), jnp.where(high, a, c)
    b, d = jnp.where(high, d, b), jnp.where(high, b, d)
    return [a, b, c, d]


def two_terms(v):
    high = lax.reduce_precision(v, 8, 7)
    return jnp.stack([high.astype(BF16), (v - high).astype(BF16)])


def rows_sent(u, v, ei, eo):
    small = jnp.concatenate([two_terms(ei), two_terms(eo), jnp.zeros((4, 640), BF16)])
    small = jnp.broadcast_to(small[None], (16, 8, 640))
    return jnp.concatenate([u.reshape(16, 40, 640), v.reshape(16, 40, 640), small], axis=1)


def product(g, x):
    d = lax.dot_general(g, x, (((0,), (0,)), ((), ())), preferred_element_type=F32)
    return d.astype(BF16).reshape(4, 1, 80, 640)


def shift(x, distance):
    return lax.ppermute(x, "mp", [(i, i ^ distance) for i in range(4)])


def swapped(inputs, out_grads, owners, lengths, sent):
    weights = token_weights(lengths, inputs.shape[0], lax.axis_size(DP))[:, None]

    def weigh(x):
        return pool((x.astype(F32) * weights).astype(BF16))

    g = pool(out_grads)
    g = jnp.where(lax.axis_index("c") == 0, g[:, :320], g[:, 320:])
    row = exchange(sent, ROW)
    x_next = shift(inputs, 1)
    g_across = shift(g, 3)
    x = weigh(inputs)
    near = product(g, x)
    owners, near = lax.optimization_barrier((owners, near))
    rows = jnp.stack([owners] + [shift(owners, d) for d in (1, 2, 3)])
    row, x_next, g_across, rows = lax.optimization_barrier((row, x_next, g_across, rows))
    x_next = weigh(x_next)
    parts = [near, product(g_across, x), product(g, x_next), product(g_across, x_next)]
    return row, rows, jnp.concatenate(parts, axis=1)


def row_sums(parts):
    summed = lax.psum_scatter(parts, "x", scatter_dimension=0, tiled=True)[0]
    back = shift(summed[2:], 1)
    return jnp.stack(by_block([summed[0], back[0], back[1], summed[1]]))


def tile_of_gradient(four):
    received = exchange(four.reshape(16, 20, 640), ("yj", "yh", "zl"))
    piece = jnp.sum(received.astype(F32), axis=0).astype(BF16)
    spread = exchange(jnp.broadcast_to(piece[None], (16, 20, 640)), ("x", "yh", "zl"))
    return pool(spread.reshape(320, 640))


def within_row(owner):
    return ((owner >> 4) & 1) * 8 + ((owner >> 2) & 3) * 2 + (owner & 1)


def within_column(owner):
    return (owner >> 5) * 2 + ((owner >> 1) & 1)


def choose_v(row, rows, z):
    def body(rows_ref, z_ref, row_ref, out_ref):
        here = z_ref[0]
        for m in range(4):
            source = within_row(rows_ref[(here ^ m) * 4 + here])
            out_ref[m] = row_ref[source, 40:88, :]

    return on_scalars(body, (rows.reshape(16), z), (row,), (4, 48, 640))


def choose_both(row, v_part, mine):
    def body(mine_ref, row_ref, v_ref, out_ref):
        for j in range(4):
            source = within_row(mine_ref[j])
            for half in range(2):
                out_ref[2 * j + half, 0:40, :] = row_ref[source, 0:40, :]
                out_ref[2 * j + half, 40:80, :] = v_ref[j, 0:40, :]
                out_ref[2 * j + half, 80:82, :] = row_ref[source, 80:82, :]
                out_ref[2 * j + half, 82:88, :] = v_ref[j, 42:48, :]

    return on_scalars(body, (mine,), (row, v_part), (8, 88, 640))


def choose_one(column, mine, tile):
    def body(mine_ref, tile_ref, column_ref, out_ref):
        out_ref[...] = column_ref[within_column(mine_ref[tile_ref[0]])]

    return on_scalars(body, (mine, tile), (column,), (88, 640))


def on_scalars(body, scalars, arrays, shape):
    return pl.pallas_call(
        body,
        in_specs=[pl.BlockSpec(memory_space=pltpu.SMEM)] * len(scalars)
        + [pl.BlockSpec(memory_space=pltpu.VMEM)] * len(arrays),
        out_specs=pl.BlockSpec(memory_space=pltpu.VMEM),
        out_shape=jax.ShapeDtypeStruct(shape, BF16),
        compiler_params=pltpu.CompilerParams(vmem_limit_bytes=16 << 20),
    )(*scalars, *arrays)


def bases_of_tile(row, rows, four):
    mine = rows[0]
    v_part = exchange(choose_v(row, rows, lax.axis_index("mp")[None]), "mp")
    both = choose_both(row, v_part, mine)
    column = exchange(both, COLUMN)
    column, four = lax.optimization_barrier((column, four))
    one = choose_one(column, mine, lax.axis_index("yj")[None])
    whole = lax.all_gather(one[None], ROW, axis=0, tiled=True)
    u_tile = whole[:, :40].reshape(640, 640)
    v_tile = whole[:, 40:80].reshape(640, 640)
    ei = jnp.sum(whole[0, 80:82].astype(F32), axis=0)
    eo = jnp.sum(whole[0, 82:84].astype(F32), axis=0)
    return four, u_tile, v_tile, ei, eo


def shards(inputs, out_grads, doc_lengths, owners, basis_in, basis_out, eig_in, eig_out):
    sent = rows_sent(basis_in, basis_out, eig_in[0], eig_out[0])
    row, rows, parts = swapped(inputs, out_grads, owners[0], doc_lengths[0], sent)
    four, u, v, ei, eo = bases_of_tile(row, rows, row_sums(parts))
    gt = tile_of_gradient(four)
    first = (lax.axis_index(DP) % 32) * 20
    v_own = lax.dynamic_slice_in_dim(v, first.astype(jnp.uint32), 20, 0)
    rotated = jnp.dot(gt, u, preferred_element_type=F32).astype(BF16)
    twice = lax.dot_general(v, rotated, (((0,), (0,)), ((), ())), preferred_element_type=F32)
    scaled = (twice / (eo[:, None] * ei[None, :] + DAMPING)).astype(BF16)
    back = jnp.dot(v_own, scaled, preferred_element_type=F32).astype(BF16)
    out = lax.dot_general(back, u, (((1,), (1,)), ((), ())), preferred_element_type=F32)
    return out.astype(BF16).T


def solution(mesh):
    fine = Mesh(mesh.devices.reshape(SPLIT), AXES)
    split = P(DP, "mp")
    placed = (split, split, P(DP, None), P("mp", None), split, split, split, split)
    return jax.shard_map(
        shards, mesh=fine, in_specs=placed, out_specs=P("mp", DP), check_vma=False
    )
```

time: 218 us -> 166 us (0.76)
  waiting for transfers between devices: 68.9 us -> 34.3 us
  between operations: 40.2 us -> 13.7 us
  starting transfers between devices: 41.4 us -> 53.6 us
  local copies, waits for them, and re-layouts: 10.5 us -> 3.74 us
  blocking collectives: 43.8 us -> 39.6 us
  Pallas kernels: 0 us -> 4 us
    ppermute x3 -> x6, waiting for transfers between devices: 33.7 us -> 12 us  [shift(): return lax.ppermute(x, 'mp', [(i, i ^ distance) for i in range(4)])]
    all_to_all x5 -> x4, waiting for transfers between devices: 35.1 us -> 16.9 us  [exchange(): return lax.all_to_all(x, axes, split_axis=0, concat_axis=0, tiled=True)]
    ppermute x3 -> x6, starting transfers between devices: 9.82 us -> 25.1 us  [shift(): return lax.ppermute(x, 'mp', [(i, i ^ distance) for i in range(4)])]
    all_gather x4, blocking collectives: 23.9 us -> 15.8 us  [pool(): return lax.all_gather(x, 'c', axis=0, tiled=True)]
    reduce_scatter x1, waiting for transfers between devices: 0.02 us -> 5.35 us  [row_sums(): summed = lax.psum_scatter(parts, 'x', scatter_dimension=0, tiled=True)[0]]
    pallas_call x0 -> x3, Pallas kernels: none -> 4 us  [on_scalars(): pl.pallas_call(body, in_specs=[pl.BlockSpec(memory_space=pltpu.SMEM)] * l...]
    all_to_all x2 -> x1, blocking collectives: 19.9 us -> 23.8 us  [exchange(): return lax.all_to_all(x, axes, split_axis=0, concat_axis=0, tiled=True)]
    all_to_all x5 -> x4, starting transfers between devices: 31.5 us -> 28.4 us  [exchange(): return lax.all_to_all(x, axes, split_axis=0, concat_axis=0, tiled=True)]
  transfers between devices with their start and end apart: 10 -> 12, of which waited for: 5 -> 5; matrix products, arithmetic and copies ran while one was open for 7% -> 3% of each run, Pallas kernels for 0% -> 2%
where the time goes in v2:
time: 166 us; the launch traced here: 165 us
  starting transfers between devices  53.6 us (32%)
  blocking collectives  39.6 us (24%)
  waiting for transfers between devices  34.3 us (21%)
  between operations  13.7 us (8%)
  other arithmetic  9.52 us (6%)
  matrix products  6.95 us (4%)
  Pallas kernels  4 us (2%)
  local copies, waits for them, and re-layouts  3.74 us (2%)
    all_to_all x4, starting transfers between devices, exchange(): return lax.all_to_all(x, axes, split_axis=0, concat_axis=0, tiled=True)  28.4 us
    ppermute x6, starting transfers between devices, shift(): return lax.ppermute(x, 'mp', [(i, i ^ distance) for i in range(4)])  25.1 us
    all_to_all x1, blocking collectives, exchange(): return lax.all_to_all(x, axes, split_axis=0, concat_axis=0, tiled=True)  23.8 us
    all_to_all x4, waiting for transfers between devices, exchange(): return lax.all_to_all(x, axes, split_axis=0, concat_axis=0, tiled=True)  16.9 us
    all_gather x4, blocking collectives, pool(): return lax.all_gather(x, 'c', axis=0, tiled=True)  15.8 us
    ppermute x6, waiting for transfers between devices, shift(): return lax.ppermute(x, 'mp', [(i, i ^ distance) for i in range(4)])  12 us
    reduce_scatter x1, waiting for transfers between devices, row_sums(): summed = lax.psum_scatter(parts, 'x', scatter_dimension=0, tiled=True)[0]  5.35 us
    pallas_call x3, Pallas kernels, on_scalars(): pl.pallas_call(body, in_specs=[pl.BlockSpec(memory_space=pltpu.SMEM)] * l...  4 us
  transfers between devices with their start and end apart: 12, of which 5 were waited for; matrix products, arithmetic and copies ran while one was open for 3% of the time, Pallas kernels for 2%

profile of v2, /device:TPU:1, one launch (start us, length us, event | category | flops | bytes accessed | tf_op | source)
XLA Modules:
  0.0 165.4 jit_solution(16663122267705742978)
XLA Ops:
  7.3 2.8 %pad_maximum_fusion = bf16[16,88,640]{2,1,0:T(8,128)(2,1)} fusion(bf16[16,8,640]{2,1,0:T(8,128)(2,1)S(1)} %broadcast_in_dim.46, bf16[16,40,640]{2,1,0:T(8,128)(2,1)} %bitcast.85, bf16[16,40,640]{2,1,0:T(8,128)(2,1)} %bitcast.86), kind=kLoop, calls=%fused_computation | loop fusion | flops 5406720 | bytes 3604480 | tf_op jit(solution)/shard_map/concatenate | solution.py:55
  10.1 10.5 %all-to-all-start = ((bf16[16,88,640]{2,1,0:T(8,128)(2,1)}), bf16[16,88,640]{2,1,0:T(8,128)(2,1)S(1)}, u32[]{:S(2)}, u32[]{:S(2)}) async-start(bf16[16,88,640]{2,1,0:T(8,128)(2,1)} %pad_maximum_fusion), calls=%async_computation | async-start | bytes 3604480 | tf_op jit(solution)/shard_map/all_to_all | solution.py:29
  20.7 2.3 %all_gather.15 = bf16[512,640]{1,0:T(8,128)(2,1)S(1)} all-gather(bf16[256,640]{1,0:T(8,128)(2,1)S(1)} %copy-done), channel_id=1, replica_groups=mesh['yj'=4,'yh'=2,'x'=4,'zl'=2,'c'=2,'mp'=4] {'c'}, dimensions={0}, use_global_device_ids=true | all-gather | bytes 983040 | tf_op jit(solution)/shard_map/all_gather | solution.py:33
  23.2 7.1 %collective-permute-start.1 = (bf16[512,320]{1,0:T(8,128)(2,1)S(1)}, bf16[512,320]{1,0:T(8,128)(2,1)}, u32[]{:S(2)}, u32[]{:S(2)}) collective-permute-start(bf16[512,320]{1,0:T(8,128)(2,1)S(1)} %slice_select_fusion), channel_id=1, source_target_pairs={{0,3},{1,2},{2,1},{3,0},{4,7},{5,6},{6,5},{7,4},{8,11},{9,10},{10,... | collective-permute-start | bytes 983048 | tf_op jit(solution)/shard_map/ppermute | solution.py:64
  30.3 2.2 %collective-permute-start = (bf16[256,640]{1,0:T(8,128)(2,1)}, bf16[256,640]{1,0:T(8,128)(2,1)}, u32[]{:S(2)}, u32[]{:S(2)}) collective-permute-start(bf16[256,640]{1,0:T(8,128)(2,1)} %param.8), channel_id=1, source_target_pairs={{0,1},{1,0},{2,3},{3,2},{4,5},{5,4},{6,7},{7,6},{8,9},{9,8},{10,11... | collective-permute-start | bytes 983048 | tf_op jit(solution)/shard_map/ppermute | solution.py:64
  33.9 2.6 %all_gather.16 = bf16[512,640]{1,0:T(8,128)(2,1)S(1)} all-gather(bf16[256,640]{1,0:T(8,128)(2,1)S(1)} %multiply_convert_fusion.1), channel_id=1, replica_groups=mesh['yj'=4,'yh'=2,'x'=4,'zl'=2,'c'=2,'mp'=4] {'c'}, dimensions={0}, use_global_device_ids=true | all-gather | bytes 983040 | tf_op jit(solution)/shard_map/all_gather | solution.py:33
  37.0 1.9 %collective-permute-start.4 = (s32[4]{0:T(128)S(1)}, s32[4]{0:T(128)S(1)}, u32[]{:S(2)}, u32[]{:S(2)}) collective-permute-start(s32[4]{0:T(128)S(1)} %bitcast.90), channel_id=1, source_target_pairs={{0,3},{1,2},{2,1},{3,0},{4,7},{5,6},{6,5},{7,4},{8,11},{9,10},{10,... | collective-permute-start | bytes 56 | tf_op jit(solution)/shard_map/ppermute | solution.py:64
  38.9 4.0 %collective-permute-start.2 = (s32[4]{0:T(128)S(1)}, s32[4]{0:T(128)S(1)}, u32[]{:S(2)}, u32[]{:S(2)}) collective-permute-start(s32[4]{0:T(128)S(1)} %bitcast.91), channel_id=1, source_target_pairs={{0,1},{1,0},{2,3},{3,2},{4,5},{5,4},{6,7},{7,6},{8,9},{9,8},{10,11... | collective-permute-start | bytes 56 | tf_op jit(solution)/shard_map/ppermute | solution.py:64
  43.0 5.5 %collective-permute-start.3 = (s32[4]{0:T(128)S(1)}, s32[4]{0:T(128)S(1)}, u32[]{:S(2)}, u32[]{:S(2)}) collective-permute-start(s32[4]{0:T(128)S(1)} %bitcast.92), channel_id=1, source_target_pairs={{0,2},{1,3},{2,0},{3,1},{4,6},{5,7},{6,4},{7,5},{8,10},{9,11},{10,... | collective-permute-start | bytes 56 | tf_op jit(solution)/shard_map/ppermute | solution.py:64
  48.4 2.7 %collective-permute-done.3 = s32[4]{0:T(128)S(1)} collective-permute-done((s32[4]{0:T(128)S(1)}, s32[4]{0:T(128)S(1)}, u32[]{:S(2)}, u32[]{:S(2)}) %collective-permute-start.3) | collective-permute-done | bytes 48 | tf_op jit(solution)/shard_map/ppermute | solution.py:64
  52.3 3.7 %all_gather.17 = bf16[512,640]{1,0:T(8,128)(2,1)S(1)} all-gather(bf16[256,640]{1,0:T(8,128)(2,1)S(1)} %multiply_convert_fusion), channel_id=1, replica_groups=mesh['yj'=4,'yh'=2,'x'=4,'zl'=2,'c'=2,'mp'=4] {'c'}, dimensions={0}, use_global_device_ids=true | all-gather | bytes 983040 | tf_op jit(solution)/shard_map/all_gather | solution.py:33
  56.5 1.4 convolution_convert_fusion.1
  62.2 5.1 %all-to-all-start.1 = ((bf16[4,48,640]{2,1,0:T(8,128)(2,1)}), bf16[4,48,640]{2,1,0:T(8,128)(2,1)S(1)}, u32[]{:S(2)}, u32[]{:S(2)}) async-start(bf16[4,48,640]{2,1,0:T(8,128)(2,1)} %shard_map.82), calls=%async_computation.1 | async-start | bytes 491520 | tf_op jit(solution)/shard_map/all_to_all | solution.py:29
  67.3 8.4 %all-to-all-done.1.v_ref = bf16[4,48,640]{2,1,0:T(8,128)(2,1)S(1)} async-done(((bf16[4,48,640]{2,1,0:T(8,128)(2,1)}), bf16[4,48,640]{2,1,0:T(8,128)(2,1)S(1)}, u32[]{:S(2)}, u32[]{:S(2)}) %all-to-all-start.1) | async-done | bytes 245792 | tf_op jit(solution)/shard_map/all_to_all | solution.py:29
  75.7 1.5 shard_map.83
  77.3 8.2 %all-to-all-start.2 = ((bf16[8,88,640]{2,1,0:T(8,128)(2,1)}), bf16[8,88,640]{2,1,0:T(8,128)(2,1)S(1)}, u32[]{:S(2)}, u32[]{:S(2)}) async-start(bf16[8,88,640]{2,1,0:T(8,128)(2,1)} %shard_map.83), calls=%async_computation.2 | async-start | bytes 1802240 | tf_op jit(solution)/shard_map/all_to_all | solution.py:29
  85.5 5.3 %reduce-scatter.2.cloned.1.call-done = bf16[1,4,80,640]{3,2,1,0:T(8,128)(2,1)} async-done(((bf16[4,4,80,640]{3,2,1,0:T(8,128)(2,1)}), bf16[1,4,80,640]{3,2,1,0:T(8,128)(2,1)}) %reduce-scatter.2.cloned.1.call-update) | async-done | bytes 409616 | tf_op jit(solution)/shard_map/reduce_scatter | solution.py:89
  91.8 4.4 %collective-permute-start.5 = (bf16[2,80,640]{2,1,0:T(8,128)(2,1)S(1)}, bf16[2,80,640]{2,1,0:T(8,128)(2,1)S(1)}, u32[]{:S(2)}, u32[]{:S(2)}) collective-permute-start(bf16[2,80,640]{2,1,0:T(8,128)(2,1)S(1)} %slice_bitcast_fusion), channel_id=1, source_target_pairs={{0,1},{1,0},{2,3},{3,2},{4,5},{5,4},{6,7},{7,6},{8,9},{9,8},{10,11... | collective-permute-start | bytes 614408 | tf_op jit(solution)/shard_map/ppermute | solution.py:64
  96.3 9.3 %collective-permute-done.5 = bf16[2,80,640]{2,1,0:T(8,128)(2,1)S(1)} collective-permute-done((bf16[2,80,640]{2,1,0:T(8,128)(2,1)S(1)}, bf16[2,80,640]{2,1,0:T(8,128)(2,1)S(1)}, u32[]{:S(2)}, u32[]{:S(2)}) %collective-permute-start.5) | collective-permute-done | bytes 204832 | tf_op jit(solution)/shard_map/ppermute | solution.py:64
  107.9 23.8 %all_to_all.25 = bf16[16,20,640]{2,1,0:T(8,128)(2,1)S(1)} all-to-all(bf16[16,20,640]{2,1,0:T(8,128)(2,1)S(1)} %reshape.78), channel_id=1, replica_groups=mesh['yj'=4,'yh'=2,'x'=4,'zl'=2,'c'=2,'mp'=4] {'yj','yh','zl'}, dimensions={0} | all-to-all | bytes 819200 | tf_op jit(solution)/shard_map/all_to_all | solution.py:29
  132.6 4.6 %all-to-all-start.4 = ((bf16[16,20,640]{2,1,0:T(8,128)(2,1)}), bf16[16,20,640]{2,1,0:T(8,128)(2,1)S(1)}, u32[]{:S(2)}, u32[]{:S(2)}) async-start(bf16[16,20,640]{2,1,0:T(8,128)(2,1)} %broadcast_in_dim.53), calls=%async_computation.5 | async-start | bytes 983040 | tf_op jit(solution)/shard_map/all_to_all | solution.py:29
  137.3 8.4 %all-to-all-done.4 = bf16[16,20,640]{2,1,0:T(8,128)(2,1)S(1)} async-done(((bf16[16,20,640]{2,1,0:T(8,128)(2,1)}), bf16[16,20,640]{2,1,0:T(8,128)(2,1)S(1)}, u32[]{:S(2)}, u32[]{:S(2)}) %all-to-all-start.4) | async-done | bytes 409632 | tf_op jit(solution)/shard_map/all_to_all | solution.py:29
  145.8 7.2 %all_gather.19 = bf16[640,640]{1,0:T(8,128)(2,1)S(1)} all-gather(bf16[320,640]{1,0:T(8,128)(2,1)S(1)} %reshape.79), channel_id=1, replica_groups=mesh['yj'=4,'yh'=2,'x'=4,'zl'=2,'c'=2,'mp'=4] {'c'}, dimensions={0}, use_global_device_ids=true | all-gather | bytes 1228800 | tf_op jit(solution)/shard_map/all_gather | solution.py:33
  153.0 1.5 fusion.12
  (50 shorter events, 17.0 us)
Async XLA Ops:
  10.1 10.6 %copy-start = (bf16[256,640]{1,0:T(8,128)(2,1)S(1)}, bf16[256,640]{1,0:T(8,128)(2,1)}, u32[]{:S(2)}) copy-start(bf16[256,640]{1,0:T(8,128)(2,1)} %param.9) | copy-start | bytes 983044
  10.1 41.1 %all-to-all-start = ((bf16[16,88,640]{2,1,0:T(8,128)(2,1)}), bf16[16,88,640]{2,1,0:T(8,128)(2,1)S(1)}, u32[]{:S(2)}, u32[]{:S(2)}) async-start(bf16[16,88,640]{2,1,0:T(8,128)(2,1)} %pad_maximum_fusion), calls=%async_computation | async-start | bytes 3604480 | tf_op jit(solution)/shard_map/all_to_all | solution.py:29
  20.6 11.8 %copy-start.1 = (s32[1,16]{1,0:T(1,128)S(1)}, s32[1,16]{1,0:T(1,128)}, u32[]{:S(2)}) copy-start(s32[1,16]{1,0:T(1,128)} %param.10) | copy-start | bytes 196
  20.6 70.2 %reduce-scatter.2.cloned.1.call-start = ((), (), s32[]{:S(2)}) async-start(), calls=%async_computation.6 | async-start | bytes 2048000 | tf_op jit(solution)/shard_map/reduce_scatter | solution.py:89
  23.2 13.8 %copy-start.2 = (s32[1,4]{1,0:T(1,128)S(1)}, s32[1,4]{1,0:T(1,128)}, u32[]{:S(2)}) copy-start(s32[1,4]{1,0:T(1,128)} %param.11) | copy-start | bytes 52
  23.2 28.0 %collective-permute-start.1 = (bf16[512,320]{1,0:T(8,128)(2,1)S(1)}, bf16[512,320]{1,0:T(8,128)(2,1)}, u32[]{:S(2)}, u32[]{:S(2)}) collective-permute-start(bf16[512,320]{1,0:T(8,128)(2,1)S(1)} %slice_select_fusion), channel_id=1, source_target_pairs={{0,3},{1,2},{2,1},{3,0},{4,7},{5,6},{6,5},{7,4},{8,11},{9,10},{10,... | collective-permute-start | bytes 983048 | tf_op jit(solution)/shard_map/ppermute | solution.py:64
  30.3 20.9 %collective-permute-start = (bf16[256,640]{1,0:T(8,128)(2,1)}, bf16[256,640]{1,0:T(8,128)(2,1)}, u32[]{:S(2)}, u32[]{:S(2)}) collective-permute-start(bf16[256,640]{1,0:T(8,128)(2,1)} %param.8), channel_id=1, source_target_pairs={{0,1},{1,0},{2,3},{3,2},{4,5},{5,4},{6,7},{7,6},{8,9},{9,8},{10,11... | collective-permute-start | bytes 983048 | tf_op jit(solution)/shard_map/ppermute | solution.py:64
  37.0 11.4 %collective-permute-start.4 = (s32[4]{0:T(128)S(1)}, s32[4]{0:T(128)S(1)}, u32[]{:S(2)}, u32[]{:S(2)}) collective-permute-start(s32[4]{0:T(128)S(1)} %bitcast.90), channel_id=1, source_target_pairs={{0,3},{1,2},{2,1},{3,0},{4,7},{5,6},{6,5},{7,4},{8,11},{9,10},{10,... | collective-permute-start | bytes 56 | tf_op jit(solution)/shard_map/ppermute | solution.py:64
  38.9 9.5 %collective-permute-start.2 = (s32[4]{0:T(128)S(1)}, s32[4]{0:T(128)S(1)}, u32[]{:S(2)}, u32[]{:S(2)}) collective-permute-start(s32[4]{0:T(128)S(1)} %bitcast.91), channel_id=1, source_target_pairs={{0,1},{1,0},{2,3},{3,2},{4,5},{5,4},{6,7},{7,6},{8,9},{9,8},{10,11... | collective-permute-start | bytes 56 | tf_op jit(solution)/shard_map/ppermute | solution.py:64
  43.0 8.2 %collective-permute-start.3 = (s32[4]{0:T(128)S(1)}, s32[4]{0:T(128)S(1)}, u32[]{:S(2)}, u32[]{:S(2)}) collective-permute-start(s32[4]{0:T(128)S(1)} %bitcast.92), channel_id=1, source_target_pairs={{0,2},{1,3},{2,0},{3,1},{4,6},{5,7},{6,4},{7,5},{8,10},{9,11},{10,... | collective-permute-start | bytes 56 | tf_op jit(solution)/shard_map/ppermute | solution.py:64
  62.2 13.6 %all-to-all-start.1 = ((bf16[4,48,640]{2,1,0:T(8,128)(2,1)}), bf16[4,48,640]{2,1,0:T(8,128)(2,1)S(1)}, u32[]{:S(2)}, u32[]{:S(2)}) async-start(bf16[4,48,640]{2,1,0:T(8,128)(2,1)} %shard_map.82), calls=%async_computation.1 | async-start | bytes 491520 | tf_op jit(solution)/shard_map/all_to_all | solution.py:29
  77.3 29.4 %all-to-all-start.2 = ((bf16[8,88,640]{2,1,0:T(8,128)(2,1)}), bf16[8,88,640]{2,1,0:T(8,128)(2,1)S(1)}, u32[]{:S(2)}, u32[]{:S(2)}) async-start(bf16[8,88,640]{2,1,0:T(8,128)(2,1)} %shard_map.83), calls=%async_computation.2 | async-start | bytes 1802240 | tf_op jit(solution)/shard_map/all_to_all | solution.py:29
  85.5 67.5 %all-gather.3.cloned.1.call-start = ((), (), s32[]{:S(2)}) async-start(), calls=%async_computation.7 | async-start | bytes 1914880 | tf_op jit(solution)/shard_map/all_gather | solution.py:157
  91.8 13.7 %collective-permute-start.5 = (bf16[2,80,640]{2,1,0:T(8,128)(2,1)S(1)}, bf16[2,80,640]{2,1,0:T(8,128)(2,1)S(1)}, u32[]{:S(2)}, u32[]{:S(2)}) collective-permute-start(bf16[2,80,640]{2,1,0:T(8,128)(2,1)S(1)} %slice_bitcast_fusion), channel_id=1, source_target_pairs={{0,1},{1,0},{2,3},{3,2},{4,5},{5,4},{6,7},{7,6},{8,9},{9,8},{10,11... | collective-permute-start | bytes 614408 | tf_op jit(solution)/shard_map/ppermute | solution.py:64
  132.6 13.1 %all-to-all-start.4 = ((bf16[16,20,640]{2,1,0:T(8,128)(2,1)}), bf16[16,20,640]{2,1,0:T(8,128)(2,1)S(1)}, u32[]{:S(2)}, u32[]{:S(2)}) async-start(bf16[16,20,640]{2,1,0:T(8,128)(2,1)} %broadcast_in_dim.53), calls=%async_computation.5 | async-start | bytes 983040 | tf_op jit(solution)/shard_map/all_to_all | solution.py:29
Sparse Core Ops, SparseCore 0:
  60.9 29.8 reduce-scatter.1
  108.0 44.9 all-gather.2

commit v3 on v2

--- a/solution.py
+++ b/solution.py
@@ -55,38 +55,41 @@
     return jnp.concatenate([u.reshape(16, 40, 640), v.reshape(16, 40, 640), small], axis=1)
 
 
-def product(g, x):
-    d = lax.dot_general(g, x, (((0,), (0,)), ((), ())), preferred_element_type=F32)
-    return d.astype(BF16).reshape(4, 1, 80, 640)
+def products(xs, gs):
+    def body(x_ref, x_next_ref, g_ref, g_across_ref, out_ref):
+        pairs = [(x, g) for x in (x_ref, x_next_ref) for g in (g_ref, g_across_ref)]
+        for i, (x, g) in enumerate(pairs):
+            whole = lax.dot_general(
+                g[...], x[...], (((0,), (0,)), ((), ())), preferred_element_type=F32
+            ).astype(BF16)
+            for place in range(4):
+                out_ref[place, i] = whole[place * 80 : place * 80 + 80]
+
+    return on_scalars(body, (), (*xs, *gs), (4, 4, 80, 640))
 
 
 def shift(x, distance):
     return lax.ppermute(x, "mp", [(i, i ^ distance) for i in range(4)])
 
 
-def swapped(inputs, out_grads, owners, lengths, sent):
+def first_phase(inputs, out_grads, owners, lengths, sent):
+    row = exchange(sent, ROW)
     weights = token_weights(lengths, inputs.shape[0], lax.axis_size(DP))[:, None]
-
-    def weigh(x):
-        return pool((x.astype(F32) * weights).astype(BF16))
-
+    x = (inputs.astype(F32) * weights).astype(BF16)
+    x_next = shift(x, 1)
     g = pool(out_grads)
     g = jnp.where(lax.axis_index("c") == 0, g[:, :320], g[:, 320:])
-    row = exchange(sent, ROW)
-    x_next = shift(inputs, 1)
     g_across = shift(g, 3)
-    x = weigh(inputs)
-    near = product(g, x)
-    owners, near = lax.optimization_barrier((owners, near))
+    x = pool(x)
+    owners, x, g = lax.optimization_barrier((owners, x, g))
     rows = jnp.stack([owners] + [shift(owners, d) for d in (1, 2, 3)])
-    row, x_next, g_across, rows = lax.optimization_barrier((row, x_next, g_across, rows))
-    x_next = weigh(x_next)
-    parts = [near, product(g_across, x), product(g, x_next), product(g_across, x_next)]
-    return row, rows, jnp.concatenate(parts, axis=1)
-
-
-def row_sums(parts):
-    summed = lax.psum_scatter(parts, "x", scatter_dimension=0, tiled=True)[0]
+    row, rows, x, x_next, g, g_across = lax.optimization_barrier(
+        (row, rows, x, x_next, g, g_across)
+    )
+    return row, rows, products((x, pool(x_next)), (g, g_across))
+
+
+def row_of_gradient(summed):
     back = shift(summed[2:], 1)
     return jnp.stack(by_block([summed[0], back[0], back[1], summed[1]]))
 
@@ -147,34 +150,58 @@
     )(*scalars, *arrays)
 
 
-def bases_of_tile(row, rows, four):
+def bases_of_tile(row, rows, summed):
     mine = rows[0]
     v_part = exchange(choose_v(row, rows, lax.axis_index("mp")[None]), "mp")
     both = choose_both(row, v_part, mine)
     column = exchange(both, COLUMN)
-    column, four = lax.optimization_barrier((column, four))
+    column, four = lax.optimization_barrier((column, row_of_gradient(summed)))
     one = choose_one(column, mine, lax.axis_index("yj")[None])
-    whole = lax.all_gather(one[None], ROW, axis=0, tiled=True)
-    u_tile = whole[:, :40].reshape(640, 640)
-    v_tile = whole[:, 40:80].reshape(640, 640)
-    ei = jnp.sum(whole[0, 80:82].astype(F32), axis=0)
-    eo = jnp.sum(whole[0, 82:84].astype(F32), axis=0)
-    return four, u_tile, v_tile, ei, eo
+    return four, lax.all_gather(one[None], ROW, axis=0, tiled=True)
+
+
+def precondition(gt, bases, first):
+    def body(first_ref, gt_ref, bases_ref, out_ref, u_ref, v_ref):
+        for b in range(16):
+            u_ref[b * 40 : b * 40 + 40, :] = bases_ref[b, 0:40, :]
+            v_ref[b * 40 : b * 40 + 40, :] = bases_ref[b, 40:80, :]
+        small = bases_ref[0, 80:84, :].astype(F32)
+        ei = small[0:1] + small[1:2]
+        eo = small[2:3] + small[3:4]
+        u = u_ref[...]
+        v = v_ref[...]
+        at = lax.broadcasted_iota(jnp.int32, (24, 640), 1) - first_ref[0]
+        own = (at == lax.broadcasted_iota(jnp.int32, (24, 640), 0)).astype(F32).astype(BF16)
+        v_own = jnp.dot(own, v, preferred_element_type=F32).astype(BF16)
+        rotated = jnp.dot(gt_ref[...], u, preferred_element_type=F32).astype(BF16)
+        twice = lax.dot_general(
+            rotated, v, (((0,), (0,)), ((), ())), preferred_element_type=F32
+        )
+        scaled = (twice / (ei.T * eo + DAMPING)).astype(BF16)
+        back = lax.dot_general(
+            v_own, scaled, (((1,), (1,)), ((), ())), preferred_element_type=F32
+        ).astype(BF16)
+        out = lax.dot_general(back, u, (((1,), (1,)), ((), ())), preferred_element_type=F32)
+        out_ref[...] = out.astype(BF16)
+
+    return pl.pallas_call(
+        body,
+        in_specs=[pl.BlockSpec(memory_space=pltpu.SMEM)]
+        + [pl.BlockSpec(memory_space=pltpu.VMEM)] * 2,
+        out_specs=pl.BlockSpec(memory_space=pltpu.VMEM),
+        out_shape=jax.ShapeDtypeStruct((24, 640), BF16),
+        scratch_shapes=[pltpu.VMEM((640, 640), BF16), pltpu.VMEM((640, 640), BF16)],
+        compiler_params=pltpu.CompilerParams(vmem_limit_bytes=24 << 20),
+    )(first, gt, bases)
 
 
 def shards(inputs, out_grads, doc_lengths, owners, basis_in, basis_out, eig_in, eig_out):
     sent = rows_sent(basis_in, basis_out, eig_in[0], eig_out[0])
-    row, rows, parts = swapped(inputs, out_grads, owners[0], doc_lengths[0], sent)
-    four, u, v, ei, eo = bases_of_tile(row, rows, row_sums(parts))
-    gt = tile_of_gradient(four)
-    first = (lax.axis_index(DP) % 32) * 20
-    v_own = lax.dynamic_slice_in_dim(v, first.astype(jnp.uint32), 20, 0)
-    rotated = jnp.dot(gt, u, preferred_element_type=F32).astype(BF16)
-    twice = lax.dot_general(v, rotated, (((0,), (0,)), ((), ())), preferred_element_type=F32)
-    scaled = (twice / (eo[:, None] * ei[None, :] + DAMPING)).astype(BF16)
-    back = jnp.dot(v_own, scaled, preferred_element_type=F32).astype(BF16)
-    out = lax.dot_general(back, u, (((1,), (1,)), ((), ())), preferred_element_type=F32)
-    return out.astype(BF16).T
+    row, rows, parts = first_phase(inputs, out_grads, owners[0], doc_lengths[0], sent)
+    summed = lax.psum_scatter(parts, "x", scatter_dimension=0, tiled=True)[0]
+    four, bases = bases_of_tile(row, rows, summed)
+    first = ((lax.axis_index(DP) % 32) * 20)[None]
+    return precondition(tile_of_gradient(four), bases, first)[:20].T
 
 
 def solution(mesh):

time: 166 us -> 162 us (0.976)
  matrix products: 6.95 us -> 0 us
  Pallas kernels: 4 us -> 8.78 us
  other arithmetic: 9.52 us -> 5.97 us
    dot_general x7 -> x0, matrix products: 6.95 us -> none  [the longest x4 3.79 us: product(): lax.dot_general(g, x, (((0,), (0,)), ((), ())), preferred_element_type=F32)]
    pallas_call x3 -> x4, Pallas kernels: 4 us -> 6.45 us  [on_scalars(): pl.pallas_call(body, in_specs=[pl.BlockSpec(memory_space=pltpu.SMEM)] * l...]
    pallas_call x0 -> x1, Pallas kernels: none -> 2.33 us  [precondition(): pl.pallas_call(body, in_specs=[pl.BlockSpec(memory_space=pltpu.SMEM)] + [...]
  transfers between devices with their start and end apart: 12 -> 12, of which waited for: 5 -> 7; matrix products, arithmetic and copies ran while one was open for 3% -> 3% of each run, Pallas kernels for 2% -> 2%
where the time goes in v3:
time: 162 us; the launch traced here: 161 us
  starting transfers between devices  53.3 us (33%)
  blocking collectives  40.1 us (25%)
  waiting for transfers between devices  34.9 us (22%)
  between operations  13.7 us (8%)
  Pallas kernels  8.78 us (5%)
  other arithmetic  5.97 us (4%)
  local copies, waits for them, and re-layouts  4.36 us (3%)
    all_to_all x4, starting transfers between devices, exchange(): return lax.all_to_all(x, axes, split_axis=0, concat_axis=0, tiled=True)  28.1 us
    ppermute x6, starting transfers between devices, shift(): return lax.ppermute(x, 'mp', [(i, i ^ distance) for i in range(4)])  25.1 us
    all_to_all x1, blocking collectives, exchange(): return lax.all_to_all(x, axes, split_axis=0, concat_axis=0, tiled=True)  22.8 us
    all_gather x4, blocking collectives, pool(): return lax.all_gather(x, 'c', axis=0, tiled=True)  17.2 us
    all_to_all x4, waiting for transfers between devices, exchange(): return lax.all_to_all(x, axes, split_axis=0, concat_axis=0, tiled=True)  16.4 us
    ppermute x6, waiting for transfers between devices, shift(): return lax.ppermute(x, 'mp', [(i, i ^ distance) for i in range(4)])  11.9 us
    pallas_call x4, Pallas kernels, on_scalars(): pl.pallas_call(body, in_specs=[pl.BlockSpec(memory_space=pltpu.SMEM)] * l...  6.45 us
    reduce_scatter x1, waiting for transfers between devices, shards(): summed = lax.psum_scatter(parts, 'x', scatter_dimension=0, tiled=True)[0]  6.13 us
  transfers between devices with their start and end apart: 12, of which 7 were waited for; matrix products, arithmetic and copies ran while one was open for 3% of the time, Pallas kernels for 2%

profile of v3, /device:TPU:1, one launch (start us, length us, event | category | flops | bytes accessed | tf_op | source)
XLA Modules:
  0.0 161.0 jit_solution(13566390403713269744)
XLA Ops:
  7.3 2.8 %pad_maximum_fusion = bf16[16,88,640]{2,1,0:T(8,128)(2,1)} fusion(bf16[16,8,640]{2,1,0:T(8,128)(2,1)S(1)} %broadcast_in_dim.48, bf16[16,40,640]{2,1,0:T(8,128)(2,1)} %bitcast.54, bf16[16,40,640]{2,1,0:T(8,128)(2,1)} %bitcast.55), kind=kLoop, calls=%fused_computation | loop fusion | flops 5406720 | bytes 3604480 | tf_op jit(solution)/shard_map/concatenate | solution.py:55
  10.1 10.5 %all-to-all-start = ((bf16[16,88,640]{2,1,0:T(8,128)(2,1)}), bf16[16,88,640]{2,1,0:T(8,128)(2,1)S(1)}, u32[]{:S(2)}, u32[]{:S(2)}) async-start(bf16[16,88,640]{2,1,0:T(8,128)(2,1)} %pad_maximum_fusion), calls=%async_computation | async-start | bytes 3604480 | tf_op jit(solution)/shard_map/all_to_all | solution.py:29
  21.9 2.3 %collective-permute-start.3 = (bf16[256,640]{1,0:T(8,128)(2,1)}, bf16[256,640]{1,0:T(8,128)(2,1)}, u32[]{:S(2)}, u32[]{:S(2)}) collective-permute-start(bf16[256,640]{1,0:T(8,128)(2,1)} %multiply_convert_fusion), channel_id=1, source_target_pairs={{0,1},{1,0},{2,3},{3,2},{4,5},{5,4},{6,7},{7,6},{8,9},{9,8},{10,11... | collective-permute-start | bytes 983048 | tf_op jit(solution)/shard_map/ppermute | solution.py:72
  24.2 2.3 %all_gather.16 = bf16[512,640]{1,0:T(8,128)(2,1)S(1)} all-gather(bf16[256,640]{1,0:T(8,128)(2,1)S(1)} %copy-done.2), channel_id=1, replica_groups=mesh['yj'=4,'yh'=2,'x'=4,'zl'=2,'c'=2,'mp'=4] {'c'}, dimensions={0}, use_global_device_ids=true | all-gather | bytes 983040 | tf_op jit(solution)/shard_map/all_gather | solution.py:33
  26.7 7.0 %collective-permute-start.4 = (bf16[512,320]{1,0:T(8,128)(2,1)S(1)}, bf16[512,320]{1,0:T(8,128)(2,1)S(1)}, u32[]{:S(2)}, u32[]{:S(2)}) collective-permute-start(bf16[512,320]{1,0:T(8,128)(2,1)S(1)} %slice_select_fusion.g_ref), channel_id=1, source_target_pairs={{0,3},{1,2},{2,1},{3,0},{4,7},{5,6},{6,5},{7,4},{8,11},{9,10},{10,... | collective-permute-start | bytes 983048 | tf_op jit(solution)/shard_map/ppermute | solution.py:72
  33.7 2.8 %all_gather.15.x_ref = bf16[512,640]{1,0:T(8,128)(2,1)S(1)} all-gather(bf16[256,640]{1,0:T(8,128)(2,1)} %multiply_convert_fusion), channel_id=1, replica_groups=mesh['yj'=4,'yh'=2,'x'=4,'zl'=2,'c'=2,'mp'=4] {'c'}, dimensions={0}, use_global_device_ids=true | all-gather | bytes 983040 | tf_op jit(solution)/shard_map/all_gather | solution.py:33
  36.5 1.9 %collective-permute-start.2 = (s32[4]{0:T(128)S(1)}, s32[4]{0:T(128)S(1)}, u32[]{:S(2)}, u32[]{:S(2)}) collective-permute-start(s32[4]{0:T(128)S(1)} %bitcast.58), channel_id=1, source_target_pairs={{0,3},{1,2},{2,1},{3,0},{4,7},{5,6},{6,5},{7,4},{8,11},{9,10},{10,... | collective-permute-start | bytes 56 | tf_op jit(solution)/shard_map/ppermute | solution.py:72
  38.4 7.3 %collective-permute-start.1 = (s32[4]{0:T(128)S(1)}, s32[4]{0:T(128)S(1)}, u32[]{:S(2)}, u32[]{:S(2)}) collective-permute-start(s32[4]{0:T(128)S(1)} %bitcast.59), channel_id=1, source_target_pairs={{0,2},{1,3},{2,0},{3,1},{4,6},{5,7},{6,4},{7,5},{8,10},{9,11},{10,... | collective-permute-start | bytes 56 | tf_op jit(solution)/shard_map/ppermute | solution.py:72
  45.7 2.2 %collective-permute-start = (s32[4]{0:T(128)S(1)}, s32[4]{0:T(128)S(1)}, u32[]{:S(2)}, u32[]{:S(2)}) collective-permute-start(s32[4]{0:T(128)S(1)} %bitcast.60), channel_id=1, source_target_pairs={{0,1},{1,0},{2,3},{3,2},{4,5},{5,4},{6,7},{7,6},{8,9},{9,8},{10,11... | collective-permute-start | bytes 56 | tf_op jit(solution)/shard_map/ppermute | solution.py:72
  47.9 2.3 %collective-permute-done.2 = s32[4]{0:T(128)S(1)} collective-permute-done((s32[4]{0:T(128)S(1)}, s32[4]{0:T(128)S(1)}, u32[]{:S(2)}, u32[]{:S(2)}) %collective-permute-start.2) | collective-permute-done | bytes 48 | tf_op jit(solution)/shard_map/ppermute | solution.py:72
  50.9 4.2 %all_gather.17.x_next_ref = bf16[512,640]{1,0:T(8,128)(2,1)S(1)} all-gather(bf16[256,640]{1,0:T(8,128)(2,1)} %collective-permute-done.3), channel_id=1, replica_groups=mesh['yj'=4,'yh'=2,'x'=4,'zl'=2,'c'=2,'mp'=4] {'c'}, dimensions={0}, use_global_device_ids=true | all-gather | bytes 983040 | tf_op jit(solution)/shard_map/all_gather | solution.py:33
  55.1 2.4 %shard_map.84 = bf16[4,4,80,640]{3,2,1,0:T(8,128)(2,1)} custom-call(bf16[512,640]{1,0:T(8,128)(2,1)S(1)} %all_gather.15.x_ref, bf16[512,640]{1,0:T(8,128)(2,1)S(1)} %all_gather.17.x_next_ref, bf16[512,320]{1,0:T(8,128)(2,1)S(1)} %slice_select_fusion.g_ref, bf16[512,320]{1,0:T(8,128)(2,1)S(1)} %collective-permute-done.4.g_across_ref), custom_call_target="tpu_custom_call" | custom-call | tf_op jit(solution)/shard_map/pallas_call | solution.py:143
  58.9 4.2 %all-to-all-start.1 = ((bf16[4,48,640]{2,1,0:T(8,128)(2,1)}), bf16[4,48,640]{2,1,0:T(8,128)(2,1)S(1)}, u32[]{:S(2)}, u32[]{:S(2)}) async-start(bf16[4,48,640]{2,1,0:T(8,128)(2,1)} %shard_map.82), calls=%async_computation.1 | async-start | bytes 491520 | tf_op jit(solution)/shard_map/all_to_all | solution.py:29
  63.1 8.2 %all-to-all-done.1.v_ref = bf16[4,48,640]{2,1,0:T(8,128)(2,1)S(1)} async-done(((bf16[4,48,640]{2,1,0:T(8,128)(2,1)}), bf16[4,48,640]{2,1,0:T(8,128)(2,1)S(1)}, u32[]{:S(2)}, u32[]{:S(2)}) %all-to-all-start.1) | async-done | bytes 245792 | tf_op jit(solution)/shard_map/all_to_all | solution.py:29
  71.3 1.5 shard_map.83
  72.9 9.4 %all-to-all-start.2 = ((bf16[8,88,640]{2,1,0:T(8,128)(2,1)}), bf16[8,88,640]{2,1,0:T(8,128)(2,1)S(1)}, u32[]{:S(2)}, u32[]{:S(2)}) async-start(bf16[8,88,640]{2,1,0:T(8,128)(2,1)} %shard_map.83), calls=%async_computation.2 | async-start | bytes 1802240 | tf_op jit(solution)/shard_map/all_to_all | solution.py:29
  82.4 6.1 %reduce-scatter.2.cloned.1.call-done = bf16[1,4,80,640]{3,2,1,0:T(8,128)(2,1)} async-done(((bf16[4,4,80,640]{3,2,1,0:T(8,128)(2,1)}), bf16[1,4,80,640]{3,2,1,0:T(8,128)(2,1)}) %reduce-scatter.2.cloned.1.call-update) | async-done | bytes 409616 | tf_op jit(solution)/shard_map/reduce_scatter | solution.py:201
  89.5 4.4 %collective-permute-start.5 = (bf16[2,80,640]{2,1,0:T(8,128)(2,1)S(1)}, bf16[2,80,640]{2,1,0:T(8,128)(2,1)S(1)}, u32[]{:S(2)}, u32[]{:S(2)}) collective-permute-start(bf16[2,80,640]{2,1,0:T(8,128)(2,1)S(1)} %slice_bitcast_fusion), channel_id=1, source_target_pairs={{0,1},{1,0},{2,3},{3,2},{4,5},{5,4},{6,7},{7,6},{8,9},{9,8},{10,11... | collective-permute-start | bytes 614408 | tf_op jit(solution)/shard_map/ppermute | solution.py:72
  93.9 8.9 %collective-permute-done.5 = bf16[2,80,640]{2,1,0:T(8,128)(2,1)S(1)} collective-permute-done((bf16[2,80,640]{2,1,0:T(8,128)(2,1)S(1)}, bf16[2,80,640]{2,1,0:T(8,128)(2,1)S(1)}, u32[]{:S(2)}, u32[]{:S(2)}) %collective-permute-start.5) | collective-permute-done | bytes 204832 | tf_op jit(solution)/shard_map/ppermute | solution.py:72
  105.2 22.8 %all_to_all.25 = bf16[16,20,640]{2,1,0:T(8,128)(2,1)S(1)} all-to-all(bf16[16,20,640]{2,1,0:T(8,128)(2,1)S(1)} %reshape.50), channel_id=1, replica_groups=mesh['yj'=4,'yh'=2,'x'=4,'zl'=2,'c'=2,'mp'=4] {'yj','yh','zl'}, dimensions={0} | all-to-all | bytes 819200 | tf_op jit(solution)/shard_map/all_to_all | solution.py:29
  128.9 4.0 %all-to-all-start.4 = ((bf16[16,20,640]{2,1,0:T(8,128)(2,1)}), bf16[16,20,640]{2,1,0:T(8,128)(2,1)S(1)}, u32[]{:S(2)}, u32[]{:S(2)}) async-start(bf16[16,20,640]{2,1,0:T(8,128)(2,1)} %broadcast_in_dim.53), calls=%async_computation.5 | async-start | bytes 983040 | tf_op jit(solution)/shard_map/all_to_all | solution.py:29
  133.0 8.1 %all-to-all-done.4 = bf16[16,20,640]{2,1,0:T(8,128)(2,1)S(1)} async-done(((bf16[16,20,640]{2,1,0:T(8,128)(2,1)}), bf16[16,20,640]{2,1,0:T(8,128)(2,1)S(1)}, u32[]{:S(2)}, u32[]{:S(2)}) %all-to-all-start.4) | async-done | bytes 409632 | tf_op jit(solution)/shard_map/all_to_all | solution.py:29
  141.2 8.0 %all_gather.18.gt_ref = bf16[640,640]{1,0:T(8,128)(2,1)S(1)} all-gather(bf16[320,640]{1,0:T(8,128)(2,1)S(1)} %reshape.51), channel_id=1, replica_groups=mesh['yj'=4,'yh'=2,'x'=4,'zl'=2,'c'=2,'mp'=4] {'c'}, dimensions={0}, use_global_device_ids=true | all-gather | bytes 1228800 | tf_op jit(solution)/shard_map/all_gather | solution.py:33
  151.1 2.3 %shard_map.86 = bf16[24,640]{1,0:T(8,128)(2,1)S(1)} custom-call(s32[1]{0:T(128)} %bitcast.first_ref, bf16[640,640]{1,0:T(8,128)(2,1)S(1)} %all_gather.18.gt_ref, bf16[16,88,640]{2,1,0:T(8,128)(2,1)S(1)} %bitcast.53), custom_call_target="tpu_custom_call" | custom-call | tf_op jit(solution)/shard_map/pallas_call | solution.py:187
  (46 shorter events, 11.2 us)
Async XLA Ops:
  10.1 10.6 %copy-start.3 = (s32[1,16]{1,0:T(1,128)S(1)}, s32[1,16]{1,0:T(1,128)}, u32[]{:S(2)}) copy-start(s32[1,16]{1,0:T(1,128)} %param.10) | copy-start | bytes 196
  10.1 10.9 %copy-start.1 = (bf16[256,640]{1,0:T(8,128)(2,1)S(1)}, bf16[256,640]{1,0:T(8,128)(2,1)}, u32[]{:S(2)}) copy-start(bf16[256,640]{1,0:T(8,128)(2,1)} %param.8) | copy-start | bytes 983044
  10.1 14.1 %copy-start.2 = (bf16[256,640]{1,0:T(8,128)(2,1)S(1)}, bf16[256,640]{1,0:T(8,128)(2,1)}, u32[]{:S(2)}) copy-start(bf16[256,640]{1,0:T(8,128)(2,1)} %param.9) | copy-start | bytes 983044
  10.1 40.8 %all-to-all-start = ((bf16[16,88,640]{2,1,0:T(8,128)(2,1)}), bf16[16,88,640]{2,1,0:T(8,128)(2,1)S(1)}, u32[]{:S(2)}, u32[]{:S(2)}) async-start(bf16[16,88,640]{2,1,0:T(8,128)(2,1)} %pad_maximum_fusion), calls=%async_computation | async-start | bytes 3604480 | tf_op jit(solution)/shard_map/all_to_all | solution.py:29
  20.6 67.9 %reduce-scatter.2.cloned.1.call-start = ((), (), s32[]{:S(2)}) async-start(), calls=%async_computation.6 | async-start | bytes 2048000 | tf_op jit(solution)/shard_map/reduce_scatter | solution.py:201
  21.1 15.4 %copy-start.4 = (s32[1,4]{1,0:T(1,128)S(1)}, s32[1,4]{1,0:T(1,128)}, u32[]{:S(2)}) copy-start(s32[1,4]{1,0:T(1,128)} %param.11) | copy-start | bytes 52
  21.9 29.0 %collective-permute-start.3 = (bf16[256,640]{1,0:T(8,128)(2,1)}, bf16[256,640]{1,0:T(8,128)(2,1)}, u32[]{:S(2)}, u32[]{:S(2)}) collective-permute-start(bf16[256,640]{1,0:T(8,128)(2,1)} %multiply_convert_fusion), channel_id=1, source_target_pairs={{0,1},{1,0},{2,3},{3,2},{4,5},{5,4},{6,7},{7,6},{8,9},{9,8},{10,11... | collective-permute-start | bytes 983048 | tf_op jit(solution)/shard_map/ppermute | solution.py:72
  26.7 24.2 %collective-permute-start.4 = (bf16[512,320]{1,0:T(8,128)(2,1)S(1)}, bf16[512,320]{1,0:T(8,128)(2,1)S(1)}, u32[]{:S(2)}, u32[]{:S(2)}) collective-permute-start(bf16[512,320]{1,0:T(8,128)(2,1)S(1)} %slice_select_fusion.g_ref), channel_id=1, source_target_pairs={{0,3},{1,2},{2,1},{3,0},{4,7},{5,6},{6,5},{7,4},{8,11},{9,10},{10,... | collective-permute-start | bytes 983048 | tf_op jit(solution)/shard_map/ppermute | solution.py:72
  36.5 13.7 %collective-permute-start.2 = (s32[4]{0:T(128)S(1)}, s32[4]{0:T(128)S(1)}, u32[]{:S(2)}, u32[]{:S(2)}) collective-permute-start(s32[4]{0:T(128)S(1)} %bitcast.58), channel_id=1, source_target_pairs={{0,3},{1,2},{2,1},{3,0},{4,7},{5,6},{6,5},{7,4},{8,11},{9,10},{10,... | collective-permute-start | bytes 56 | tf_op jit(solution)/shard_map/ppermute | solution.py:72
  38.4 11.8 %collective-permute-start.1 = (s32[4]{0:T(128)S(1)}, s32[4]{0:T(128)S(1)}, u32[]{:S(2)}, u32[]{:S(2)}) collective-permute-start(s32[4]{0:T(128)S(1)} %bitcast.59), channel_id=1, source_target_pairs={{0,2},{1,3},{2,0},{3,1},{4,6},{5,7},{6,4},{7,5},{8,10},{9,11},{10,... | collective-permute-start | bytes 56 | tf_op jit(solution)/shard_map/ppermute | solution.py:72
  45.7 5.2 %collective-permute-start = (s32[4]{0:T(128)S(1)}, s32[4]{0:T(128)S(1)}, u32[]{:S(2)}, u32[]{:S(2)}) collective-permute-start(s32[4]{0:T(128)S(1)} %bitcast.60), channel_id=1, source_target_pairs={{0,1},{1,0},{2,3},{3,2},{4,5},{5,4},{6,7},{7,6},{8,9},{9,8},{10,11... | collective-permute-start | bytes 56 | tf_op jit(solution)/shard_map/ppermute | solution.py:72
  58.9 12.4 %all-to-all-start.1 = ((bf16[4,48,640]{2,1,0:T(8,128)(2,1)}), bf16[4,48,640]{2,1,0:T(8,128)(2,1)S(1)}, u32[]{:S(2)}, u32[]{:S(2)}) async-start(bf16[4,48,640]{2,1,0:T(8,128)(2,1)} %shard_map.82), calls=%async_computation.1 | async-start | bytes 491520 | tf_op jit(solution)/shard_map/all_to_all | solution.py:29
  72.9 31.0 %all-to-all-start.2 = ((bf16[8,88,640]{2,1,0:T(8,128)(2,1)}), bf16[8,88,640]{2,1,0:T(8,128)(2,1)S(1)}, u32[]{:S(2)}, u32[]{:S(2)}) async-start(bf16[8,88,640]{2,1,0:T(8,128)(2,1)} %shard_map.83), calls=%async_computation.2 | async-start | bytes 1802240 | tf_op jit(solution)/shard_map/all_to_all | solution.py:29
  82.3 67.3 %all-gather.3.cloned.1.call-start = ((), (), s32[]{:S(2)}) async-start(), calls=%async_computation.7 | async-start | bytes 1914880 | tf_op jit(solution)/shard_map/all_gather | solution.py:160
  89.5 13.3 %collective-permute-start.5 = (bf16[2,80,640]{2,1,0:T(8,128)(2,1)S(1)}, bf16[2,80,640]{2,1,0:T(8,128)(2,1)S(1)}, u32[]{:S(2)}, u32[]{:S(2)}) collective-permute-start(bf16[2,80,640]{2,1,0:T(8,128)(2,1)S(1)} %slice_bitcast_fusion), channel_id=1, source_target_pairs={{0,1},{1,0},{2,3},{3,2},{4,5},{5,4},{6,7},{7,6},{8,9},{9,8},{10,11... | collective-permute-start | bytes 614408 | tf_op jit(solution)/shard_map/ppermute | solution.py:72
  128.9 12.2 %all-to-all-start.4 = ((bf16[16,20,640]{2,1,0:T(8,128)(2,1)}), bf16[16,20,640]{2,1,0:T(8,128)(2,1)S(1)}, u32[]{:S(2)}, u32[]{:S(2)}) async-start(bf16[16,20,640]{2,1,0:T(8,128)(2,1)} %broadcast_in_dim.53), calls=%async_computation.5 | async-start | bytes 983040 | tf_op jit(solution)/shard_map/all_to_all | solution.py:29
  149.6 1.5 copy-start
Sparse Core Ops, SparseCore 0:
  57.7 30.7 reduce-scatter.1
  105.2 44.3 all-gather.2

commit v4 on v3

--- a/solution.py
+++ b/solution.py
@@ -11,7 +11,6 @@
 AXES = ("yj", "yh", "x", "zl", "c", "mp")
 DP = AXES[:5]
 ROW = ("yh", "x", "c")
-COLUMN = ("yj", "zl")
 F32 = jnp.float32
 BF16 = jnp.bfloat16
 
@@ -31,6 +30,15 @@
 
 def pool(x):
     return lax.all_gather(x, "c", axis=0, tiled=True)
+
+
+def shift(x, distance, axes="mp"):
+    return lax.ppermute(x, axes, [(i, i ^ distance) for i in range(lax.axis_size(axes))])
+
+
+def sum_over_x(parts):
+    parts = [parts[0]] + [shift(parts[d], d, "x") for d in (1, 2, 3)]
+    return sum(p.astype(F32) for p in parts).astype(BF16)
 
 
 def by_block(entries):
@@ -55,21 +63,26 @@
     return jnp.concatenate([u.reshape(16, 40, 640), v.reshape(16, 40, 640), small], axis=1)
 
 
-def products(xs, gs):
-    def body(x_ref, x_next_ref, g_ref, g_across_ref, out_ref):
-        pairs = [(x, g) for x in (x_ref, x_next_ref) for g in (g_ref, g_across_ref)]
-        for i, (x, g) in enumerate(pairs):
-            whole = lax.dot_general(
-                g[...], x[...], (((0,), (0,)), ((), ())), preferred_element_type=F32
-            ).astype(BF16)
-            for place in range(4):
-                out_ref[place, i] = whole[place * 80 : place * 80 + 80]
-
-    return on_scalars(body, (), (*xs, *gs), (4, 4, 80, 640))
-
-
-def shift(x, distance):
-    return lax.ppermute(x, "mp", [(i, i ^ distance) for i in range(4)])
+def products(x, g, g_across, place):
+    def body(place_ref, x_ref, g_ref, across_ref, *refs):
+        whole = refs[4]
+        for j, g_of_j in enumerate((g_ref, across_ref)):
+            whole[...] = lax.dot_general(
+                g_of_j[...], x_ref[...], (((0,), (0,)), ((), ())), preferred_element_type=F32
+            )
+            for d in range(4):
+                first = pl.multiple_of((place_ref[0] ^ d) * 80, 16)
+                refs[d][j] = whole[pl.ds(first, 80), :].astype(BF16)
+
+    return pl.pallas_call(
+        body,
+        in_specs=[pl.BlockSpec(memory_space=pltpu.SMEM)]
+        + [pl.BlockSpec(memory_space=pltpu.VMEM)] * 3,
+        out_specs=[pl.BlockSpec(memory_space=pltpu.VMEM)] * 4,
+        out_shape=[jax.ShapeDtypeStruct((2, 80, 640), BF16)] * 4,
+        scratch_shapes=[pltpu.VMEM((320, 640), F32)],
+        compiler_params=pltpu.CompilerParams(vmem_limit_bytes=16 << 20),
+    )(place, x, g, g_across)
 
 
 def first_phase(inputs, out_grads, owners, lengths, sent):
@@ -86,12 +99,10 @@
     row, rows, x, x_next, g, g_across = lax.optimization_barrier(
         (row, rows, x, x_next, g, g_across)
     )
-    return row, rows, products((x, pool(x_next)), (g, g_across))
-
-
-def row_of_gradient(summed):
-    back = shift(summed[2:], 1)
-    return jnp.stack(by_block([summed[0], back[0], back[1], summed[1]]))
+    place = lax.axis_index("x")[None]
+    away = products(pool(x_next), g, g_across, place)
+    here = products(x, g, g_across, place)
+    return row, rows, away, here
 
 
 def tile_of_gradient(four):
@@ -103,10 +114,6 @@
 
 def within_row(owner):
     return ((owner >> 4) & 1) * 8 + ((owner >> 2) & 3) * 2 + (owner & 1)
-
-
-def within_column(owner):
-    return (owner >> 5) * 2 + ((owner >> 1) & 1)
 
 
 def choose_v(row, rows, z):
@@ -123,20 +130,38 @@
     def body(mine_ref, row_ref, v_ref, out_ref):
         for j in range(4):
             source = within_row(mine_ref[j])
-            for half in range(2):
-                out_ref[2 * j + half, 0:40, :] = row_ref[source, 0:40, :]
-                out_ref[2 * j + half, 40:80, :] = v_ref[j, 0:40, :]
-                out_ref[2 * j + half, 80:82, :] = row_ref[source, 80:82, :]
-                out_ref[2 * j + half, 82:88, :] = v_ref[j, 42:48, :]
-
-    return on_scalars(body, (mine,), (row, v_part), (8, 88, 640))
+            out_ref[j, 0:40, :] = row_ref[source, 0:40, :]
+            out_ref[j, 40:80, :] = v_ref[j, 0:40, :]
+            out_ref[j, 80:82, :] = row_ref[source, 80:82, :]
+            out_ref[j, 82:88, :] = v_ref[j, 42:48, :]
+
+    return on_scalars(body, (mine,), (row, v_part), (4, 88, 640))
 
 
 def choose_one(column, mine, tile):
     def body(mine_ref, tile_ref, column_ref, out_ref):
-        out_ref[...] = column_ref[within_column(mine_ref[tile_ref[0]])]
+        out_ref[...] = column_ref[mine_ref[tile_ref[0]] >> 5]
 
     return on_scalars(body, (mine, tile), (column,), (88, 640))
+
+
+def choose_pair(parts, mine, tile, yh, zl):
+    def body(mine_ref, tile_ref, yh_ref, zl_ref, *refs):
+        out_ref = refs[4]
+        here, other = yh_ref[0], 1 - yh_ref[0]
+        same = ((mine_ref[tile_ref[0]] >> 1) & 1) == zl_ref[0]
+
+        @pl.when(same)
+        def _():
+            out_ref[here] = refs[0][...]
+            out_ref[other] = refs[2][...]
+
+        @pl.when(jnp.logical_not(same))
+        def _():
+            out_ref[here] = refs[1][...]
+            out_ref[other] = refs[3][...]
+
+    return on_scalars(body, (mine, tile, yh, zl), parts, (2, 88, 640))
 
 
 def on_scalars(body, scalars, arrays, shape):
@@ -150,26 +175,38 @@
     )(*scalars, *arrays)
 
 
-def bases_of_tile(row, rows, summed):
+def second_phase(row, rows, away, here):
     mine = rows[0]
     v_part = exchange(choose_v(row, rows, lax.axis_index("mp")[None]), "mp")
-    both = choose_both(row, v_part, mine)
-    column = exchange(both, COLUMN)
-    column, four = lax.optimization_barrier((column, row_of_gradient(summed)))
-    one = choose_one(column, mine, lax.axis_index("yj")[None])
-    return four, lax.all_gather(one[None], ROW, axis=0, tiled=True)
-
-
-def precondition(gt, bases, first):
-    def body(first_ref, gt_ref, bases_ref, out_ref, u_ref, v_ref):
-        for b in range(16):
-            u_ref[b * 40 : b * 40 + 40, :] = bases_ref[b, 0:40, :]
-            v_ref[b * 40 : b * 40 + 40, :] = bases_ref[b, 40:80, :]
-        small = bases_ref[0, 80:84, :].astype(F32)
+    v_part, away = lax.optimization_barrier((v_part, away))
+    column = exchange(choose_both(row, v_part, mine), "yj")
+    column, away = lax.optimization_barrier((column, sum_over_x(away)))
+    back = shift(away, 1)
+    here = sum_over_x(here)
+    four = jnp.stack(by_block([here[0], back[0], back[1], here[1]]))
+    tile, yh, zl = [lax.axis_index(a)[None] for a in ("yj", "yh", "zl")]
+    one = choose_one(column, mine, tile)
+    parts = [one] + [shift(one, d, ("yh", "zl")) for d in (1, 2, 3)]
+    four, parts = lax.optimization_barrier((four, parts))
+    pair = choose_pair(parts, mine, tile, yh, zl)
+    return four, jnp.stack([pair] + [shift(pair, d, "x") for d in (1, 2, 3)])
+
+
+def precondition(gt, near, far, place, core, first):
+    def body(place_ref, core_ref, first_ref, gt_ref, near_ref, far_ref, out_ref, u_ref, v_ref):
+        for e, ref in enumerate((near_ref, far_ref)):
+            for d in range(4):
+                for h in range(2):
+                    at = h * 8 + (place_ref[0] ^ d) * 2 + (core_ref[0] ^ e)
+                    rows = pl.ds(pl.multiple_of(at * 40, 8), 40)
+                    part = ref[d, h].astype(F32)
+                    u_ref[rows, :] = part[0:40]
+                    v_ref[rows, :] = part[40:80]
+        small = near_ref[0, 0, 80:84, :].astype(F32)
         ei = small[0:1] + small[1:2]
         eo = small[2:3] + small[3:4]
-        u = u_ref[...]
-        v = v_ref[...]
+        u = u_ref[...].astype(BF16)
+        v = v_ref[...].astype(BF16)
         at = lax.broadcasted_iota(jnp.int32, (24, 640), 1) - first_ref[0]
         own = (at == lax.broadcasted_iota(jnp.int32, (24, 640), 0)).astype(F32).astype(BF16)
         v_own = jnp.dot(own, v, preferred_element_type=F32).astype(BF16)
@@ -186,22 +223,23 @@
 
     return pl.pallas_call(
         body,
-        in_specs=[pl.BlockSpec(memory_space=pltpu.SMEM)]
-        + [pl.BlockSpec(memory_space=pltpu.VMEM)] * 2,
+        in_specs=[pl.BlockSpec(memory_space=pltpu.SMEM)] * 3
+        + [pl.BlockSpec(memory_space=pltpu.VMEM)] * 3,
         out_specs=pl.BlockSpec(memory_space=pltpu.VMEM),
         out_shape=jax.ShapeDtypeStruct((24, 640), BF16),
-        scratch_shapes=[pltpu.VMEM((640, 640), BF16), pltpu.VMEM((640, 640), BF16)],
+        scratch_shapes=[pltpu.VMEM((640, 640), F32)] * 2,
         compiler_params=pltpu.CompilerParams(vmem_limit_bytes=24 << 20),
-    )(first, gt, bases)
+    )(place, core, first, gt, near, far)
 
 
 def shards(inputs, out_grads, doc_lengths, owners, basis_in, basis_out, eig_in, eig_out):
     sent = rows_sent(basis_in, basis_out, eig_in[0], eig_out[0])
-    row, rows, parts = first_phase(inputs, out_grads, owners[0], doc_lengths[0], sent)
-    summed = lax.psum_scatter(parts, "x", scatter_dimension=0, tiled=True)[0]
-    four, bases = bases_of_tile(row, rows, summed)
+    first = first_phase(inputs, out_grads, owners[0], doc_lengths[0], sent)
+    four, near = second_phase(*first)
+    far = lax.ppermute(near, "c", [(0, 1), (1, 0)])
+    place, core = lax.axis_index("x")[None], lax.axis_index("c")[None]
     first = ((lax.axis_index(DP) % 32) * 20)[None]
-    return precondition(tile_of_gradient(four), bases, first)[:20].T
+    return precondition(tile_of_gradient(four), near, far, place, core, first)[:20].T
 
 
 def solution(mesh):

time: 162 us -> 153 us (0.944)
  starting transfers between devices: 53.3 us -> 103 us
  blocking collectives: 40.1 us -> 17.4 us
  waiting for transfers between devices: 34.9 us -> 12.3 us
  between operations: 13.7 us -> 0.51 us
    ppermute x6 -> x19, starting transfers between devices: 25.1 us -> 71.2 us  [the longest x18 63.1 us: shift(): lax.ppermute(x, axes, [(i, i ^ distance) for i in range(lax.axis_size(axe...]
    all_to_all x1 -> x0, blocking collectives: 22.8 us -> none  [exchange(): return lax.all_to_all(x, axes, split_axis=0, concat_axis=0, tiled=True)]
    all_to_all x4 -> x5, waiting for transfers between devices: 16.4 us -> 3 us  [exchange(): return lax.all_to_all(x, axes, split_axis=0, concat_axis=0, tiled=True)]
    reduce_scatter x1 -> x0, waiting for transfers between devices: 6.13 us -> none  [shards(): summed = lax.psum_scatter(parts, 'x', scatter_dimension=0, tiled=True)[0]]
    all_to_all x4 -> x5, starting transfers between devices: 28.1 us -> 32 us  [exchange(): return lax.all_to_all(x, axes, split_axis=0, concat_axis=0, tiled=True)]
    pallas_call x4, Pallas kernels: 6.45 us -> 3.74 us  [on_scalars(): pl.pallas_call(body, in_specs=[pl.BlockSpec(memory_space=pltpu.SMEM)] * l...]
    ppermute x6 -> x19, waiting for transfers between devices: 11.9 us -> 9.27 us  [the longest x18 9.27 us: shift(): lax.ppermute(x, axes, [(i, i ^ distance) for i in range(lax.axis_size(axe...]
    pallas_call x1 -> x3, Pallas kernels: 2.33 us -> 4.05 us  [the longest x1 2.51 us: precondition(): pl.pallas_call(body, in_specs=[pl.BlockSpec(memory_space=pltpu.SMEM)] * 3...]
  transfers between devices with their start and end apart: 12 -> 24, of which waited for: 7 -> 7; matrix products, arithmetic and copies ran while one was open for 3% -> 2% of each run, Pallas kernels for 2% -> 2%
where the time goes in v4:
time: 153 us; the launch traced here: 152 us
  starting transfers between devices  103 us (67%)
  blocking collectives  17.4 us (11%)
  waiting for transfers between devices  12.3 us (8%)
  Pallas kernels  7.79 us (5%)
  local copies, waits for them, and re-layouts  5.44 us (4%)
  other arithmetic  5.38 us (4%)
    ppermute x18, starting transfers between devices, shift(): lax.ppermute(x, axes, [(i, i ^ distance) for i in range(lax.axis_size(axe...  63.1 us
    all_to_all x5, starting transfers between devices, exchange(): return lax.all_to_all(x, axes, split_axis=0, concat_axis=0, tiled=True)  32 us
    all_gather x4, blocking collectives, pool(): return lax.all_gather(x, 'c', axis=0, tiled=True)  17.4 us
    ppermute x18, waiting for transfers between devices, shift(): lax.ppermute(x, axes, [(i, i ^ distance) for i in range(lax.axis_size(axe...  9.27 us
    ppermute x1, starting transfers between devices, shards(): far = lax.ppermute(near, 'c', [(0, 1), (1, 0)])  8.14 us
    pallas_call x4, Pallas kernels, on_scalars(): pl.pallas_call(body, in_specs=[pl.BlockSpec(memory_space=pltpu.SMEM)] * l...  3.74 us
  transfers between devices with their start and end apart: 24, of which 7 were waited for; matrix products, arithmetic and copies ran while one was open for 2% of the time, Pallas kernels for 2%

profile of v4, /device:TPU:1, one launch (start us, length us, event | category | flops | bytes accessed | tf_op | source)
XLA Modules:
  0.0 152.0 jit_solution(13181011764599366784)
XLA Ops:
  0.8 2.8 %pad_maximum_fusion = bf16[16,88,640]{2,1,0:T(8,128)(2,1)} fusion(bf16[16,8,640]{2,1,0:T(8,128)(2,1)S(1)} %broadcast_in_dim.60, bf16[16,40,640]{2,1,0:T(8,128)(2,1)} %bitcast.31, bf16[16,40,640]{2,1,0:T(8,128)(2,1)} %bitcast.32), kind=kLoop, calls=%fused_computation | loop fusion | flops 5406720 | bytes 3604480 | tf_op jit(solution)/shard_map/concatenate | solution.py:63
  3.6 10.5 %all-to-all-start = ((bf16[16,88,640]{2,1,0:T(8,128)(2,1)}), bf16[16,88,640]{2,1,0:T(8,128)(2,1)S(1)}, u32[]{:S(2)}, u32[]{:S(2)}) async-start(bf16[16,88,640]{2,1,0:T(8,128)(2,1)} %pad_maximum_fusion), calls=%async_computation | async-start | bytes 3604480 | tf_op jit(solution)/shard_map/all_to_all | solution.py:28
  20.1 7.0 %collective-permute-start.4 = (bf16[512,320]{1,0:T(8,128)(2,1)S(1)}, bf16[512,320]{1,0:T(8,128)(2,1)S(1)}, u32[]{:S(2)}, u32[]{:S(2)}) collective-permute-start(bf16[512,320]{1,0:T(8,128)(2,1)S(1)} %slice_select_fusion.g_ref), channel_id=1, source_target_pairs={{0,3},{1,2},{2,1},{3,0},{4,7},{5,6},{6,5},{7,4},{8,11},{9,10},{10,... | collective-permute-start | bytes 983048 | tf_op jit(solution)/shard_map/ppermute | solution.py:36
  27.1 2.8 %all_gather.12.x_ref = bf16[512,640]{1,0:T(8,128)(2,1)S(1)} all-gather(bf16[256,640]{1,0:T(8,128)(2,1)} %multiply_convert_fusion), channel_id=1, replica_groups=mesh['yj'=4,'yh'=2,'x'=4,'zl'=2,'c'=2,'mp'=4] {'c'}, dimensions={0}, use_global_device_ids=true | all-gather | bytes 983040 | tf_op jit(solution)/shard_map/all_gather | solution.py:32
  31.8 7.3 %collective-permute-start.1 = (s32[4]{0:T(128)S(1)}, s32[4]{0:T(128)S(1)}, u32[]{:S(2)}, u32[]{:S(2)}) collective-permute-start(s32[4]{0:T(128)S(1)} %bitcast.39), channel_id=1, source_target_pairs={{0,2},{1,3},{2,0},{3,1},{4,6},{5,7},{6,4},{7,5},{8,10},{9,11},{10,... | collective-permute-start | bytes 56 | tf_op jit(solution)/shard_map/ppermute | solution.py:36
  45.6 5.0 %all-to-all-start.1 = ((bf16[4,48,640]{2,1,0:T(8,128)(2,1)}), bf16[4,48,640]{2,1,0:T(8,128)(2,1)S(1)}, u32[]{:S(2)}, u32[]{:S(2)}) async-start(bf16[4,48,640]{2,1,0:T(8,128)(2,1)} %shard_map.83), calls=%async_computation.1 | async-start | bytes 491520 | tf_op jit(solution)/shard_map/all_to_all | solution.py:28
  50.6 3.6 %all_gather.14.x_ref = bf16[512,640]{1,0:T(8,128)(2,1)S(1)} all-gather(bf16[256,640]{1,0:T(8,128)(2,1)} %collective-permute-done.3), channel_id=1, replica_groups=mesh['yj'=4,'yh'=2,'x'=4,'zl'=2,'c'=2,'mp'=4] {'c'}, dimensions={0}, use_global_device_ids=true | all-gather | bytes 983040 | tf_op jit(solution)/shard_map/all_gather | solution.py:32
  60.1 6.0 %all-to-all-start.2 = ((bf16[4,88,640]{2,1,0:T(8,128)(2,1)}), bf16[4,88,640]{2,1,0:T(8,128)(2,1)S(1)}, u32[]{:S(2)}, u32[]{:S(2)}) async-start(bf16[4,88,640]{2,1,0:T(8,128)(2,1)} %shard_map.85), calls=%async_computation.2 | async-start | bytes 901120 | tf_op jit(solution)/shard_map/all_to_all | solution.py:28
  66.1 4.7 %collective-permute-start.10 = (bf16[2,80,640]{2,1,0:T(8,128)(2,1)}, bf16[2,80,640]{2,1,0:T(8,128)(2,1)S(1)}, u32[]{:S(2)}, u32[]{:S(2)}) collective-permute-start(bf16[2,80,640]{2,1,0:T(8,128)(2,1)} %copy-done.4), channel_id=1, source_target_pairs={{0,48},{16,32},{32,16},{48,0},{1,49},{17,33},{33,17},{49,1},{2,50}... | collective-permute-start | bytes 614408 | tf_op jit(solution)/shard_map/ppermute | solution.py:36
  70.8 2.5 %collective-permute-start.9 = (bf16[2,80,640]{2,1,0:T(8,128)(2,1)}, bf16[2,80,640]{2,1,0:T(8,128)(2,1)S(1)}, u32[]{:S(2)}, u32[]{:S(2)}) collective-permute-start(bf16[2,80,640]{2,1,0:T(8,128)(2,1)} %copy-done.3), channel_id=1, source_target_pairs={{0,32},{16,48},{32,0},{48,16},{1,33},{17,49},{33,1},{49,17},{2,34}... | collective-permute-start | bytes 614408 | tf_op jit(solution)/shard_map/ppermute | solution.py:36
  76.1 4.6 %collective-permute-start.7 = (bf16[2,80,640]{2,1,0:T(8,128)(2,1)S(1)}, bf16[2,80,640]{2,1,0:T(8,128)(2,1)S(1)}, u32[]{:S(2)}, u32[]{:S(2)}) collective-permute-start(bf16[2,80,640]{2,1,0:T(8,128)(2,1)S(1)} %get-tuple-element.43), channel_id=1, source_target_pairs={{0,48},{16,32},{32,16},{48,0},{1,49},{17,33},{33,17},{49,1},{2,50}... | collective-permute-start | bytes 614408 | tf_op jit(solution)/shard_map/ppermute | solution.py:36
  80.6 2.5 %collective-permute-start.6 = (bf16[2,80,640]{2,1,0:T(8,128)(2,1)S(1)}, bf16[2,80,640]{2,1,0:T(8,128)(2,1)S(1)}, u32[]{:S(2)}, u32[]{:S(2)}) collective-permute-start(bf16[2,80,640]{2,1,0:T(8,128)(2,1)S(1)} %get-tuple-element.42), channel_id=1, source_target_pairs={{0,32},{16,48},{32,0},{48,16},{1,33},{17,49},{33,1},{49,17},{2,34}... | collective-permute-start | bytes 614408 | tf_op jit(solution)/shard_map/ppermute | solution.py:36
  85.2 3.7 %collective-permute-start.11 = (bf16[2,80,640]{2,1,0:T(8,128)(2,1)S(1)}, bf16[2,80,640]{2,1,0:T(8,128)(2,1)S(1)}, u32[]{:S(2)}, u32[]{:S(2)}) collective-permute-start(bf16[2,80,640]{2,1,0:T(8,128)(2,1)S(1)} %add_convert_fusion), channel_id=1, source_target_pairs={{0,1},{1,0},{2,3},{3,2},{4,5},{5,4},{6,7},{7,6},{8,9},{9,8},{10,11... | collective-permute-start | bytes 614408 | tf_op jit(solution)/shard_map/ppermute | solution.py:36
  91.3 6.6 %collective-permute-start.12 = (bf16[88,640]{1,0:T(8,128)(2,1)S(1)}, bf16[88,640]{1,0:T(8,128)(2,1)S(1)}, u32[]{:S(2)}, u32[]{:S(2)}) collective-permute-start(bf16[88,640]{1,0:T(8,128)(2,1)S(1)} %shard_map.86.refs_0_), channel_id=1, source_target_pairs={{0,8},{8,0},{64,72},{72,64},{1,9},{9,1},{65,73},{73,65},{2,10},{10... | collective-permute-start | bytes 337928 | tf_op jit(solution)/shard_map/ppermute | solution.py:36
  97.9 2.6 %collective-permute-start.13 = (bf16[88,640]{1,0:T(8,128)(2,1)S(1)}, bf16[88,640]{1,0:T(8,128)(2,1)S(1)}, u32[]{:S(2)}, u32[]{:S(2)}) collective-permute-start(bf16[88,640]{1,0:T(8,128)(2,1)S(1)} %shard_map.86.refs_0_), channel_id=1, source_target_pairs={{0,64},{8,72},{64,0},{72,8},{1,65},{9,73},{65,1},{73,9},{2,66},{10... | collective-permute-start | bytes 337928 | tf_op jit(solution)/shard_map/ppermute | solution.py:36
  103.4 4.3 %collective-permute-done.14.refs_3_ = bf16[88,640]{1,0:T(8,128)(2,1)S(1)} collective-permute-done((bf16[88,640]{1,0:T(8,128)(2,1)S(1)}, bf16[88,640]{1,0:T(8,128)(2,1)S(1)}, u32[]{:S(2)}, u32[]{:S(2)}) %collective-permute-start.14) | collective-permute-done | bytes 112672 | tf_op jit(solution)/shard_map/ppermute | solution.py:36
  108.6 6.8 %all-to-all-start.3 = ((bf16[16,20,640]{2,1,0:T(8,128)(2,1)}), bf16[16,20,640]{2,1,0:T(8,128)(2,1)S(1)}, u32[]{:S(2)}, u32[]{:S(2)}) async-start(bf16[16,20,640]{2,1,0:T(8,128)(2,1)} %reshape.37), calls=%async_computation.3 | async-start | bytes 983040 | tf_op jit(solution)/shard_map/all_to_all | solution.py:28
  116.0 2.5 %collective-permute-start.17 = (bf16[2,88,640]{2,1,0:T(8,128)(2,1)S(1)}, bf16[2,88,640]{2,1,0:T(8,128)(2,1)S(1)}, u32[]{:S(2)}, u32[]{:S(2)}) collective-permute-start(bf16[2,88,640]{2,1,0:T(8,128)(2,1)S(1)} %shard_map.87), channel_id=1, source_target_pairs={{0,48},{16,32},{32,16},{48,0},{1,49},{17,33},{33,17},{49,1},{2,50}... | collective-permute-start | bytes 675848 | tf_op jit(solution)/shard_map/ppermute | solution.py:36
  118.5 3.2 %collective-permute-start.16 = (bf16[2,88,640]{2,1,0:T(8,128)(2,1)S(1)}, bf16[2,88,640]{2,1,0:T(8,128)(2,1)S(1)}, u32[]{:S(2)}, u32[]{:S(2)}) collective-permute-start(bf16[2,88,640]{2,1,0:T(8,128)(2,1)S(1)} %shard_map.87), channel_id=1, source_target_pairs={{0,32},{16,48},{32,0},{48,16},{1,33},{17,49},{33,1},{49,17},{2,34}... | collective-permute-start | bytes 675848 | tf_op jit(solution)/shard_map/ppermute | solution.py:36
  121.7 3.4 %collective-permute-start.15 = (bf16[2,88,640]{2,1,0:T(8,128)(2,1)S(1)}, bf16[2,88,640]{2,1,0:T(8,128)(2,1)S(1)}, u32[]{:S(2)}, u32[]{:S(2)}) collective-permute-start(bf16[2,88,640]{2,1,0:T(8,128)(2,1)S(1)} %shard_map.87), channel_id=1, source_target_pairs={{0,16},{16,0},{32,48},{48,32},{1,17},{17,1},{33,49},{49,33},{2,18}... | collective-permute-start | bytes 675848 | tf_op jit(solution)/shard_map/ppermute | solution.py:36
  128.1 3.6 %all-to-all-start.4 = ((bf16[16,20,640]{2,1,0:T(8,128)(2,1)}), bf16[16,20,640]{2,1,0:T(8,128)(2,1)S(1)}, u32[]{:S(2)}, u32[]{:S(2)}) async-start(bf16[16,20,640]{2,1,0:T(8,128)(2,1)} %broadcast_in_dim.66), calls=%async_computation.4 | async-start | bytes 983040 | tf_op jit(solution)/shard_map/all_to_all | solution.py:28
  131.8 8.1 %collective-permute-start.18 = (bf16[4,2,88,640]{3,2,1,0:T(8,128)(2,1)S(1)}, bf16[4,2,88,640]{3,2,1,0:T(8,128)(2,1)S(1)}, u32[]{:S(2)}, u32[]{:S(2)}) collective-permute-start(bf16[4,2,88,640]{3,2,1,0:T(8,128)(2,1)S(1)} %pad_maximum_fusion.1.near_ref), channel_id=1, source_target_pairs={{0,4},{4,0},{1,5},{5,1},{2,6},{6,2},{3,7},{7,3},{8,12},{12,8},{9,1... | collective-permute-start | bytes 2703368 | tf_op jit(solution)/shard_map/ppermute | solution.py:239
  140.1 8.7 %all_gather.15.gt_ref = bf16[640,640]{1,0:T(8,128)(2,1)S(1)} all-gather(bf16[320,640]{1,0:T(8,128)(2,1)S(1)} %reshape.38), channel_id=1, replica_groups=mesh['yj'=4,'yh'=2,'x'=4,'zl'=2,'c'=2,'mp'=4] {'c'}, dimensions={0}, use_global_device_ids=true | all-gather | bytes 1228800 | tf_op jit(solution)/shard_map/all_gather | solution.py:32
  148.8 2.5 %shard_map.88 = bf16[24,640]{1,0:T(8,128)(2,1)S(1)} custom-call(s32[1]{0:T(128)} %bitcast.place_ref, s32[1]{0:T(128)} %bitcast.1.core_ref, s32[1]{0:T(128)} %bitcast.2.first_ref, bf16[640,640]{1,0:T(8,128)(2,1)S(1)} %all_gather.15.gt_ref, bf16[4,2,88,640]{3,2,1,0:T(8,128)(2,1)S(1)} %pad_maximum_fusion.1.near_ref, ...), custom_call_target="tpu_custom_call" | custom-call | tf_op jit(solution)/shard_map/pallas_call | solution.py:224
  (79 shorter events, 36.2 us)
Async XLA Ops:
  3.6 40.7 %all-to-all-start = ((bf16[16,88,640]{2,1,0:T(8,128)(2,1)}), bf16[16,88,640]{2,1,0:T(8,128)(2,1)S(1)}, u32[]{:S(2)}, u32[]{:S(2)}) async-start(bf16[16,88,640]{2,1,0:T(8,128)(2,1)} %pad_maximum_fusion), calls=%async_computation | async-start | bytes 3604480 | tf_op jit(solution)/shard_map/all_to_all | solution.py:28
  15.3 29.0 %collective-permute-start.3 = (bf16[256,640]{1,0:T(8,128)(2,1)}, bf16[256,640]{1,0:T(8,128)(2,1)}, u32[]{:S(2)}, u32[]{:S(2)}) collective-permute-start(bf16[256,640]{1,0:T(8,128)(2,1)} %multiply_convert_fusion), channel_id=1, source_target_pairs={{0,1},{1,0},{2,3},{3,2},{4,5},{5,4},{6,7},{7,6},{8,9},{9,8},{10,11... | collective-permute-start | bytes 983048 | tf_op jit(solution)/shard_map/ppermute | solution.py:36
  20.1 24.2 %collective-permute-start.4 = (bf16[512,320]{1,0:T(8,128)(2,1)S(1)}, bf16[512,320]{1,0:T(8,128)(2,1)S(1)}, u32[]{:S(2)}, u32[]{:S(2)}) collective-permute-start(bf16[512,320]{1,0:T(8,128)(2,1)S(1)} %slice_select_fusion.g_ref), channel_id=1, source_target_pairs={{0,3},{1,2},{2,1},{3,0},{4,7},{5,6},{6,5},{7,4},{8,11},{9,10},{10,... | collective-permute-start | bytes 983048 | tf_op jit(solution)/shard_map/ppermute | solution.py:36
  29.9 13.7 %collective-permute-start.2 = (s32[4]{0:T(128)S(1)}, s32[4]{0:T(128)S(1)}, u32[]{:S(2)}, u32[]{:S(2)}) collective-permute-start(s32[4]{0:T(128)S(1)} %bitcast.38), channel_id=1, source_target_pairs={{0,3},{1,2},{2,1},{3,0},{4,7},{5,6},{6,5},{7,4},{8,11},{9,10},{10,... | collective-permute-start | bytes 56 | tf_op jit(solution)/shard_map/ppermute | solution.py:36
  31.8 11.8 %collective-permute-start.1 = (s32[4]{0:T(128)S(1)}, s32[4]{0:T(128)S(1)}, u32[]{:S(2)}, u32[]{:S(2)}) collective-permute-start(s32[4]{0:T(128)S(1)} %bitcast.39), channel_id=1, source_target_pairs={{0,2},{1,3},{2,0},{3,1},{4,6},{5,7},{6,4},{7,5},{8,10},{9,11},{10,... | collective-permute-start | bytes 56 | tf_op jit(solution)/shard_map/ppermute | solution.py:36
  39.1 5.2 %collective-permute-start = (s32[4]{0:T(128)S(1)}, s32[4]{0:T(128)S(1)}, u32[]{:S(2)}, u32[]{:S(2)}) collective-permute-start(s32[4]{0:T(128)S(1)} %bitcast.40), channel_id=1, source_target_pairs={{0,1},{1,0},{2,3},{3,2},{4,5},{5,4},{6,7},{7,6},{8,9},{9,8},{10,11... | collective-permute-start | bytes 56 | tf_op jit(solution)/shard_map/ppermute | solution.py:36
  45.6 13.1 %all-to-all-start.1 = ((bf16[4,48,640]{2,1,0:T(8,128)(2,1)}), bf16[4,48,640]{2,1,0:T(8,128)(2,1)S(1)}, u32[]{:S(2)}, u32[]{:S(2)}) async-start(bf16[4,48,640]{2,1,0:T(8,128)(2,1)} %shard_map.83), calls=%async_computation.1 | async-start | bytes 491520 | tf_op jit(solution)/shard_map/all_to_all | solution.py:28
  60.1 25.2 %all-to-all-start.2 = ((bf16[4,88,640]{2,1,0:T(8,128)(2,1)}), bf16[4,88,640]{2,1,0:T(8,128)(2,1)S(1)}, u32[]{:S(2)}, u32[]{:S(2)}) async-start(bf16[4,88,640]{2,1,0:T(8,128)(2,1)} %shard_map.85), calls=%async_computation.2 | async-start | bytes 901120 | tf_op jit(solution)/shard_map/all_to_all | solution.py:28
  66.1 17.0 %collective-permute-start.10 = (bf16[2,80,640]{2,1,0:T(8,128)(2,1)}, bf16[2,80,640]{2,1,0:T(8,128)(2,1)S(1)}, u32[]{:S(2)}, u32[]{:S(2)}) collective-permute-start(bf16[2,80,640]{2,1,0:T(8,128)(2,1)} %copy-done.4), channel_id=1, source_target_pairs={{0,48},{16,32},{32,16},{48,0},{1,49},{17,33},{33,17},{49,1},{2,50}... | collective-permute-start | bytes 614408 | tf_op jit(solution)/shard_map/ppermute | solution.py:36
  70.8 14.2 %collective-permute-start.9 = (bf16[2,80,640]{2,1,0:T(8,128)(2,1)}, bf16[2,80,640]{2,1,0:T(8,128)(2,1)S(1)}, u32[]{:S(2)}, u32[]{:S(2)}) collective-permute-start(bf16[2,80,640]{2,1,0:T(8,128)(2,1)} %copy-done.3), channel_id=1, source_target_pairs={{0,32},{16,48},{32,0},{48,16},{1,33},{17,49},{33,1},{49,17},{2,34}... | collective-permute-start | bytes 614408 | tf_op jit(solution)/shard_map/ppermute | solution.py:36
  73.3 11.8 %collective-permute-start.8 = (bf16[2,80,640]{2,1,0:T(8,128)(2,1)}, bf16[2,80,640]{2,1,0:T(8,128)(2,1)S(1)}, u32[]{:S(2)}, u32[]{:S(2)}) collective-permute-start(bf16[2,80,640]{2,1,0:T(8,128)(2,1)} %copy-done.2), channel_id=1, source_target_pairs={{0,16},{16,0},{32,48},{48,32},{1,17},{17,1},{33,49},{49,33},{2,18}... | collective-permute-start | bytes 614408 | tf_op jit(solution)/shard_map/ppermute | solution.py:36
  76.1 12.9 %collective-permute-start.7 = (bf16[2,80,640]{2,1,0:T(8,128)(2,1)S(1)}, bf16[2,80,640]{2,1,0:T(8,128)(2,1)S(1)}, u32[]{:S(2)}, u32[]{:S(2)}) collective-permute-start(bf16[2,80,640]{2,1,0:T(8,128)(2,1)S(1)} %get-tuple-element.43), channel_id=1, source_target_pairs={{0,48},{16,32},{32,16},{48,0},{1,49},{17,33},{33,17},{49,1},{2,50}... | collective-permute-start | bytes 614408 | tf_op jit(solution)/shard_map/ppermute | solution.py:36
  80.6 8.3 %collective-permute-start.6 = (bf16[2,80,640]{2,1,0:T(8,128)(2,1)S(1)}, bf16[2,80,640]{2,1,0:T(8,128)(2,1)S(1)}, u32[]{:S(2)}, u32[]{:S(2)}) collective-permute-start(bf16[2,80,640]{2,1,0:T(8,128)(2,1)S(1)} %get-tuple-element.42), channel_id=1, source_target_pairs={{0,32},{16,48},{32,0},{48,16},{1,33},{17,49},{33,1},{49,17},{2,34}... | collective-permute-start | bytes 614408 | tf_op jit(solution)/shard_map/ppermute | solution.py:36
  83.1 7.4 %collective-permute-start.5 = (bf16[2,80,640]{2,1,0:T(8,128)(2,1)S(1)}, bf16[2,80,640]{2,1,0:T(8,128)(2,1)S(1)}, u32[]{:S(2)}, u32[]{:S(2)}) collective-permute-start(bf16[2,80,640]{2,1,0:T(8,128)(2,1)S(1)} %get-tuple-element.41), channel_id=1, source_target_pairs={{0,16},{16,0},{32,48},{48,32},{1,17},{17,1},{33,49},{49,33},{2,18}... | collective-permute-start | bytes 614408 | tf_op jit(solution)/shard_map/ppermute | solution.py:36
  85.2 17.7 %collective-permute-start.11 = (bf16[2,80,640]{2,1,0:T(8,128)(2,1)S(1)}, bf16[2,80,640]{2,1,0:T(8,128)(2,1)S(1)}, u32[]{:S(2)}, u32[]{:S(2)}) collective-permute-start(bf16[2,80,640]{2,1,0:T(8,128)(2,1)S(1)} %add_convert_fusion), channel_id=1, source_target_pairs={{0,1},{1,0},{2,3},{3,2},{4,5},{5,4},{6,7},{7,6},{8,9},{9,8},{10,11... | collective-permute-start | bytes 614408 | tf_op jit(solution)/shard_map/ppermute | solution.py:36
  91.3 11.8 %collective-permute-start.12 = (bf16[88,640]{1,0:T(8,128)(2,1)S(1)}, bf16[88,640]{1,0:T(8,128)(2,1)S(1)}, u32[]{:S(2)}, u32[]{:S(2)}) collective-permute-start(bf16[88,640]{1,0:T(8,128)(2,1)S(1)} %shard_map.86.refs_0_), channel_id=1, source_target_pairs={{0,8},{8,0},{64,72},{72,64},{1,9},{9,1},{65,73},{73,65},{2,10},{10... | collective-permute-start | bytes 337928 | tf_op jit(solution)/shard_map/ppermute | solution.py:36
  97.9 5.5 %collective-permute-start.13 = (bf16[88,640]{1,0:T(8,128)(2,1)S(1)}, bf16[88,640]{1,0:T(8,128)(2,1)S(1)}, u32[]{:S(2)}, u32[]{:S(2)}) collective-permute-start(bf16[88,640]{1,0:T(8,128)(2,1)S(1)} %shard_map.86.refs_0_), channel_id=1, source_target_pairs={{0,64},{8,72},{64,0},{72,8},{1,65},{9,73},{65,1},{73,9},{2,66},{10... | collective-permute-start | bytes 337928 | tf_op jit(solution)/shard_map/ppermute | solution.py:36
  100.5 7.2 %collective-permute-start.14 = (bf16[88,640]{1,0:T(8,128)(2,1)S(1)}, bf16[88,640]{1,0:T(8,128)(2,1)S(1)}, u32[]{:S(2)}, u32[]{:S(2)}) collective-permute-start(bf16[88,640]{1,0:T(8,128)(2,1)S(1)} %shard_map.86.refs_0_), channel_id=1, source_target_pairs={{0,72},{8,64},{64,8},{72,0},{1,73},{9,65},{65,9},{73,1},{2,74},{10... | collective-permute-start | bytes 337928 | tf_op jit(solution)/shard_map/ppermute | solution.py:36
  108.6 18.6 %all-to-all-start.3 = ((bf16[16,20,640]{2,1,0:T(8,128)(2,1)}), bf16[16,20,640]{2,1,0:T(8,128)(2,1)S(1)}, u32[]{:S(2)}, u32[]{:S(2)}) async-start(bf16[16,20,640]{2,1,0:T(8,128)(2,1)} %reshape.37), calls=%async_computation.3 | async-start | bytes 983040 | tf_op jit(solution)/shard_map/all_to_all | solution.py:28
  116.0 15.6 %collective-permute-start.17 = (bf16[2,88,640]{2,1,0:T(8,128)(2,1)S(1)}, bf16[2,88,640]{2,1,0:T(8,128)(2,1)S(1)}, u32[]{:S(2)}, u32[]{:S(2)}) collective-permute-start(bf16[2,88,640]{2,1,0:T(8,128)(2,1)S(1)} %shard_map.87), channel_id=1, source_target_pairs={{0,48},{16,32},{32,16},{48,0},{1,49},{17,33},{33,17},{49,1},{2,50}... | collective-permute-start | bytes 675848 | tf_op jit(solution)/shard_map/ppermute | solution.py:36
  118.5 13.2 %collective-permute-start.16 = (bf16[2,88,640]{2,1,0:T(8,128)(2,1)S(1)}, bf16[2,88,640]{2,1,0:T(8,128)(2,1)S(1)}, u32[]{:S(2)}, u32[]{:S(2)}) collective-permute-start(bf16[2,88,640]{2,1,0:T(8,128)(2,1)S(1)} %shard_map.87), channel_id=1, source_target_pairs={{0,32},{16,48},{32,0},{48,16},{1,33},{17,49},{33,1},{49,17},{2,34}... | collective-permute-start | bytes 675848 | tf_op jit(solution)/shard_map/ppermute | solution.py:36
  121.7 10.0 %collective-permute-start.15 = (bf16[2,88,640]{2,1,0:T(8,128)(2,1)S(1)}, bf16[2,88,640]{2,1,0:T(8,128)(2,1)S(1)}, u32[]{:S(2)}, u32[]{:S(2)}) collective-permute-start(bf16[2,88,640]{2,1,0:T(8,128)(2,1)S(1)} %shard_map.87), channel_id=1, source_target_pairs={{0,16},{16,0},{32,48},{48,32},{1,17},{17,1},{33,49},{49,33},{2,18}... | collective-permute-start | bytes 675848 | tf_op jit(solution)/shard_map/ppermute | solution.py:36
  128.1 11.9 %all-to-all-start.4 = ((bf16[16,20,640]{2,1,0:T(8,128)(2,1)}), bf16[16,20,640]{2,1,0:T(8,128)(2,1)S(1)}, u32[]{:S(2)}, u32[]{:S(2)}) async-start(bf16[16,20,640]{2,1,0:T(8,128)(2,1)} %broadcast_in_dim.66), calls=%async_computation.4 | async-start | bytes 983040 | tf_op jit(solution)/shard_map/all_to_all | solution.py:28
  131.8 17.0 %collective-permute-start.18 = (bf16[4,2,88,640]{3,2,1,0:T(8,128)(2,1)S(1)}, bf16[4,2,88,640]{3,2,1,0:T(8,128)(2,1)S(1)}, u32[]{:S(2)}, u32[]{:S(2)}) collective-permute-start(bf16[4,2,88,640]{3,2,1,0:T(8,128)(2,1)S(1)} %pad_maximum_fusion.1.near_ref), channel_id=1, source_target_pairs={{0,4},{4,0},{1,5},{5,1},{2,6},{6,2},{3,7},{7,3},{8,12},{12,8},{9,1... | collective-permute-start | bytes 2703368 | tf_op jit(solution)/shard_map/ppermute | solution.py:239
  (9 other events, 78.6 us)

commit v5 on v4

--- a/solution.py
+++ b/solution.py
@@ -130,38 +130,37 @@
     def body(mine_ref, row_ref, v_ref, out_ref):
         for j in range(4):
             source = within_row(mine_ref[j])
-            out_ref[j, 0:40, :] = row_ref[source, 0:40, :]
-            out_ref[j, 40:80, :] = v_ref[j, 0:40, :]
-            out_ref[j, 80:82, :] = row_ref[source, 80:82, :]
-            out_ref[j, 82:88, :] = v_ref[j, 42:48, :]
-
-    return on_scalars(body, (mine,), (row, v_part), (4, 88, 640))
-
-
-def choose_one(column, mine, tile):
+            for half in range(2):
+                out_ref[2 * j + half, 0:40, :] = row_ref[source, 0:40, :]
+                out_ref[2 * j + half, 40:80, :] = v_ref[j, 0:40, :]
+                out_ref[2 * j + half, 80:82, :] = row_ref[source, 80:82, :]
+                out_ref[2 * j + half, 82:88, :] = v_ref[j, 42:48, :]
+
+    return on_scalars(body, (mine,), (row, v_part), (8, 88, 640))
+
+
+def choose_pair(column, mine, tile):
     def body(mine_ref, tile_ref, column_ref, out_ref):
-        out_ref[...] = column_ref[mine_ref[tile_ref[0]] >> 5]
-
-    return on_scalars(body, (mine, tile), (column,), (88, 640))
-
-
-def choose_pair(parts, mine, tile, yh, zl):
-    def body(mine_ref, tile_ref, yh_ref, zl_ref, *refs):
-        out_ref = refs[4]
-        here, other = yh_ref[0], 1 - yh_ref[0]
+        source = mine_ref[tile_ref[0]] >> 5
+        for half in range(2):
+            out_ref[half] = column_ref[2 * source + half]
+
+    return on_scalars(body, (mine, tile), (column,), (2, 88, 640))
+
+
+def choose_near(pair, other, mine, tile, zl):
+    def body(mine_ref, tile_ref, zl_ref, pair_ref, other_ref, out_ref):
         same = ((mine_ref[tile_ref[0]] >> 1) & 1) == zl_ref[0]
 
         @pl.when(same)
         def _():
-            out_ref[here] = refs[0][...]
-            out_ref[other] = refs[2][...]
+            out_ref[...] = pair_ref[...]
 
         @pl.when(jnp.logical_not(same))
         def _():
-            out_ref[here] = refs[1][...]
-            out_ref[other] = refs[3][...]
-
-    return on_scalars(body, (mine, tile, yh, zl), parts, (2, 88, 640))
+            out_ref[...] = other_ref[...]
+
+    return on_scalars(body, (mine, tile, zl), (pair, other), (2, 88, 640))
 
 
 def on_scalars(body, scalars, arrays, shape):
@@ -178,17 +177,18 @@
 def second_phase(row, rows, away, here):
     mine = rows[0]
     v_part = exchange(choose_v(row, rows, lax.axis_index("mp")[None]), "mp")
-    v_part, away = lax.optimization_barrier((v_part, away))
-    column = exchange(choose_both(row, v_part, mine), "yj")
+    away = list(away)
+    v_part, away[0] = lax.optimization_barrier((v_part, away[0]))
+    column = exchange(choose_both(row, v_part, mine), ("yj", "yh"))
     column, away = lax.optimization_barrier((column, sum_over_x(away)))
     back = shift(away, 1)
     here = sum_over_x(here)
     four = jnp.stack(by_block([here[0], back[0], back[1], here[1]]))
-    tile, yh, zl = [lax.axis_index(a)[None] for a in ("yj", "yh", "zl")]
-    one = choose_one(column, mine, tile)
-    parts = [one] + [shift(one, d, ("yh", "zl")) for d in (1, 2, 3)]
-    four, parts = lax.optimization_barrier((four, parts))
-    pair = choose_pair(parts, mine, tile, yh, zl)
+    tile, zl = [lax.axis_index(a)[None] for a in ("yj", "zl")]
+    pair = choose_pair(column, mine, tile)
+    other = shift(pair, 1, "zl")
+    four, other = lax.optimization_barrier((four, other))
+    pair = choose_near(pair, other, mine, tile, zl)
     return four, jnp.stack([pair] + [shift(pair, d, "x") for d in (1, 2, 3)])
 
 

time: 153 us -> 150 us (0.980)
  starting transfers between devices: 103 us -> 96.5 us
  waiting for transfers between devices: 12.3 us -> 14.1 us
    ppermute x18 -> x16, starting transfers between devices: 63.1 us -> 59.1 us  [shift(): lax.ppermute(x, axes, [(i, i ^ distance) for i in range(lax.axis_size(axe...]
    ppermute x18 -> x16, waiting for transfers between devices: 9.27 us -> 11.1 us  [shift(): lax.ppermute(x, axes, [(i, i ^ distance) for i in range(lax.axis_size(axe...]
    unnamed x18 -> x26, local copies, waits for them, and re-layouts: 2.76 us -> 3.47 us
  transfers between devices with their start and end apart: 24 -> 22, of which waited for: 7 -> 9; matrix products, arithmetic and copies ran while one was open for 2% -> 3% of each run, Pallas kernels for 2% -> 2%
where the time goes in v5:
time: 150 us; the launch traced here: 149 us
  starting transfers between devices  96.5 us (64%)
  blocking collectives  17.4 us (12%)
  waiting for transfers between devices  14.1 us (9%)
  Pallas kernels  8.09 us (5%)
  other arithmetic  6.53 us (4%)
  local copies, waits for them, and re-layouts  6.2 us (4%)
    ppermute x16, starting transfers between devices, shift(): lax.ppermute(x, axes, [(i, i ^ distance) for i in range(lax.axis_size(axe...  59.1 us
    all_to_all x5, starting transfers between devices, exchange(): return lax.all_to_all(x, axes, split_axis=0, concat_axis=0, tiled=True)  30.5 us
    all_gather x4, blocking collectives, pool(): return lax.all_gather(x, 'c', axis=0, tiled=True)  17.4 us
    ppermute x16, waiting for transfers between devices, shift(): lax.ppermute(x, axes, [(i, i ^ distance) for i in range(lax.axis_size(axe...  11.1 us
    ppermute x1, starting transfers between devices, shards(): far = lax.ppermute(near, 'c', [(0, 1), (1, 0)])  6.95 us
    unnamed x26, local copies, waits for them, and re-layouts  3.47 us
    pallas_call x4, Pallas kernels, on_scalars(): pl.pallas_call(body, in_specs=[pl.BlockSpec(memory_space=pltpu.SMEM)] * l...  3.26 us
    all_to_all x5, waiting for transfers between devices, exchange(): return lax.all_to_all(x, axes, split_axis=0, concat_axis=0, tiled=True)  3.01 us
  transfers between devices with their start and end apart: 22, of which 9 were waited for; matrix products, arithmetic and copies ran while one was open for 3% of the time, Pallas kernels for 2%

profile of v5, /device:TPU:1, one launch (start us, length us, event | category | flops | bytes accessed | tf_op | source)
XLA Modules:
  0.0 149.4 jit_solution(17539980621126102364)
XLA Ops:
  0.8 2.8 %pad_maximum_fusion = bf16[16,88,640]{2,1,0:T(8,128)(2,1)} fusion(bf16[16,8,640]{2,1,0:T(8,128)(2,1)S(1)} %broadcast_in_dim.57, bf16[16,40,640]{2,1,0:T(8,128)(2,1)} %bitcast.30, bf16[16,40,640]{2,1,0:T(8,128)(2,1)} %bitcast.31), kind=kLoop, calls=%fused_computation | loop fusion | flops 5406720 | bytes 3604480 | tf_op jit(solution)/shard_map/concatenate | solution.py:63
  3.6 10.5 %all-to-all-start = ((bf16[16,88,640]{2,1,0:T(8,128)(2,1)}), bf16[16,88,640]{2,1,0:T(8,128)(2,1)S(1)}, u32[]{:S(2)}, u32[]{:S(2)}) async-start(bf16[16,88,640]{2,1,0:T(8,128)(2,1)} %pad_maximum_fusion), calls=%async_computation | async-start | bytes 3604480 | tf_op jit(solution)/shard_map/all_to_all | solution.py:28
  14.2 2.4 %all_gather.13 = bf16[512,640]{1,0:T(8,128)(2,1)S(1)} all-gather(bf16[256,640]{1,0:T(8,128)(2,1)S(1)} %copy-done.10), channel_id=1, replica_groups=mesh['yj'=4,'yh'=2,'x'=4,'zl'=2,'c'=2,'mp'=4] {'c'}, dimensions={0}, use_global_device_ids=true | all-gather | bytes 983040 | tf_op jit(solution)/shard_map/all_gather | solution.py:32
  16.7 7.1 %collective-permute-start.4 = (bf16[512,320]{1,0:T(8,128)(2,1)S(1)}, bf16[512,320]{1,0:T(8,128)(2,1)S(1)}, u32[]{:S(2)}, u32[]{:S(2)}) collective-permute-start(bf16[512,320]{1,0:T(8,128)(2,1)S(1)} %slice_select_fusion.g_ref), channel_id=1, source_target_pairs={{0,3},{1,2},{2,1},{3,0},{4,7},{5,6},{6,5},{7,4},{8,11},{9,10},{10,... | collective-permute-start | bytes 983048 | tf_op jit(solution)/shard_map/ppermute | solution.py:36
  27.2 2.8 %all_gather.12.x_ref = bf16[512,640]{1,0:T(8,128)(2,1)S(1)} all-gather(bf16[256,640]{1,0:T(8,128)(2,1)} %multiply_convert_fusion), channel_id=1, replica_groups=mesh['yj'=4,'yh'=2,'x'=4,'zl'=2,'c'=2,'mp'=4] {'c'}, dimensions={0}, use_global_device_ids=true | all-gather | bytes 983040 | tf_op jit(solution)/shard_map/all_gather | solution.py:32
  30.1 4.0 %collective-permute-start = (s32[4]{0:T(128)S(1)}, s32[4]{0:T(128)S(1)}, u32[]{:S(2)}, u32[]{:S(2)}) collective-permute-start(s32[4]{0:T(128)S(1)} %bitcast.37), channel_id=1, source_target_pairs={{0,1},{1,0},{2,3},{3,2},{4,5},{5,4},{6,7},{7,6},{8,9},{9,8},{10,11... | collective-permute-start | bytes 56 | tf_op jit(solution)/shard_map/ppermute | solution.py:36
  36.0 5.5 %collective-permute-start.2 = (s32[4]{0:T(128)S(1)}, s32[4]{0:T(128)S(1)}, u32[]{:S(2)}, u32[]{:S(2)}) collective-permute-start(s32[4]{0:T(128)S(1)} %bitcast.39), channel_id=1, source_target_pairs={{0,3},{1,2},{2,1},{3,0},{4,7},{5,6},{6,5},{7,4},{8,11},{9,10},{10,... | collective-permute-start | bytes 56 | tf_op jit(solution)/shard_map/ppermute | solution.py:36
  42.4 2.6 %collective-permute-done.1 = s32[4]{0:T(128)S(1)} collective-permute-done((s32[4]{0:T(128)S(1)}, s32[4]{0:T(128)S(1)}, u32[]{:S(2)}, u32[]{:S(2)}) %collective-permute-start.1) | collective-permute-done | bytes 48 | tf_op jit(solution)/shard_map/ppermute | solution.py:36
  46.5 4.5 %all-to-all-start.1 = ((bf16[4,48,640]{2,1,0:T(8,128)(2,1)}), bf16[4,48,640]{2,1,0:T(8,128)(2,1)S(1)}, u32[]{:S(2)}, u32[]{:S(2)}) async-start(bf16[4,48,640]{2,1,0:T(8,128)(2,1)} %copy-done), calls=%async_computation.1 | async-start | bytes 491520 | tf_op jit(solution)/shard_map/all_to_all | solution.py:28
  51.0 4.0 %all_gather.14.x_ref = bf16[512,640]{1,0:T(8,128)(2,1)S(1)} all-gather(bf16[256,640]{1,0:T(8,128)(2,1)} %collective-permute-done.3), channel_id=1, replica_groups=mesh['yj'=4,'yh'=2,'x'=4,'zl'=2,'c'=2,'mp'=4] {'c'}, dimensions={0}, use_global_device_ids=true | all-gather | bytes 983040 | tf_op jit(solution)/shard_map/all_gather | solution.py:32
  60.6 6.1 %all-to-all-start.2 = ((bf16[8,88,640]{2,1,0:T(8,128)(2,1)}), bf16[8,88,640]{2,1,0:T(8,128)(2,1)S(1)}, u32[]{:S(2)}, u32[]{:S(2)}) async-start(bf16[8,88,640]{2,1,0:T(8,128)(2,1)} %shard_map.85), calls=%async_computation.2 | async-start | bytes 1802240 | tf_op jit(solution)/shard_map/all_to_all | solution.py:28
  66.6 4.3 %collective-permute-start.10 = (bf16[2,80,640]{2,1,0:T(8,128)(2,1)S(1)}, bf16[2,80,640]{2,1,0:T(8,128)(2,1)}, u32[]{:S(2)}, u32[]{:S(2)}) collective-permute-start(bf16[2,80,640]{2,1,0:T(8,128)(2,1)S(1)} %copy-done.8), channel_id=1, source_target_pairs={{0,48},{16,32},{32,16},{48,0},{1,49},{17,33},{33,17},{49,1},{2,50}... | collective-permute-start | bytes 614408 | tf_op jit(solution)/shard_map/ppermute | solution.py:36
  72.9 3.4 %collective-permute-start.9 = (bf16[2,80,640]{2,1,0:T(8,128)(2,1)S(1)}, bf16[2,80,640]{2,1,0:T(8,128)(2,1)}, u32[]{:S(2)}, u32[]{:S(2)}) collective-permute-start(bf16[2,80,640]{2,1,0:T(8,128)(2,1)S(1)} %copy-done.4), channel_id=1, source_target_pairs={{0,32},{16,48},{32,0},{48,16},{1,33},{17,49},{33,1},{49,17},{2,34}... | collective-permute-start | bytes 614408 | tf_op jit(solution)/shard_map/ppermute | solution.py:36
  79.8 5.5 %collective-permute-start.6 = (bf16[2,80,640]{2,1,0:T(8,128)(2,1)}, bf16[2,80,640]{2,1,0:T(8,128)(2,1)S(1)}, u32[]{:S(2)}, u32[]{:S(2)}) collective-permute-start(bf16[2,80,640]{2,1,0:T(8,128)(2,1)} %get-tuple-element.36), channel_id=1, source_target_pairs={{0,32},{16,48},{32,0},{48,16},{1,33},{17,49},{33,1},{49,17},{2,34}... | collective-permute-start | bytes 614408 | tf_op jit(solution)/shard_map/ppermute | solution.py:36
  89.2 4.9 %collective-permute-start.11 = (bf16[2,80,640]{2,1,0:T(8,128)(2,1)S(1)}, bf16[2,80,640]{2,1,0:T(8,128)(2,1)S(1)}, u32[]{:S(2)}, u32[]{:S(2)}) collective-permute-start(bf16[2,80,640]{2,1,0:T(8,128)(2,1)S(1)} %add_convert_fusion), channel_id=1, source_target_pairs={{0,1},{1,0},{2,3},{3,2},{4,5},{5,4},{6,7},{7,6},{8,9},{9,8},{10,11... | collective-permute-start | bytes 614408 | tf_op jit(solution)/shard_map/ppermute | solution.py:36
  96.1 4.8 %collective-permute-start.12 = (bf16[2,88,640]{2,1,0:T(8,128)(2,1)S(1)}, bf16[2,88,640]{2,1,0:T(8,128)(2,1)S(1)}, u32[]{:S(2)}, u32[]{:S(2)}) collective-permute-start(bf16[2,88,640]{2,1,0:T(8,128)(2,1)S(1)} %shard_map.86.pair_ref), channel_id=1, source_target_pairs={{0,8},{8,0},{1,9},{9,1},{2,10},{10,2},{3,11},{11,3},{4,12},{12,4},... | collective-permute-start | bytes 675848 | tf_op jit(solution)/shard_map/ppermute | solution.py:36
  101.1 6.1 %collective-permute-done.12.other_ref = bf16[2,88,640]{2,1,0:T(8,128)(2,1)S(1)} collective-permute-done((bf16[2,88,640]{2,1,0:T(8,128)(2,1)S(1)}, bf16[2,88,640]{2,1,0:T(8,128)(2,1)S(1)}, u32[]{:S(2)}, u32[]{:S(2)}) %collective-permute-start.12) | collective-permute-done | bytes 225312 | tf_op jit(solution)/shard_map/ppermute | solution.py:36
  108.1 5.1 %all-to-all-start.3 = ((bf16[16,20,640]{2,1,0:T(8,128)(2,1)}), bf16[16,20,640]{2,1,0:T(8,128)(2,1)S(1)}, u32[]{:S(2)}, u32[]{:S(2)}) async-start(bf16[16,20,640]{2,1,0:T(8,128)(2,1)} %reshape.37), calls=%async_computation.3 | async-start | bytes 983040 | tf_op jit(solution)/shard_map/all_to_all | solution.py:28
  115.8 3.8 %collective-permute-start.14 = (bf16[2,88,640]{2,1,0:T(8,128)(2,1)S(1)}, bf16[2,88,640]{2,1,0:T(8,128)(2,1)S(1)}, u32[]{:S(2)}, u32[]{:S(2)}) collective-permute-start(bf16[2,88,640]{2,1,0:T(8,128)(2,1)S(1)} %shard_map.87), channel_id=1, source_target_pairs={{0,32},{16,48},{32,0},{48,16},{1,33},{17,49},{33,1},{49,17},{2,34}... | collective-permute-start | bytes 675848 | tf_op jit(solution)/shard_map/ppermute | solution.py:36
  119.6 3.7 %collective-permute-start.15 = (bf16[2,88,640]{2,1,0:T(8,128)(2,1)S(1)}, bf16[2,88,640]{2,1,0:T(8,128)(2,1)S(1)}, u32[]{:S(2)}, u32[]{:S(2)}) collective-permute-start(bf16[2,88,640]{2,1,0:T(8,128)(2,1)S(1)} %shard_map.87), channel_id=1, source_target_pairs={{0,48},{16,32},{32,16},{48,0},{1,49},{17,33},{33,17},{49,1},{2,50}... | collective-permute-start | bytes 675848 | tf_op jit(solution)/shard_map/ppermute | solution.py:36
  125.8 4.3 %all-to-all-start.4 = ((bf16[16,20,640]{2,1,0:T(8,128)(2,1)}), bf16[16,20,640]{2,1,0:T(8,128)(2,1)S(1)}, u32[]{:S(2)}, u32[]{:S(2)}) async-start(bf16[16,20,640]{2,1,0:T(8,128)(2,1)} %broadcast_in_dim.63), calls=%async_computation.4 | async-start | bytes 983040 | tf_op jit(solution)/shard_map/all_to_all | solution.py:28
  130.4 7.0 %collective-permute-start.16 = (bf16[4,2,88,640]{3,2,1,0:T(8,128)(2,1)S(1)}, bf16[4,2,88,640]{3,2,1,0:T(8,128)(2,1)S(1)}, u32[]{:S(2)}, u32[]{:S(2)}) collective-permute-start(bf16[4,2,88,640]{3,2,1,0:T(8,128)(2,1)S(1)} %pad_maximum_fusion.1.near_ref), channel_id=1, source_target_pairs={{0,4},{4,0},{1,5},{5,1},{2,6},{6,2},{3,7},{7,3},{8,12},{12,8},{9,1... | collective-permute-start | bytes 2703368 | tf_op jit(solution)/shard_map/ppermute | solution.py:239
  138.0 8.3 %all_gather.15.gt_ref = bf16[640,640]{1,0:T(8,128)(2,1)S(1)} all-gather(bf16[320,640]{1,0:T(8,128)(2,1)S(1)} %reshape.38), channel_id=1, replica_groups=mesh['yj'=4,'yh'=2,'x'=4,'zl'=2,'c'=2,'mp'=4] {'c'}, dimensions={0}, use_global_device_ids=true | all-gather | bytes 1228800 | tf_op jit(solution)/shard_map/all_gather | solution.py:32
  146.2 2.5 %shard_map.88 = bf16[24,640]{1,0:T(8,128)(2,1)S(1)} custom-call(s32[1]{0:T(128)} %bitcast.place_ref, s32[1]{0:T(128)} %bitcast.1.core_ref, s32[1]{0:T(128)} %bitcast.2.first_ref, bf16[640,640]{1,0:T(8,128)(2,1)S(1)} %all_gather.15.gt_ref, bf16[4,2,88,640]{3,2,1,0:T(8,128)(2,1)S(1)} %pad_maximum_fusion.1.near_ref, ...), custom_call_target="tpu_custom_call" | custom-call | tf_op jit(solution)/shard_map/pallas_call | solution.py:224
  (83 shorter events, 33.0 us)
Async XLA Ops:
  3.6 41.5 %all-to-all-start = ((bf16[16,88,640]{2,1,0:T(8,128)(2,1)}), bf16[16,88,640]{2,1,0:T(8,128)(2,1)S(1)}, u32[]{:S(2)}, u32[]{:S(2)}) async-start(bf16[16,88,640]{2,1,0:T(8,128)(2,1)} %pad_maximum_fusion), calls=%async_computation | async-start | bytes 3604480 | tf_op jit(solution)/shard_map/all_to_all | solution.py:28
  14.1 15.9 %copy-start.12 = (s32[1,4]{1,0:T(1,128)S(1)}, s32[1,4]{1,0:T(1,128)}, u32[]{:S(2)}) copy-start(s32[1,4]{1,0:T(1,128)} %param.11) | copy-start | bytes 52
  16.7 28.3 %collective-permute-start.4 = (bf16[512,320]{1,0:T(8,128)(2,1)S(1)}, bf16[512,320]{1,0:T(8,128)(2,1)S(1)}, u32[]{:S(2)}, u32[]{:S(2)}) collective-permute-start(bf16[512,320]{1,0:T(8,128)(2,1)S(1)} %slice_select_fusion.g_ref), channel_id=1, source_target_pairs={{0,3},{1,2},{2,1},{3,0},{4,7},{5,6},{6,5},{7,4},{8,11},{9,10},{10,... | collective-permute-start | bytes 983048 | tf_op jit(solution)/shard_map/ppermute | solution.py:36
  25.1 20.0 %collective-permute-start.3 = (bf16[256,640]{1,0:T(8,128)(2,1)}, bf16[256,640]{1,0:T(8,128)(2,1)}, u32[]{:S(2)}, u32[]{:S(2)}) collective-permute-start(bf16[256,640]{1,0:T(8,128)(2,1)} %multiply_convert_fusion), channel_id=1, source_target_pairs={{0,1},{1,0},{2,3},{3,2},{4,5},{5,4},{6,7},{7,6},{8,9},{9,8},{10,11... | collective-permute-start | bytes 983048 | tf_op jit(solution)/shard_map/ppermute | solution.py:36
  30.1 12.4 %collective-permute-start = (s32[4]{0:T(128)S(1)}, s32[4]{0:T(128)S(1)}, u32[]{:S(2)}, u32[]{:S(2)}) collective-permute-start(s32[4]{0:T(128)S(1)} %bitcast.37), channel_id=1, source_target_pairs={{0,1},{1,0},{2,3},{3,2},{4,5},{5,4},{6,7},{7,6},{8,9},{9,8},{10,11... | collective-permute-start | bytes 56 | tf_op jit(solution)/shard_map/ppermute | solution.py:36
  34.1 11.0 %collective-permute-start.1 = (s32[4]{0:T(128)S(1)}, s32[4]{0:T(128)S(1)}, u32[]{:S(2)}, u32[]{:S(2)}) collective-permute-start(s32[4]{0:T(128)S(1)} %bitcast.38), channel_id=1, source_target_pairs={{0,2},{1,3},{2,0},{3,1},{4,6},{5,7},{6,4},{7,5},{8,10},{9,11},{10,... | collective-permute-start | bytes 56 | tf_op jit(solution)/shard_map/ppermute | solution.py:36
  36.0 9.0 %collective-permute-start.2 = (s32[4]{0:T(128)S(1)}, s32[4]{0:T(128)S(1)}, u32[]{:S(2)}, u32[]{:S(2)}) collective-permute-start(s32[4]{0:T(128)S(1)} %bitcast.39), channel_id=1, source_target_pairs={{0,3},{1,2},{2,1},{3,0},{4,7},{5,6},{6,5},{7,4},{8,11},{9,10},{10,... | collective-permute-start | bytes 56 | tf_op jit(solution)/shard_map/ppermute | solution.py:36
  46.5 12.5 %all-to-all-start.1 = ((bf16[4,48,640]{2,1,0:T(8,128)(2,1)}), bf16[4,48,640]{2,1,0:T(8,128)(2,1)S(1)}, u32[]{:S(2)}, u32[]{:S(2)}) async-start(bf16[4,48,640]{2,1,0:T(8,128)(2,1)} %copy-done), calls=%async_computation.1 | async-start | bytes 491520 | tf_op jit(solution)/shard_map/all_to_all | solution.py:28
  60.6 26.9 %copy-start.2 = (bf16[2,80,640]{2,1,0:T(8,128)(2,1)S(1)}, bf16[2,80,640]{2,1,0:T(8,128)(2,1)}, u32[]{:S(2)}) copy-start(bf16[2,80,640]{2,1,0:T(8,128)(2,1)} %copy-done.1) | copy-start | bytes 614404
  60.6 28.7 %all-to-all-start.2 = ((bf16[8,88,640]{2,1,0:T(8,128)(2,1)}), bf16[8,88,640]{2,1,0:T(8,128)(2,1)S(1)}, u32[]{:S(2)}, u32[]{:S(2)}) async-start(bf16[8,88,640]{2,1,0:T(8,128)(2,1)} %shard_map.85), calls=%async_computation.2 | async-start | bytes 1802240 | tf_op jit(solution)/shard_map/all_to_all | solution.py:28
  66.6 18.6 %collective-permute-start.10 = (bf16[2,80,640]{2,1,0:T(8,128)(2,1)S(1)}, bf16[2,80,640]{2,1,0:T(8,128)(2,1)}, u32[]{:S(2)}, u32[]{:S(2)}) collective-permute-start(bf16[2,80,640]{2,1,0:T(8,128)(2,1)S(1)} %copy-done.8), channel_id=1, source_target_pairs={{0,48},{16,32},{32,16},{48,0},{1,49},{17,33},{33,17},{49,1},{2,50}... | collective-permute-start | bytes 614408 | tf_op jit(solution)/shard_map/ppermute | solution.py:36
  70.9 16.5 %collective-permute-start.8 = (bf16[2,80,640]{2,1,0:T(8,128)(2,1)S(1)}, bf16[2,80,640]{2,1,0:T(8,128)(2,1)}, u32[]{:S(2)}, u32[]{:S(2)}) collective-permute-start(bf16[2,80,640]{2,1,0:T(8,128)(2,1)S(1)} %copy-done.6), channel_id=1, source_target_pairs={{0,16},{16,0},{32,48},{48,32},{1,17},{17,1},{33,49},{49,33},{2,18}... | collective-permute-start | bytes 614408 | tf_op jit(solution)/shard_map/ppermute | solution.py:36
  72.9 14.6 %collective-permute-start.9 = (bf16[2,80,640]{2,1,0:T(8,128)(2,1)S(1)}, bf16[2,80,640]{2,1,0:T(8,128)(2,1)}, u32[]{:S(2)}, u32[]{:S(2)}) collective-permute-start(bf16[2,80,640]{2,1,0:T(8,128)(2,1)S(1)} %copy-done.4), channel_id=1, source_target_pairs={{0,32},{16,48},{32,0},{48,16},{1,33},{17,49},{33,1},{49,17},{2,34}... | collective-permute-start | bytes 614408 | tf_op jit(solution)/shard_map/ppermute | solution.py:36
  77.9 16.3 %collective-permute-start.5 = (bf16[2,80,640]{2,1,0:T(8,128)(2,1)}, bf16[2,80,640]{2,1,0:T(8,128)(2,1)S(1)}, u32[]{:S(2)}, u32[]{:S(2)}) collective-permute-start(bf16[2,80,640]{2,1,0:T(8,128)(2,1)} %get-tuple-element.35), channel_id=1, source_target_pairs={{0,16},{16,0},{32,48},{48,32},{1,17},{17,1},{33,49},{49,33},{2,18}... | collective-permute-start | bytes 614408 | tf_op jit(solution)/shard_map/ppermute | solution.py:36
  79.8 14.4 %collective-permute-start.6 = (bf16[2,80,640]{2,1,0:T(8,128)(2,1)}, bf16[2,80,640]{2,1,0:T(8,128)(2,1)S(1)}, u32[]{:S(2)}, u32[]{:S(2)}) collective-permute-start(bf16[2,80,640]{2,1,0:T(8,128)(2,1)} %get-tuple-element.36), channel_id=1, source_target_pairs={{0,32},{16,48},{32,0},{48,16},{1,33},{17,49},{33,1},{49,17},{2,34}... | collective-permute-start | bytes 614408 | tf_op jit(solution)/shard_map/ppermute | solution.py:36
  85.3 10.1 %collective-permute-start.7 = (bf16[2,80,640]{2,1,0:T(8,128)(2,1)}, bf16[2,80,640]{2,1,0:T(8,128)(2,1)S(1)}, u32[]{:S(2)}, u32[]{:S(2)}) collective-permute-start(bf16[2,80,640]{2,1,0:T(8,128)(2,1)} %get-tuple-element.37), channel_id=1, source_target_pairs={{0,48},{16,32},{32,16},{48,0},{1,49},{17,33},{33,17},{49,1},{2,50}... | collective-permute-start | bytes 614408 | tf_op jit(solution)/shard_map/ppermute | solution.py:36
  89.2 11.7 %collective-permute-start.11 = (bf16[2,80,640]{2,1,0:T(8,128)(2,1)S(1)}, bf16[2,80,640]{2,1,0:T(8,128)(2,1)S(1)}, u32[]{:S(2)}, u32[]{:S(2)}) collective-permute-start(bf16[2,80,640]{2,1,0:T(8,128)(2,1)S(1)} %add_convert_fusion), channel_id=1, source_target_pairs={{0,1},{1,0},{2,3},{3,2},{4,5},{5,4},{6,7},{7,6},{8,9},{9,8},{10,11... | collective-permute-start | bytes 614408 | tf_op jit(solution)/shard_map/ppermute | solution.py:36
  96.1 11.1 %collective-permute-start.12 = (bf16[2,88,640]{2,1,0:T(8,128)(2,1)S(1)}, bf16[2,88,640]{2,1,0:T(8,128)(2,1)S(1)}, u32[]{:S(2)}, u32[]{:S(2)}) collective-permute-start(bf16[2,88,640]{2,1,0:T(8,128)(2,1)S(1)} %shard_map.86.pair_ref), channel_id=1, source_target_pairs={{0,8},{8,0},{1,9},{9,1},{2,10},{10,2},{3,11},{11,3},{4,12},{12,4},... | collective-permute-start | bytes 675848 | tf_op jit(solution)/shard_map/ppermute | solution.py:36
  108.1 16.8 %all-to-all-start.3 = ((bf16[16,20,640]{2,1,0:T(8,128)(2,1)}), bf16[16,20,640]{2,1,0:T(8,128)(2,1)S(1)}, u32[]{:S(2)}, u32[]{:S(2)}) async-start(bf16[16,20,640]{2,1,0:T(8,128)(2,1)} %reshape.37), calls=%async_computation.3 | async-start | bytes 983040 | tf_op jit(solution)/shard_map/all_to_all | solution.py:28
  113.7 16.4 %collective-permute-start.13 = (bf16[2,88,640]{2,1,0:T(8,128)(2,1)S(1)}, bf16[2,88,640]{2,1,0:T(8,128)(2,1)S(1)}, u32[]{:S(2)}, u32[]{:S(2)}) collective-permute-start(bf16[2,88,640]{2,1,0:T(8,128)(2,1)S(1)} %shard_map.87), channel_id=1, source_target_pairs={{0,16},{16,0},{32,48},{48,32},{1,17},{17,1},{33,49},{49,33},{2,18}... | collective-permute-start | bytes 675848 | tf_op jit(solution)/shard_map/ppermute | solution.py:36
  115.8 14.4 %collective-permute-start.14 = (bf16[2,88,640]{2,1,0:T(8,128)(2,1)S(1)}, bf16[2,88,640]{2,1,0:T(8,128)(2,1)S(1)}, u32[]{:S(2)}, u32[]{:S(2)}) collective-permute-start(bf16[2,88,640]{2,1,0:T(8,128)(2,1)S(1)} %shard_map.87), channel_id=1, source_target_pairs={{0,32},{16,48},{32,0},{48,16},{1,33},{17,49},{33,1},{49,17},{2,34}... | collective-permute-start | bytes 675848 | tf_op jit(solution)/shard_map/ppermute | solution.py:36
  119.6 10.6 %collective-permute-start.15 = (bf16[2,88,640]{2,1,0:T(8,128)(2,1)S(1)}, bf16[2,88,640]{2,1,0:T(8,128)(2,1)S(1)}, u32[]{:S(2)}, u32[]{:S(2)}) collective-permute-start(bf16[2,88,640]{2,1,0:T(8,128)(2,1)S(1)} %shard_map.87), channel_id=1, source_target_pairs={{0,48},{16,32},{32,16},{48,0},{1,49},{17,33},{33,17},{49,1},{2,50}... | collective-permute-start | bytes 675848 | tf_op jit(solution)/shard_map/ppermute | solution.py:36
  125.8 12.0 %all-to-all-start.4 = ((bf16[16,20,640]{2,1,0:T(8,128)(2,1)}), bf16[16,20,640]{2,1,0:T(8,128)(2,1)S(1)}, u32[]{:S(2)}, u32[]{:S(2)}) async-start(bf16[16,20,640]{2,1,0:T(8,128)(2,1)} %broadcast_in_dim.63), calls=%async_computation.4 | async-start | bytes 983040 | tf_op jit(solution)/shard_map/all_to_all | solution.py:28
  130.4 15.8 %collective-permute-start.16 = (bf16[4,2,88,640]{3,2,1,0:T(8,128)(2,1)S(1)}, bf16[4,2,88,640]{3,2,1,0:T(8,128)(2,1)S(1)}, u32[]{:S(2)}, u32[]{:S(2)}) collective-permute-start(bf16[4,2,88,640]{3,2,1,0:T(8,128)(2,1)S(1)} %pad_maximum_fusion.1.near_ref), channel_id=1, source_target_pairs={{0,4},{4,0},{1,5},{5,1},{2,6},{6,2},{3,7},{7,3},{8,12},{12,8},{9,1... | collective-permute-start | bytes 2703368 | tf_op jit(solution)/shard_map/ppermute | solution.py:239
  (11 other events, 62.6 us)

commit v6 on v5

--- a/solution.py
+++ b/solution.py
@@ -105,10 +105,21 @@
     return row, rows, away, here
 
 
+def sum_for_all(received):
+    def body(received_ref, out_ref):
+        total = jnp.zeros((20, 640), F32)
+        for i in range(16):
+            total += received_ref[i].astype(F32)
+        piece = total.astype(BF16)
+        for i in range(16):
+            out_ref[i] = piece
+
+    return on_scalars(body, (), (received,), (16, 20, 640))
+
+
 def tile_of_gradient(four):
     received = exchange(four.reshape(16, 20, 640), ("yj", "yh", "zl"))
-    piece = jnp.sum(received.astype(F32), axis=0).astype(BF16)
-    spread = exchange(jnp.broadcast_to(piece[None], (16, 20, 640)), ("x", "yh", "zl"))
+    spread = exchange(sum_for_all(received), ("x", "yh", "zl"))
     return pool(spread.reshape(320, 640))
 
 
@@ -219,14 +230,14 @@
             v_own, scaled, (((1,), (1,)), ((), ())), preferred_element_type=F32
         ).astype(BF16)
         out = lax.dot_general(back, u, (((1,), (1,)), ((), ())), preferred_element_type=F32)
-        out_ref[...] = out.astype(BF16)
+        out_ref[...] = out[0:20].astype(BF16)
 
     return pl.pallas_call(
         body,
         in_specs=[pl.BlockSpec(memory_space=pltpu.SMEM)] * 3
         + [pl.BlockSpec(memory_space=pltpu.VMEM)] * 3,
         out_specs=pl.BlockSpec(memory_space=pltpu.VMEM),
-        out_shape=jax.ShapeDtypeStruct((24, 640), BF16),
+        out_shape=jax.ShapeDtypeStruct((20, 640), BF16),
         scratch_shapes=[pltpu.VMEM((640, 640), F32)] * 2,
         compiler_params=pltpu.CompilerParams(vmem_limit_bytes=24 << 20),
     )(place, core, first, gt, near, far)
@@ -239,7 +250,7 @@
     far = lax.ppermute(near, "c", [(0, 1), (1, 0)])
     place, core = lax.axis_index("x")[None], lax.axis_index("c")[None]
     first = ((lax.axis_index(DP) % 32) * 20)[None]
-    return precondition(tile_of_gradient(four), near, far, place, core, first)[:20].T
+    return precondition(tile_of_gradient(four), near, far, place, core, first).T
 
 
 def solution(mesh):

time: 150 us -> 150 us (level)
  local copies, waits for them, and re-layouts: 6.2 us -> 4.61 us
  Pallas kernels: 8.09 us -> 9.64 us
    pallas_call x4 -> x5, Pallas kernels: 3.26 us -> 4.11 us  [on_scalars(): pl.pallas_call(body, in_specs=[pl.BlockSpec(memory_space=pltpu.SMEM)] * l...]
  transfers between devices with their start and end apart: 22 -> 22, of which waited for: 9 -> 9; matrix products, arithmetic and copies ran while one was open for 3% -> 2% of each run, Pallas kernels for 2% -> 3%
where the time goes in v6:
time: 150 us; the launch traced here: 149 us
  starting transfers between devices  96.6 us (64%)
  blocking collectives  17.5 us (12%)
  waiting for transfers between devices  14 us (9%)
  Pallas kernels  9.64 us (6%)
  other arithmetic  6.45 us (4%)
  local copies, waits for them, and re-layouts  4.61 us (3%)
    ppermute x16, starting transfers between devices, shift(): lax.ppermute(x, axes, [(i, i ^ distance) for i in range(lax.axis_size(axe...  59 us
    all_to_all x5, starting transfers between devices, exchange(): return lax.all_to_all(x, axes, split_axis=0, concat_axis=0, tiled=True)  30.6 us
    all_gather x4, blocking collectives, pool(): return lax.all_gather(x, 'c', axis=0, tiled=True)  17.5 us
    ppermute x16, waiting for transfers between devices, shift(): lax.ppermute(x, axes, [(i, i ^ distance) for i in range(lax.axis_size(axe...  11 us
    ppermute x1, starting transfers between devices, shards(): far = lax.ppermute(near, 'c', [(0, 1), (1, 0)])  6.98 us
    pallas_call x5, Pallas kernels, on_scalars(): pl.pallas_call(body, in_specs=[pl.BlockSpec(memory_space=pltpu.SMEM)] * l...  4.11 us
    unnamed x26, local copies, waits for them, and re-layouts  3.44 us
    pallas_call x1, Pallas kernels, precondition(): pl.pallas_call(body, in_specs=[pl.BlockSpec(memory_space=pltpu.SMEM)] * 3...  3.16 us
  transfers between devices with their start and end apart: 22, of which 9 were waited for; matrix products, arithmetic and copies ran while one was open for 2% of the time, Pallas kernels for 3%

profile of v6, /device:TPU:1, one launch (start us, length us, event | category | flops | bytes accessed | tf_op | source)
XLA Modules:
  0.0 149.3 jit_solution(15162359184825359528)
XLA Ops:
  0.8 2.8 %pad_maximum_fusion = bf16[16,88,640]{2,1,0:T(8,128)(2,1)} fusion(bf16[16,8,640]{2,1,0:T(8,128)(2,1)S(1)} %broadcast_in_dim.51, bf16[16,40,640]{2,1,0:T(8,128)(2,1)} %bitcast.29, bf16[16,40,640]{2,1,0:T(8,128)(2,1)} %bitcast.30), kind=kLoop, calls=%fused_computation | loop fusion | flops 5406720 | bytes 3604480 | tf_op jit(solution)/shard_map/concatenate | solution.py:63
  3.6 10.5 %all-to-all-start = ((bf16[16,88,640]{2,1,0:T(8,128)(2,1)}), bf16[16,88,640]{2,1,0:T(8,128)(2,1)S(1)}, u32[]{:S(2)}, u32[]{:S(2)}) async-start(bf16[16,88,640]{2,1,0:T(8,128)(2,1)} %pad_maximum_fusion), calls=%async_computation | async-start | bytes 3604480 | tf_op jit(solution)/shard_map/all_to_all | solution.py:28
  14.2 2.4 %all_gather.13 = bf16[512,640]{1,0:T(8,128)(2,1)S(1)} all-gather(bf16[256,640]{1,0:T(8,128)(2,1)S(1)} %copy-done.10), channel_id=1, replica_groups=mesh['yj'=4,'yh'=2,'x'=4,'zl'=2,'c'=2,'mp'=4] {'c'}, dimensions={0}, use_global_device_ids=true | all-gather | bytes 983040 | tf_op jit(solution)/shard_map/all_gather | solution.py:32
  16.7 7.1 %collective-permute-start.4 = (bf16[512,320]{1,0:T(8,128)(2,1)S(1)}, bf16[512,320]{1,0:T(8,128)(2,1)S(1)}, u32[]{:S(2)}, u32[]{:S(2)}) collective-permute-start(bf16[512,320]{1,0:T(8,128)(2,1)S(1)} %slice_select_fusion.g_ref), channel_id=1, source_target_pairs={{0,3},{1,2},{2,1},{3,0},{4,7},{5,6},{6,5},{7,4},{8,11},{9,10},{10,... | collective-permute-start | bytes 983048 | tf_op jit(solution)/shard_map/ppermute | solution.py:36
  27.3 2.8 %all_gather.12.x_ref = bf16[512,640]{1,0:T(8,128)(2,1)S(1)} all-gather(bf16[256,640]{1,0:T(8,128)(2,1)} %multiply_convert_fusion), channel_id=1, replica_groups=mesh['yj'=4,'yh'=2,'x'=4,'zl'=2,'c'=2,'mp'=4] {'c'}, dimensions={0}, use_global_device_ids=true | all-gather | bytes 983040 | tf_op jit(solution)/shard_map/all_gather | solution.py:32
  30.1 4.0 %collective-permute-start = (s32[4]{0:T(128)S(1)}, s32[4]{0:T(128)S(1)}, u32[]{:S(2)}, u32[]{:S(2)}) collective-permute-start(s32[4]{0:T(128)S(1)} %bitcast.36), channel_id=1, source_target_pairs={{0,1},{1,0},{2,3},{3,2},{4,5},{5,4},{6,7},{7,6},{8,9},{9,8},{10,11... | collective-permute-start | bytes 56 | tf_op jit(solution)/shard_map/ppermute | solution.py:36
  36.0 5.5 %collective-permute-start.2 = (s32[4]{0:T(128)S(1)}, s32[4]{0:T(128)S(1)}, u32[]{:S(2)}, u32[]{:S(2)}) collective-permute-start(s32[4]{0:T(128)S(1)} %bitcast.38), channel_id=1, source_target_pairs={{0,3},{1,2},{2,1},{3,0},{4,7},{5,6},{6,5},{7,4},{8,11},{9,10},{10,... | collective-permute-start | bytes 56 | tf_op jit(solution)/shard_map/ppermute | solution.py:36
  42.4 2.6 %collective-permute-done.1 = s32[4]{0:T(128)S(1)} collective-permute-done((s32[4]{0:T(128)S(1)}, s32[4]{0:T(128)S(1)}, u32[]{:S(2)}, u32[]{:S(2)}) %collective-permute-start.1) | collective-permute-done | bytes 48 | tf_op jit(solution)/shard_map/ppermute | solution.py:36
  46.5 4.5 %all-to-all-start.1 = ((bf16[4,48,640]{2,1,0:T(8,128)(2,1)}), bf16[4,48,640]{2,1,0:T(8,128)(2,1)S(1)}, u32[]{:S(2)}, u32[]{:S(2)}) async-start(bf16[4,48,640]{2,1,0:T(8,128)(2,1)} %copy-done), calls=%async_computation.1 | async-start | bytes 491520 | tf_op jit(solution)/shard_map/all_to_all | solution.py:28
  51.0 4.0 %all_gather.14.x_ref = bf16[512,640]{1,0:T(8,128)(2,1)S(1)} all-gather(bf16[256,640]{1,0:T(8,128)(2,1)} %collective-permute-done.3), channel_id=1, replica_groups=mesh['yj'=4,'yh'=2,'x'=4,'zl'=2,'c'=2,'mp'=4] {'c'}, dimensions={0}, use_global_device_ids=true | all-gather | bytes 983040 | tf_op jit(solution)/shard_map/all_gather | solution.py:32
  60.6 6.1 %all-to-all-start.2 = ((bf16[8,88,640]{2,1,0:T(8,128)(2,1)}), bf16[8,88,640]{2,1,0:T(8,128)(2,1)S(1)}, u32[]{:S(2)}, u32[]{:S(2)}) async-start(bf16[8,88,640]{2,1,0:T(8,128)(2,1)} %shard_map.85), calls=%async_computation.2 | async-start | bytes 1802240 | tf_op jit(solution)/shard_map/all_to_all | solution.py:28
  66.6 4.3 %collective-permute-start.10 = (bf16[2,80,640]{2,1,0:T(8,128)(2,1)S(1)}, bf16[2,80,640]{2,1,0:T(8,128)(2,1)}, u32[]{:S(2)}, u32[]{:S(2)}) collective-permute-start(bf16[2,80,640]{2,1,0:T(8,128)(2,1)S(1)} %copy-done.8), channel_id=1, source_target_pairs={{0,48},{16,32},{32,16},{48,0},{1,49},{17,33},{33,17},{49,1},{2,50}... | collective-permute-start | bytes 614408 | tf_op jit(solution)/shard_map/ppermute | solution.py:36
  72.9 3.4 %collective-permute-start.9 = (bf16[2,80,640]{2,1,0:T(8,128)(2,1)S(1)}, bf16[2,80,640]{2,1,0:T(8,128)(2,1)}, u32[]{:S(2)}, u32[]{:S(2)}) collective-permute-start(bf16[2,80,640]{2,1,0:T(8,128)(2,1)S(1)} %copy-done.4), channel_id=1, source_target_pairs={{0,32},{16,48},{32,0},{48,16},{1,33},{17,49},{33,1},{49,17},{2,34}... | collective-permute-start | bytes 614408 | tf_op jit(solution)/shard_map/ppermute | solution.py:36
  79.8 5.4 %collective-permute-start.6 = (bf16[2,80,640]{2,1,0:T(8,128)(2,1)}, bf16[2,80,640]{2,1,0:T(8,128)(2,1)S(1)}, u32[]{:S(2)}, u32[]{:S(2)}) collective-permute-start(bf16[2,80,640]{2,1,0:T(8,128)(2,1)} %get-tuple-element.36), channel_id=1, source_target_pairs={{0,32},{16,48},{32,0},{48,16},{1,33},{17,49},{33,1},{49,17},{2,34}... | collective-permute-start | bytes 614408 | tf_op jit(solution)/shard_map/ppermute | solution.py:36
  89.2 4.9 %collective-permute-start.11 = (bf16[2,80,640]{2,1,0:T(8,128)(2,1)S(1)}, bf16[2,80,640]{2,1,0:T(8,128)(2,1)S(1)}, u32[]{:S(2)}, u32[]{:S(2)}) collective-permute-start(bf16[2,80,640]{2,1,0:T(8,128)(2,1)S(1)} %add_convert_fusion), channel_id=1, source_target_pairs={{0,1},{1,0},{2,3},{3,2},{4,5},{5,4},{6,7},{7,6},{8,9},{9,8},{10,11... | collective-permute-start | bytes 614408 | tf_op jit(solution)/shard_map/ppermute | solution.py:36
  96.1 4.8 %collective-permute-start.12 = (bf16[2,88,640]{2,1,0:T(8,128)(2,1)S(1)}, bf16[2,88,640]{2,1,0:T(8,128)(2,1)S(1)}, u32[]{:S(2)}, u32[]{:S(2)}) collective-permute-start(bf16[2,88,640]{2,1,0:T(8,128)(2,1)S(1)} %shard_map.86.pair_ref), channel_id=1, source_target_pairs={{0,8},{8,0},{1,9},{9,1},{2,10},{10,2},{3,11},{11,3},{4,12},{12,4},... | collective-permute-start | bytes 675848 | tf_op jit(solution)/shard_map/ppermute | solution.py:36
  101.0 6.1 %collective-permute-done.12.other_ref = bf16[2,88,640]{2,1,0:T(8,128)(2,1)S(1)} collective-permute-done((bf16[2,88,640]{2,1,0:T(8,128)(2,1)S(1)}, bf16[2,88,640]{2,1,0:T(8,128)(2,1)S(1)}, u32[]{:S(2)}, u32[]{:S(2)}) %collective-permute-start.12) | collective-permute-done | bytes 225312 | tf_op jit(solution)/shard_map/ppermute | solution.py:36
  108.0 5.2 %all-to-all-start.3 = ((bf16[16,20,640]{2,1,0:T(8,128)(2,1)}), bf16[16,20,640]{2,1,0:T(8,128)(2,1)S(1)}, u32[]{:S(2)}, u32[]{:S(2)}) async-start(bf16[16,20,640]{2,1,0:T(8,128)(2,1)} %reshape.36), calls=%async_computation.3 | async-start | bytes 983040 | tf_op jit(solution)/shard_map/all_to_all | solution.py:28
  115.8 3.7 %collective-permute-start.14 = (bf16[2,88,640]{2,1,0:T(8,128)(2,1)S(1)}, bf16[2,88,640]{2,1,0:T(8,128)(2,1)S(1)}, u32[]{:S(2)}, u32[]{:S(2)}) collective-permute-start(bf16[2,88,640]{2,1,0:T(8,128)(2,1)S(1)} %shard_map.88), channel_id=1, source_target_pairs={{0,32},{16,48},{32,0},{48,16},{1,33},{17,49},{33,1},{49,17},{2,34}... | collective-permute-start | bytes 675848 | tf_op jit(solution)/shard_map/ppermute | solution.py:36
  119.5 3.8 %collective-permute-start.15 = (bf16[2,88,640]{2,1,0:T(8,128)(2,1)S(1)}, bf16[2,88,640]{2,1,0:T(8,128)(2,1)S(1)}, u32[]{:S(2)}, u32[]{:S(2)}) collective-permute-start(bf16[2,88,640]{2,1,0:T(8,128)(2,1)S(1)} %shard_map.88), channel_id=1, source_target_pairs={{0,48},{16,32},{32,16},{48,0},{1,49},{17,33},{33,17},{49,1},{2,50}... | collective-permute-start | bytes 675848 | tf_op jit(solution)/shard_map/ppermute | solution.py:36
  125.7 4.3 %all-to-all-start.4 = ((bf16[16,20,640]{2,1,0:T(8,128)(2,1)}), bf16[16,20,640]{2,1,0:T(8,128)(2,1)S(1)}, u32[]{:S(2)}, u32[]{:S(2)}) async-start(bf16[16,20,640]{2,1,0:T(8,128)(2,1)} %shard_map.87), calls=%async_computation.4 | async-start | bytes 983040 | tf_op jit(solution)/shard_map/all_to_all | solution.py:28
  130.3 7.0 %collective-permute-start.16 = (bf16[4,2,88,640]{3,2,1,0:T(8,128)(2,1)S(1)}, bf16[4,2,88,640]{3,2,1,0:T(8,128)(2,1)S(1)}, u32[]{:S(2)}, u32[]{:S(2)}) collective-permute-start(bf16[4,2,88,640]{3,2,1,0:T(8,128)(2,1)S(1)} %pad_maximum_fusion.1.near_ref), channel_id=1, source_target_pairs={{0,4},{4,0},{1,5},{5,1},{2,6},{6,2},{3,7},{7,3},{8,12},{12,8},{9,1... | collective-permute-start | bytes 2703368 | tf_op jit(solution)/shard_map/ppermute | solution.py:250
  137.8 8.3 %all_gather.15.gt_ref = bf16[640,640]{1,0:T(8,128)(2,1)S(1)} all-gather(bf16[320,640]{1,0:T(8,128)(2,1)S(1)} %reshape.37), channel_id=1, replica_groups=mesh['yj'=4,'yh'=2,'x'=4,'zl'=2,'c'=2,'mp'=4] {'c'}, dimensions={0}, use_global_device_ids=true | all-gather | bytes 1228800 | tf_op jit(solution)/shard_map/all_gather | solution.py:32
  146.1 3.2 %shard_map.89 = bf16[20,640]{1,0:T(8,128)(2,1)} custom-call(s32[1]{0:T(128)} %bitcast.place_ref, s32[1]{0:T(128)} %bitcast.1.core_ref, s32[1]{0:T(128)} %bitcast.2.first_ref, bf16[640,640]{1,0:T(8,128)(2,1)S(1)} %all_gather.15.gt_ref, bf16[4,2,88,640]{3,2,1,0:T(8,128)(2,1)S(1)} %pad_maximum_fusion.1.near_ref, ...), custom_call_target="tpu_custom_call" | custom-call | tf_op jit(solution)/shard_map/pallas_call | solution.py:235
  (81 shorter events, 32.2 us)
Async XLA Ops:
  3.6 41.5 %all-to-all-start = ((bf16[16,88,640]{2,1,0:T(8,128)(2,1)}), bf16[16,88,640]{2,1,0:T(8,128)(2,1)S(1)}, u32[]{:S(2)}, u32[]{:S(2)}) async-start(bf16[16,88,640]{2,1,0:T(8,128)(2,1)} %pad_maximum_fusion), calls=%async_computation | async-start | bytes 3604480 | tf_op jit(solution)/shard_map/all_to_all | solution.py:28
  14.1 15.9 %copy-start.12 = (s32[1,4]{1,0:T(1,128)S(1)}, s32[1,4]{1,0:T(1,128)}, u32[]{:S(2)}) copy-start(s32[1,4]{1,0:T(1,128)} %param.11) | copy-start | bytes 52
  16.7 28.3 %collective-permute-start.4 = (bf16[512,320]{1,0:T(8,128)(2,1)S(1)}, bf16[512,320]{1,0:T(8,128)(2,1)S(1)}, u32[]{:S(2)}, u32[]{:S(2)}) collective-permute-start(bf16[512,320]{1,0:T(8,128)(2,1)S(1)} %slice_select_fusion.g_ref), channel_id=1, source_target_pairs={{0,3},{1,2},{2,1},{3,0},{4,7},{5,6},{6,5},{7,4},{8,11},{9,10},{10,... | collective-permute-start | bytes 983048 | tf_op jit(solution)/shard_map/ppermute | solution.py:36
  25.1 20.0 %collective-permute-start.3 = (bf16[256,640]{1,0:T(8,128)(2,1)}, bf16[256,640]{1,0:T(8,128)(2,1)}, u32[]{:S(2)}, u32[]{:S(2)}) collective-permute-start(bf16[256,640]{1,0:T(8,128)(2,1)} %multiply_convert_fusion), channel_id=1, source_target_pairs={{0,1},{1,0},{2,3},{3,2},{4,5},{5,4},{6,7},{7,6},{8,9},{9,8},{10,11... | collective-permute-start | bytes 983048 | tf_op jit(solution)/shard_map/ppermute | solution.py:36
  30.1 12.4 %collective-permute-start = (s32[4]{0:T(128)S(1)}, s32[4]{0:T(128)S(1)}, u32[]{:S(2)}, u32[]{:S(2)}) collective-permute-start(s32[4]{0:T(128)S(1)} %bitcast.36), channel_id=1, source_target_pairs={{0,1},{1,0},{2,3},{3,2},{4,5},{5,4},{6,7},{7,6},{8,9},{9,8},{10,11... | collective-permute-start | bytes 56 | tf_op jit(solution)/shard_map/ppermute | solution.py:36
  34.1 11.0 %collective-permute-start.1 = (s32[4]{0:T(128)S(1)}, s32[4]{0:T(128)S(1)}, u32[]{:S(2)}, u32[]{:S(2)}) collective-permute-start(s32[4]{0:T(128)S(1)} %bitcast.37), channel_id=1, source_target_pairs={{0,2},{1,3},{2,0},{3,1},{4,6},{5,7},{6,4},{7,5},{8,10},{9,11},{10,... | collective-permute-start | bytes 56 | tf_op jit(solution)/shard_map/ppermute | solution.py:36
  36.0 9.0 %collective-permute-start.2 = (s32[4]{0:T(128)S(1)}, s32[4]{0:T(128)S(1)}, u32[]{:S(2)}, u32[]{:S(2)}) collective-permute-start(s32[4]{0:T(128)S(1)} %bitcast.38), channel_id=1, source_target_pairs={{0,3},{1,2},{2,1},{3,0},{4,7},{5,6},{6,5},{7,4},{8,11},{9,10},{10,... | collective-permute-start | bytes 56 | tf_op jit(solution)/shard_map/ppermute | solution.py:36
  46.5 12.5 %all-to-all-start.1 = ((bf16[4,48,640]{2,1,0:T(8,128)(2,1)}), bf16[4,48,640]{2,1,0:T(8,128)(2,1)S(1)}, u32[]{:S(2)}, u32[]{:S(2)}) async-start(bf16[4,48,640]{2,1,0:T(8,128)(2,1)} %copy-done), calls=%async_computation.1 | async-start | bytes 491520 | tf_op jit(solution)/shard_map/all_to_all | solution.py:28
  60.6 27.0 %copy-start.2 = (bf16[2,80,640]{2,1,0:T(8,128)(2,1)S(1)}, bf16[2,80,640]{2,1,0:T(8,128)(2,1)}, u32[]{:S(2)}) copy-start(bf16[2,80,640]{2,1,0:T(8,128)(2,1)} %copy-done.1) | copy-start | bytes 614404
  60.6 28.7 %all-to-all-start.2 = ((bf16[8,88,640]{2,1,0:T(8,128)(2,1)}), bf16[8,88,640]{2,1,0:T(8,128)(2,1)S(1)}, u32[]{:S(2)}, u32[]{:S(2)}) async-start(bf16[8,88,640]{2,1,0:T(8,128)(2,1)} %shard_map.85), calls=%async_computation.2 | async-start | bytes 1802240 | tf_op jit(solution)/shard_map/all_to_all | solution.py:28
  66.6 18.6 %collective-permute-start.10 = (bf16[2,80,640]{2,1,0:T(8,128)(2,1)S(1)}, bf16[2,80,640]{2,1,0:T(8,128)(2,1)}, u32[]{:S(2)}, u32[]{:S(2)}) collective-permute-start(bf16[2,80,640]{2,1,0:T(8,128)(2,1)S(1)} %copy-done.8), channel_id=1, source_target_pairs={{0,48},{16,32},{32,16},{48,0},{1,49},{17,33},{33,17},{49,1},{2,50}... | collective-permute-start | bytes 614408 | tf_op jit(solution)/shard_map/ppermute | solution.py:36
  70.9 16.6 %collective-permute-start.8 = (bf16[2,80,640]{2,1,0:T(8,128)(2,1)S(1)}, bf16[2,80,640]{2,1,0:T(8,128)(2,1)}, u32[]{:S(2)}, u32[]{:S(2)}) collective-permute-start(bf16[2,80,640]{2,1,0:T(8,128)(2,1)S(1)} %copy-done.6), channel_id=1, source_target_pairs={{0,16},{16,0},{32,48},{48,32},{1,17},{17,1},{33,49},{49,33},{2,18}... | collective-permute-start | bytes 614408 | tf_op jit(solution)/shard_map/ppermute | solution.py:36
  72.9 14.6 %collective-permute-start.9 = (bf16[2,80,640]{2,1,0:T(8,128)(2,1)S(1)}, bf16[2,80,640]{2,1,0:T(8,128)(2,1)}, u32[]{:S(2)}, u32[]{:S(2)}) collective-permute-start(bf16[2,80,640]{2,1,0:T(8,128)(2,1)S(1)} %copy-done.4), channel_id=1, source_target_pairs={{0,32},{16,48},{32,0},{48,16},{1,33},{17,49},{33,1},{49,17},{2,34}... | collective-permute-start | bytes 614408 | tf_op jit(solution)/shard_map/ppermute | solution.py:36
  77.9 16.2 %collective-permute-start.5 = (bf16[2,80,640]{2,1,0:T(8,128)(2,1)}, bf16[2,80,640]{2,1,0:T(8,128)(2,1)S(1)}, u32[]{:S(2)}, u32[]{:S(2)}) collective-permute-start(bf16[2,80,640]{2,1,0:T(8,128)(2,1)} %get-tuple-element.35), channel_id=1, source_target_pairs={{0,16},{16,0},{32,48},{48,32},{1,17},{17,1},{33,49},{49,33},{2,18}... | collective-permute-start | bytes 614408 | tf_op jit(solution)/shard_map/ppermute | solution.py:36
  79.8 14.3 %collective-permute-start.6 = (bf16[2,80,640]{2,1,0:T(8,128)(2,1)}, bf16[2,80,640]{2,1,0:T(8,128)(2,1)S(1)}, u32[]{:S(2)}, u32[]{:S(2)}) collective-permute-start(bf16[2,80,640]{2,1,0:T(8,128)(2,1)} %get-tuple-element.36), channel_id=1, source_target_pairs={{0,32},{16,48},{32,0},{48,16},{1,33},{17,49},{33,1},{49,17},{2,34}... | collective-permute-start | bytes 614408 | tf_op jit(solution)/shard_map/ppermute | solution.py:36
  85.3 10.1 %collective-permute-start.7 = (bf16[2,80,640]{2,1,0:T(8,128)(2,1)}, bf16[2,80,640]{2,1,0:T(8,128)(2,1)S(1)}, u32[]{:S(2)}, u32[]{:S(2)}) collective-permute-start(bf16[2,80,640]{2,1,0:T(8,128)(2,1)} %get-tuple-element.37), channel_id=1, source_target_pairs={{0,48},{16,32},{32,16},{48,0},{1,49},{17,33},{33,17},{49,1},{2,50}... | collective-permute-start | bytes 614408 | tf_op jit(solution)/shard_map/ppermute | solution.py:36
  89.2 11.7 %collective-permute-start.11 = (bf16[2,80,640]{2,1,0:T(8,128)(2,1)S(1)}, bf16[2,80,640]{2,1,0:T(8,128)(2,1)S(1)}, u32[]{:S(2)}, u32[]{:S(2)}) collective-permute-start(bf16[2,80,640]{2,1,0:T(8,128)(2,1)S(1)} %add_convert_fusion), channel_id=1, source_target_pairs={{0,1},{1,0},{2,3},{3,2},{4,5},{5,4},{6,7},{7,6},{8,9},{9,8},{10,11... | collective-permute-start | bytes 614408 | tf_op jit(solution)/shard_map/ppermute | solution.py:36
  96.1 11.0 %collective-permute-start.12 = (bf16[2,88,640]{2,1,0:T(8,128)(2,1)S(1)}, bf16[2,88,640]{2,1,0:T(8,128)(2,1)S(1)}, u32[]{:S(2)}, u32[]{:S(2)}) collective-permute-start(bf16[2,88,640]{2,1,0:T(8,128)(2,1)S(1)} %shard_map.86.pair_ref), channel_id=1, source_target_pairs={{0,8},{8,0},{1,9},{9,1},{2,10},{10,2},{3,11},{11,3},{4,12},{12,4},... | collective-permute-start | bytes 675848 | tf_op jit(solution)/shard_map/ppermute | solution.py:36
  108.0 16.9 %all-to-all-start.3 = ((bf16[16,20,640]{2,1,0:T(8,128)(2,1)}), bf16[16,20,640]{2,1,0:T(8,128)(2,1)S(1)}, u32[]{:S(2)}, u32[]{:S(2)}) async-start(bf16[16,20,640]{2,1,0:T(8,128)(2,1)} %reshape.36), calls=%async_computation.3 | async-start | bytes 983040 | tf_op jit(solution)/shard_map/all_to_all | solution.py:28
  113.7 16.3 %collective-permute-start.13 = (bf16[2,88,640]{2,1,0:T(8,128)(2,1)S(1)}, bf16[2,88,640]{2,1,0:T(8,128)(2,1)S(1)}, u32[]{:S(2)}, u32[]{:S(2)}) collective-permute-start(bf16[2,88,640]{2,1,0:T(8,128)(2,1)S(1)} %shard_map.88), channel_id=1, source_target_pairs={{0,16},{16,0},{32,48},{48,32},{1,17},{17,1},{33,49},{49,33},{2,18}... | collective-permute-start | bytes 675848 | tf_op jit(solution)/shard_map/ppermute | solution.py:36
  115.8 14.3 %collective-permute-start.14 = (bf16[2,88,640]{2,1,0:T(8,128)(2,1)S(1)}, bf16[2,88,640]{2,1,0:T(8,128)(2,1)S(1)}, u32[]{:S(2)}, u32[]{:S(2)}) collective-permute-start(bf16[2,88,640]{2,1,0:T(8,128)(2,1)S(1)} %shard_map.88), channel_id=1, source_target_pairs={{0,32},{16,48},{32,0},{48,16},{1,33},{17,49},{33,1},{49,17},{2,34}... | collective-permute-start | bytes 675848 | tf_op jit(solution)/shard_map/ppermute | solution.py:36
  119.5 10.6 %collective-permute-start.15 = (bf16[2,88,640]{2,1,0:T(8,128)(2,1)S(1)}, bf16[2,88,640]{2,1,0:T(8,128)(2,1)S(1)}, u32[]{:S(2)}, u32[]{:S(2)}) collective-permute-start(bf16[2,88,640]{2,1,0:T(8,128)(2,1)S(1)} %shard_map.88), channel_id=1, source_target_pairs={{0,48},{16,32},{32,16},{48,0},{1,49},{17,33},{33,17},{49,1},{2,50}... | collective-permute-start | bytes 675848 | tf_op jit(solution)/shard_map/ppermute | solution.py:36
  125.7 12.0 %all-to-all-start.4 = ((bf16[16,20,640]{2,1,0:T(8,128)(2,1)}), bf16[16,20,640]{2,1,0:T(8,128)(2,1)S(1)}, u32[]{:S(2)}, u32[]{:S(2)}) async-start(bf16[16,20,640]{2,1,0:T(8,128)(2,1)} %shard_map.87), calls=%async_computation.4 | async-start | bytes 983040 | tf_op jit(solution)/shard_map/all_to_all | solution.py:28
  130.3 15.8 %collective-permute-start.16 = (bf16[4,2,88,640]{3,2,1,0:T(8,128)(2,1)S(1)}, bf16[4,2,88,640]{3,2,1,0:T(8,128)(2,1)S(1)}, u32[]{:S(2)}, u32[]{:S(2)}) collective-permute-start(bf16[4,2,88,640]{3,2,1,0:T(8,128)(2,1)S(1)} %pad_maximum_fusion.1.near_ref), channel_id=1, source_target_pairs={{0,4},{4,0},{1,5},{5,1},{2,6},{6,2},{3,7},{7,3},{8,12},{12,8},{9,1... | collective-permute-start | bytes 2703368 | tf_op jit(solution)/shard_map/ppermute | solution.py:250
  (11 other events, 62.6 us)
